TPU v7x, 512 devices: a whole 4x4x16 slice. The times are simulated.
512 devices in a mesh: dp: 16 (over z_hi, x), expert: 32 (over y, z_lo, core).
Axes of the slice: x: 4, y: 4, z: 16 (z_hi: 4, z_lo: 4; z = z_hi * 4 + z_lo), core: 2. Of those that a mesh axis runs over, the one named last changes fastest.
Arguments:
- tokens: bfloat16 [65536, 1024], P(('dp', 'expert')), may hold values from -6 to 6
- expert_id: int32 [65536, 1], P(('dp', 'expert')), may hold values from 0 to 31; in each aligned block of 128 rows (0 to 127, 128 to 255, ...) at most 8 rows name the same one
- gate_prob: bfloat16 [65536], P(('dp', 'expert')), may hold values from 0.29882812 to 1
- w_in: bfloat16 [32, 1024, 4096], P('expert', None, 'dp'), may hold values from -0.1875 to 0.1875
- w_out: bfloat16 [32, 4096, 1024], P('expert', 'dp'), may hold values from -0.09375 to 0.09375
- head: bfloat16 [1024, 512], replicated, may hold values from -0.1875 to 0.1875
- image_cache: bfloat16 [4096, 512], P(('dp', 'expert')), may hold values from -25 to 25
- text_cache: bfloat16 [4096, 512], P(('dp', 'expert')), may hold values from -5.1 to 5.1
- pair_label: int32 [4096], P(('dp', 'expert')), may hold values from 0 to 4095, each once
Outputs:
- grad_image: float32 [4096, 512], P(('dp', 'expert'))
- grad_in: float32 [32, 1024, 4096], P('expert', None, 'dp')
- grad_out: float32 [32, 4096, 1024], P('expert', 'dp')
Inputs may be any that keep to these rules, and one draw needn't show every extreme that they name: `expert_id`: among the 128 tokens of one device no expert is named more than 8 times, a bound that some block reaches. `pair_label`: each caption index appears once.
All inputs are finite; a program needn't handle non-finite values.
Results may differ from a plain program's by a relative error of at most 0.015.
Values may be sent and summed in bfloat16 or wider, within the bound.
No kernel may reach another device: no remote copies, remote signals or barrier semaphores. Data moves between devices by JAX's collectives and lax.ppermute only.
A program may use at most 64 MiB of HBM per device.

v0:
```python
import jax
import jax.numpy as jnp
from jax import lax
from jax.sharding import PartitionSpec as P

LOGIT_SCALE = 0.125
GELU_K = 0.7978845608
GELU_C = 0.044715


def gelu_parts(pre):
    inner = GELU_K * (pre + GELU_C * pre * pre * pre)
    tangent = jnp.tanh(inner)
    value = 0.5 * pre * (1.0 + tangent)
    slope = 0.5 * (1.0 + tangent) + 0.5 * pre * (1.0 - tangent * tangent) * GELU_K * (
        1.0 + 3.0 * GELU_C * pre * pre
    )
    return (value, slope)


def expert_terms(x_rows, dy_rows, first, second):
    pre = jnp.dot(x_rows, first, preferred_element_type=jnp.float32)
    value, slope = gelu_parts(pre)
    hidden = value.astype(jnp.bfloat16)
    back = lax.dot_general(
        dy_rows, second, (((1,), (1,)), ((), ())), preferred_element_type=jnp.float32
    )
    hidden_grad = (back * slope).astype(jnp.bfloat16)
    grad_first = lax.dot_general(
        x_rows, hidden_grad, (((0,), (0,)), ((), ())), preferred_element_type=jnp.float32
    )
    grad_second = lax.dot_general(
        hidden, dy_rows, (((0,), (0,)), ((), ())), preferred_element_type=jnp.float32
    )
    return (grad_first, grad_second)


def caption_block(carry, image_cache, pair_label, piece):
    run_top, run_total, run_mix, run_label = carry
    logits = LOGIT_SCALE * lax.dot_general(
        image_cache, piece, (((1,), (1,)), ((), ())), preferred_element_type=jnp.float32
    )
    new_top = jnp.maximum(run_top, jnp.max(logits, axis=1, keepdims=True))
    expo = jnp.exp(logits - new_top)
    new_total = jnp.sum(expo, axis=1, keepdims=True)
    new_mix = jnp.dot(expo.astype(jnp.bfloat16), piece, preferred_element_type=jnp.float32)
    columns = jnp.arange(piece.shape[0], dtype=jnp.int32)
    hits = (pair_label[:, None] == columns[None, :]).astype(jnp.bfloat16)
    new_label = jnp.dot(hits, piece, preferred_element_type=jnp.float32)
    return (new_top, new_total, new_mix, new_label)


def body(tokens, expert_id, gate_prob, w_in, w_out, head, image_cache, text_cache, pair_label):
    n_tok = tokens.shape[0]
    n_exp = lax.axis_size("expert")
    capacity = 2 * n_tok // n_exp
    n_pairs = image_cache.shape[0]
    width = image_cache.shape[1]
    start_carry = (
        jnp.full((n_pairs, 1), -1e30, jnp.float32),
        jnp.zeros((n_pairs, 1), jnp.float32),
        jnp.zeros((n_pairs, width), jnp.float32),
        jnp.zeros((n_pairs, width), jnp.float32),
    )
    captions = lax.all_gather(text_cache, ("dp", "expert"), axis=0, tiled=True)
    result = caption_block(start_carry, image_cache, pair_label, captions)
    grad_image = LOGIT_SCALE * (result[2] / result[1] - result[3])
    rep_grad = grad_image[0].astype(jnp.bfloat16)
    cotangent = jnp.dot(head, rep_grad, preferred_element_type=jnp.float32).astype(jnp.bfloat16)
    chosen = expert_id[:, 0]
    onehot = (chosen[:, None] == jnp.arange(n_exp, dtype=jnp.int32)[None, :]).astype(jnp.float32)
    lower = (jnp.arange(n_tok)[:, None] > jnp.arange(n_tok)[None, :]).astype(jnp.float32)
    before = jnp.dot(lower, onehot, precision=lax.Precision.HIGHEST)
    rank = jnp.sum(before * onehot, axis=1).astype(jnp.int32)
    position = chosen * capacity + rank
    dispatch = (position[:, None] == jnp.arange(n_exp * capacity, dtype=jnp.int32)[None, :]).astype(
        jnp.bfloat16
    )
    x_buffer = lax.dot_general(
        dispatch, tokens, (((0,), (0,)), ((), ())), preferred_element_type=jnp.float32
    ).astype(jnp.bfloat16)
    first = w_in[0]
    second = w_out[0]
    out_grad = (
        gate_prob.astype(jnp.float32)[:, None] * cotangent.astype(jnp.float32)[None, :]
    ).astype(jnp.bfloat16)
    g_buffer = lax.dot_general(
        dispatch, out_grad, (((0,), (0,)), ((), ())), preferred_element_type=jnp.float32
    ).astype(jnp.bfloat16)
    x_recv, g_recv = (
        lax.all_to_all(x_buffer, "expert", split_axis=0, concat_axis=0, tiled=True),
        lax.all_to_all(g_buffer, "expert", split_axis=0, concat_axis=0, tiled=True),
    )
    grads = expert_terms(
        lax.all_gather(x_recv, "dp", axis=0, tiled=True),
        lax.all_gather(g_recv, "dp", axis=0, tiled=True),
        first,
        second,
    )
    return (grad_image, grads[0][None], grads[1][None])


def solution(mesh):
    placed = (
        P(("dp", "expert"), None),
        P(("dp", "expert"), None),
        P(("dp", "expert")),
        P("expert", None, "dp"),
        P("expert", "dp", None),
        P(),
        P(("dp", "expert"), None),
        P(("dp", "expert"), None),
        P(("dp", "expert")),
    )
    return jax.shard_map(
        body,
        mesh=mesh,
        in_specs=placed,
        out_specs=(P(("dp", "expert"), None), P("expert", None, "dp"), P("expert", "dp", None)),
        check_vma=False,
    )
```

profile of v0, /device:TPU:1, one launch (start us, length us, event | category | flops | bytes accessed | tf_op | source)
XLA Modules:
  0.0 1289.8 jit_solution(7456019575707785858)
XLA Ops:
  7.2 0.0 copy-start
  7.2 0.0 all-gather.4.cloned.1.call-start
  7.2 0.7 all-gather.4.cloned.1.call-update
  7.9 0.0 all-gather.6.cloned.1.call-start
  8.0 0.9 fusion.15
  8.8 0.7 fusion.33
  9.5 1.3 fusion.12
  10.9 27.1 %all_to_all.24 = bf16[32,8,1024]{2,1,0:T(8,128)(2,1)} all-to-all(bf16[32,8,1024]{2,1,0:T(8,128)(2,1)S(1)} %fusion.12), channel_id=1, replica_groups=mesh['dp'=16,'expert'=32] {'expert'}, dimensions={0} | all-to-all | bytes 1048576 | tf_op jit(solution)/shard_map/all_to_all | solution.py:91
  38.0 0.0 all-gather.6.cloned.1.call-update
  38.0 0.0 all-gather.8.cloned.1.call-start
  38.1 0.7 convert_element_type.52
  38.7 0.0 copy-start.3
  38.7 783.1 %all-gather.4.cloned.1.call-done = bf16[4096,512]{1,0:T(8,128)(2,1)} async-done(((bf16[8,512]{1,0:T(8,128)(2,1)}), bf16[4096,512]{1,0:T(8,128)(2,1)}) %all-gather.4.cloned.1.call-update) | async-done | bytes 4194320 | tf_op jit(solution)/shard_map/all_gather | solution.py:65
  821.8 0.0 copy-start.1
  821.8 3.7 fusion.43
  825.5 0.2 fusion.22
  825.7 0.0 copy-done.1
  825.7 0.7 convolution_divide_fusion
  826.4 0.0 copy-done.3
  826.4 0.0 copy-start.4
  826.4 0.7 fusion.14
  827.1 0.0 copy-done
  827.1 0.0 copy-start.2
  827.1 0.4 fusion.31
  827.5 0.4 fusion.13
  827.9 52.1 %all_to_all.25 = bf16[32,8,1024]{2,1,0:T(8,128)(2,1)} all-to-all(bf16[32,8,1024]{2,1,0:T(8,128)(2,1)S(1)} %fusion.13), channel_id=1, replica_groups=mesh['dp'=16,'expert'=32] {'expert'}, dimensions={0} | all-to-all | bytes 1048576 | tf_op jit(solution)/shard_map/all_to_all | solution.py:92
  880.0 0.0 all-gather.8.cloned.1.call-update
  880.1 165.4 %all-gather.6.cloned.1.call-done = bf16[4096,1024]{1,0:T(8,128)(2,1)} async-done(((bf16[256,1024]{1,0:T(8,128)(2,1)}), bf16[4096,1024]{1,0:T(8,128)(2,1)}) %all-gather.6.cloned.1.call-update) | async-done | bytes 8388624 | tf_op jit(solution)/shard_map/all_gather | solution.py:95
  1045.5 0.0 copy-done.4
  1045.5 7.7 fusion.16
  1053.2 0.0 copy-done.2
  1053.2 0.0 copy-start.5
  1053.2 207.2 %all-gather.8.cloned.1.call-done = bf16[4096,1024]{1,0:T(8,128)(2,1)} async-done(((bf16[256,1024]{1,0:T(8,128)(2,1)}), bf16[4096,1024]{1,0:T(8,128)(2,1)}) %all-gather.8.cloned.1.call-update) | async-done | bytes 8388624 | tf_op jit(solution)/shard_map/all_gather | solution.py:96
  1260.4 8.2 fusion.11
  1268.6 0.0 copy-done.5
  1268.6 14.7 %convolution_bitcast_fusion = f32[1,1024,256]{2,1,0:T(8,128)} fusion(bf16[4096,1024]{1,0:T(8,128)(2,1)} %all-gather.6.cloned.1.call-done, bf16[4096,1024]{1,0:T(8,128)(2,1)} %all-gather.8.cloned.1.call-done, f32[4096,256]{1,0:T(8,128)} %fusion.16, bf16[1,256,1024]{2,1,0:T(8,128)(2,1)S(1)} %copy-done.5), kind=kOutput, calls=%fused_computation.17 | convolution fusion | flops 4314890240 | bytes 22544384 | tf_op jit(solution)/shard_map/dot_general | solution.py:29
  (2 shorter events, 0.0 us)
Async XLA Ops:
  7.2 820.0 %copy-start = (bf16[1024,512]{1,0:T(8,128)(2,1)S(1)}, bf16[1024,512]{1,0:T(8,128)(2,1)}, u32[]{:S(2)}) copy-start(bf16[1024,512]{1,0:T(8,128)(2,1)} %param.14) | copy-start | bytes 3145732
  7.2 814.6 %all-gather.4.cloned.1.call-start = ((), (), s32[]{:S(2)}) async-start(), calls=%async_computation.2 | async-start | bytes 4202496 | tf_op jit(solution)/shard_map/all_gather | solution.py:65
  7.9 1037.6 %all-gather.6.cloned.1.call-start = ((), (), s32[]{:S(2)}) async-start(), calls=%async_computation.3 | async-start | bytes 8912896 | tf_op jit(solution)/shard_map/all_gather | solution.py:95
  38.0 1222.4 %all-gather.8.cloned.1.call-start = ((), (), s32[]{:S(2)}) async-start(), calls=%async_computation.4 | async-start | bytes 8912896 | tf_op jit(solution)/shard_map/all_gather | solution.py:96
  38.7 787.7 %copy-start.3 = (s32[8]{0:T(128)S(1)}, s32[8]{0:T(128)}, u32[]{:S(2)}) copy-start(s32[8]{0:T(128)} %param.17) | copy-start | bytes 100
  821.8 3.9 copy-start.1
  826.4 219.1 %copy-start.4 = (bf16[1,1024,256]{2,1,0:T(8,128)(2,1)S(1)}, bf16[1,1024,256]{2,1,0:T(8,128)(2,1)}, u32[]{:S(2)}) copy-start(bf16[1,1024,256]{2,1,0:T(8,128)(2,1)} %param.12) | copy-start | bytes 1572868
  827.1 226.1 %copy-start.2 = (f32[8,512]{1,0:T(8,128)}, f32[8,512]{1,0:T(8,128)S(1)}, u32[]{:S(2)}) copy-start(f32[8,512]{1,0:T(8,128)S(1)} %fusion.14) | copy-start | bytes 49156
  1053.2 215.4 %copy-start.5 = (bf16[1,256,1024]{2,1,0:T(8,128)(2,1)S(1)}, bf16[1,256,1024]{2,1,0:T(8,128)(2,1)}, u32[]{:S(2)}) copy-start(bf16[1,256,1024]{2,1,0:T(8,128)(2,1)} %param.13) | copy-start | bytes 1572868
Sparse Core Ops, SparseCore 0:
  10.2 811.5 all-gather.3
  824.8 220.6 all-gather.5
  1048.5 211.8 all-gather.7
where the time goes:
time: 1290 us
  waiting for transfers between devices  1160 us (90%)
  blocking collectives  79.2 us (6%)
  matrix products  38.6 us (3%)
  between operations  13.8 us (1%)
    all_gather x1, waiting for transfers between devices, body(): captions = lax.all_gather(text_cache, ('dp', 'expert'), axis=0, tiled=True)  783 us
    all_gather x1, waiting for transfers between devices, body(): lax.all_gather(g_recv, 'dp', axis=0, tiled=True)  207 us
    all_gather x1, waiting for transfers between devices, body(): lax.all_gather(x_recv, 'dp', axis=0, tiled=True)  165 us
    all_to_all x1, blocking collectives, body(): lax.all_to_all(g_buffer, 'expert', split_axis=0, concat_axis=0, tiled=True)  52.1 us
    all_to_all x1, blocking collectives, body(): lax.all_to_all(x_buffer, 'expert', split_axis=0, concat_axis=0, tiled=True)  27.1 us
  transfers between devices with their start and end apart: 3, of which 3 were waited for; matrix products, arithmetic and copies ran while one was open for 1% of the time, Pallas kernels for 0%

commit v1 on v0

v1 whole, which is shorter than its diff:
```python
import jax
import jax.numpy as jnp
from jax import lax
from jax.experimental import pallas as pl
from jax.experimental.pallas import tpu as pltpu
from jax.sharding import PartitionSpec as P

LOGIT_SCALE = 0.125
GELU_K = 0.7978845608
GELU_C = 0.044715
SIDE = 4
HOPS = (0, -1, 1, 2)
BF = jnp.bfloat16
F32 = jnp.float32


def contract(a, b, da, db):
    return lax.dot_general(a, b, (((da,), (db,)), ((), ())), preferred_element_type=F32)


def gelu_parts(pre):
    inner = GELU_K * (pre + GELU_C * pre * pre * pre)
    tangent = jnp.tanh(inner)
    value = 0.5 * pre * (1.0 + tangent)
    slope = 0.5 * (1.0 + tangent) + 0.5 * pre * (1.0 - tangent * tangent) * GELU_K * (
        1.0 + 3.0 * GELU_C * pre * pre
    )
    return (value, slope)


def shift_z(a, by):
    ring = [
        (z * SIDE + x, (z + by) % SIDE * SIDE + x) for z in range(SIDE) for x in range(SIDE)
    ]
    return lax.ppermute(a, "dp", ring)


def shift_x(a, by):
    ring = [
        (z * SIDE + x, z * SIDE + (x + by) % SIDE) for z in range(SIDE) for x in range(SIDE)
    ]
    return lax.ppermute(a, "dp", ring)


def gather_z(own):
    half = own.shape[0] // 2
    before, after = shift_z(own, 1), shift_z(own, -1)
    far = [shift_z(before[:half], 1), shift_z(after[half:], -1)]
    return [own, before, after, jnp.concatenate(far, axis=0)]


def gather_x(own, way):
    before, after = shift_x(own, 1), shift_x(own, -1)
    far = shift_x(before, 1) if way > 0 else shift_x(after, -1)
    return [own, before, after, far]


def expert_kernel(*refs):
    n = SIDE * SIDE
    x_refs = refs[:n]
    first_ref, back_hi_ref, back_lo_ref, gate_ref, cot_ref, grad_in_ref, grad_out_ref, acc, sums = refs[n:]
    rows = x_refs[0].shape[0]
    images = sums.shape[0] // n
    per = rows // images
    first = first_ref[...]
    mask = (
        lax.broadcasted_iota(jnp.int32, (images, rows), 1) // per
        == lax.broadcasted_iota(jnp.int32, (images, rows), 0)
    )
    for c in range(n):
        here = pl.ds(c * images, images)
        x = x_refs[c][...]
        spread = jnp.where(mask, gate_ref[c : c + 1, :].astype(F32), 0.0).astype(BF)
        pre = jnp.dot(x, first, preferred_element_type=F32)
        value, slope = gelu_parts(pre)
        hidden = value.astype(BF)
        back = contract(spread, back_hi_ref[here, :], 0, 0) + contract(
            spread, back_lo_ref[here, :], 0, 0
        )
        hidden_grad = (back * slope).astype(BF)
        term = contract(hidden_grad, x, 0, 0)
        if c == 0:
            acc[...] = term
        else:
            acc[...] += term
        sums[here, :] = jnp.dot(spread, hidden, preferred_element_type=F32).astype(BF)
    grad_in_ref[...] = acc[...].T
    grad_out_ref[...] = contract(sums[...], cot_ref[...], 0, 0)


def expert_grads(pieces, first, back_hi, back_lo, gates, cot):
    rows, width = pieces[0].shape
    hidden = first.shape[1]
    vmem = pl.BlockSpec(memory_space=pltpu.VMEM)
    return pl.pallas_call(
        expert_kernel,
        out_shape=(
            jax.ShapeDtypeStruct((width, hidden), F32),
            jax.ShapeDtypeStruct((hidden, width), F32),
        ),
        in_specs=[vmem] * (len(pieces) + 5),
        out_specs=(vmem, vmem),
        scratch_shapes=[
            pltpu.VMEM((hidden, width), F32),
            pltpu.VMEM((cot.shape[0], hidden), BF),
        ],
        compiler_params=pltpu.CompilerParams(vmem_limit_bytes=32 * 1024 * 1024),
        cost_estimate=pl.CostEstimate(
            flops=5_000_000_000, bytes_accessed=13_000_000, transcendentals=1_000_000
        ),
    )(*pieces, first, back_hi, back_lo, gates, cot)


def body(tokens, expert_id, gate_prob, w_in, w_out, head, image_cache, text_cache, pair_label):
    n_tok, width = tokens.shape
    n_exp = lax.axis_size("expert")
    n_dp = lax.axis_size("dp")
    capacity = 2 * n_tok // n_exp
    n_slots = n_exp * capacity
    n_pairs, wide = image_cache.shape
    row = lax.axis_index("dp")
    first = w_in[0]
    second = w_out[0]

    label_parts = jnp.stack([pair_label // 64, pair_label % 64], axis=1).astype(BF)
    label_parts = jnp.pad(label_parts, ((0, 0), (0, 126)))
    column = lax.all_gather(
        jnp.concatenate([image_cache, label_parts], axis=1), "dp", axis=0, tiled=True
    )

    chosen = expert_id[:, 0]
    onehot = (chosen[:, None] == jnp.arange(n_exp, dtype=jnp.int32)[None, :]).astype(BF)
    lower = (jnp.arange(n_tok)[:, None] > jnp.arange(n_tok)[None, :]).astype(BF)
    before = jnp.dot(lower, onehot, preferred_element_type=F32)
    rank = jnp.sum(before * onehot.astype(F32), axis=1).astype(jnp.int32)
    position = chosen * capacity + rank
    dispatch = (position[:, None] == jnp.arange(n_slots, dtype=jnp.int32)[None, :]).astype(BF)
    x_buffer = contract(dispatch, tokens, 0, 0).astype(BF).reshape(n_exp, capacity, width)
    slot_gate = contract(dispatch, jnp.broadcast_to(gate_prob[:, None], (n_tok, 128)), 0, 0)
    slot_gate = slot_gate.astype(BF).reshape(n_exp, capacity, 128)
    captions = jnp.broadcast_to(text_cache[None], (n_exp, n_pairs, wide))
    sent = jnp.concatenate([x_buffer, captions, slot_gate], axis=2)
    got = lax.all_to_all(sent, "expert", split_axis=0, concat_axis=0, tiled=True)
    own = got[:, :, :width].reshape(n_slots, width)
    block = got[:, :, width : width + wide].reshape(n_exp * n_pairs, wide)
    gate_col = got[:, :, width + wide :].reshape(n_slots, 128)
    eye = (jnp.arange(n_slots)[:, None] == jnp.arange(n_slots)[None, :]).astype(F32)
    gate_row = jnp.sum(eye * gate_col[:, :1].astype(F32), axis=0, keepdims=True).astype(BF)

    pieces = []
    for i, piece in enumerate(gather_z(own)):
        pieces += gather_x(piece, 1 if i % 2 == 0 else -1)

    images = column[:, :wide]
    labels = column[:, wide].astype(jnp.int32) * 64 + column[:, wide + 1].astype(jnp.int32)
    logits = LOGIT_SCALE * contract(images, block, 1, 1)
    top = lax.reduce_precision(jnp.max(logits, axis=1, keepdims=True), 8, 7)
    expo = jnp.exp(logits - top)
    total = jnp.sum(expo, axis=1, keepdims=True)
    mix = jnp.dot(expo.astype(BF), block, preferred_element_type=F32)
    ids = row * block.shape[0] + jnp.arange(block.shape[0], dtype=jnp.int32)
    hits = (labels[:, None] == ids[None, :]).astype(BF)
    labelled = jnp.dot(hits, block, preferred_element_type=F32)
    total_hi = lax.reduce_precision(total, 8, 7)
    stats = jnp.concatenate([top, total_hi, total - total_hi], axis=1)
    stats = jnp.pad(stats, ((0, 0), (0, 125))).astype(BF)
    gates_out = jnp.broadcast_to(gate_row, (n_dp * n_pairs, n_slots))
    part = jnp.concatenate([mix.astype(BF), labelled.astype(BF), gates_out, stats], axis=1)
    part = part.reshape(n_dp, n_pairs, part.shape[1])
    part = lax.all_to_all(part, "dp", split_axis=0, concat_axis=0, tiled=True)
    stats = part[:, :, 2 * wide + n_slots :].astype(F32)
    tops = stats[:, :, 0:1]
    scale = jnp.exp(tops - jnp.max(tops, axis=0, keepdims=True))
    total = jnp.sum((stats[:, :, 1:2] + stats[:, :, 2:3]) * scale, axis=0)
    mixed = jnp.sum(part[:, :, :wide].astype(F32) * scale, axis=0) / total
    labelled = jnp.sum(part[:, :, wide : 2 * wide].astype(F32), axis=0)
    grad_image = LOGIT_SCALE * (mixed - labelled)
    rep_grad = grad_image[:1].astype(BF)

    z_hi, x = row // SIDE, row % SIDE
    order = jnp.stack(
        [(z_hi + i) % SIDE * SIDE + (x + j) % SIDE for i in HOPS for j in HOPS]
    )
    pick = (order[:, None] == jnp.arange(n_dp, dtype=jnp.int32)[None, :]).astype(BF)
    gates = jnp.dot(pick, part[:, 0, 2 * wide : 2 * wide + n_slots], preferred_element_type=F32)
    reps = lax.all_to_all(
        jnp.broadcast_to(rep_grad[None], (n_dp, 1, wide)), "dp", split_axis=0, concat_axis=0, tiled=True
    )
    reps = jnp.dot(pick, reps[:, 0], preferred_element_type=F32).astype(BF)
    reps = lax.all_to_all(
        jnp.broadcast_to(reps[None], (n_exp, n_dp, wide)), "expert", split_axis=0, concat_axis=0, tiled=True
    )
    reps = jnp.transpose(reps, (1, 0, 2)).reshape(n_dp * n_exp, wide)
    cot = contract(reps, head, 1, 1).astype(BF)
    back = contract(cot, second, 1, 1)
    back_hi = lax.reduce_precision(back, 8, 7)
    grad_in, grad_out = expert_grads(
        pieces, first, back_hi.astype(BF), (back - back_hi).astype(BF), gates.astype(BF), cot
    )
    return (grad_image, grad_in[None], grad_out[None])


def solution(mesh):
    placed = (
        P(("dp", "expert"), None),
        P(("dp", "expert"), None),
        P(("dp", "expert")),
        P("expert", None, "dp"),
        P("expert", "dp", None),
        P(),
        P(("dp", "expert"), None),
        P(("dp", "expert"), None),
        P(("dp", "expert")),
    )
    return jax.shard_map(
        body,
        mesh=mesh,
        in_specs=placed,
        out_specs=(P(("dp", "expert"), None), P("expert", None, "dp"), P("expert", "dp", None)),
        check_vma=False,
    )
```

time: 1290 us -> 304 us (0.24)
  waiting for transfers between devices: 1160 us -> 90.2 us
  starting transfers between devices: 0.12 us -> 98.2 us
  matrix products: 38.6 us -> 5.56 us
  Pallas kernels: 0 us -> 13.8 us
    all_gather x3 -> x0, waiting for transfers between devices: 1160 us -> none  [the longest x1 783 us: body(): captions = lax.all_gather(text_cache, ('dp', 'expert'), axis=0, tiled=True)]
    ppermute x0 -> x16, waiting for transfers between devices: none -> 76.8 us  [the longest x4 48.1 us: shift_z(): return lax.ppermute(a, 'dp', ring)]
    ppermute x0 -> x16, starting transfers between devices: none -> 59.2 us  [the longest x12 40.8 us: shift_x(): return lax.ppermute(a, 'dp', ring)]
    all_to_all x2 -> x1, blocking collectives: 79.2 us -> 22.1 us  [body(): part = lax.all_to_all(part, 'dp', split_axis=0, concat_axis=0, tiled=True)]
    all_gather x0 -> x1, blocking collectives: none -> 54.4 us  [body(): lax.all_gather(jnp.concatenate([image_cache, label_parts], axis=1), 'dp',...]
    all_to_all x0 -> x3, starting transfers between devices: none -> 39 us  [the longest x1 24.8 us: body(): lax.all_to_all(jnp.broadcast_to(reps[None], (n_exp, n_dp, wide)), 'expert...]
    dot_general x10, matrix products: 38.6 us -> 5.56 us  [the longest x5 3.81 us: contract(): lax.dot_general(a, b, (((da,), (db,)), ((), ())), preferred_element_type=...]
    pallas_call x0 -> x1, Pallas kernels: none -> 13.8 us  [expert_grads(): pl.pallas_call(expert_kernel, out_shape=(jax.ShapeDtypeStruct((width, hid...]
  transfers between devices with their start and end apart: 3 -> 19, of which waited for: 3 -> 7; matrix products, arithmetic and copies ran while one was open for 1% -> 2% of each run, Pallas kernels for 0% -> 0%
where the time goes in v1:
time: 304 us; the launch traced here: 298 us
  starting transfers between devices  98.2 us (32%)
  waiting for transfers between devices  90.2 us (30%)
  blocking collectives  76.5 us (25%)
  Pallas kernels  13.8 us (5%)
  local copies, waits for them, and re-layouts  8.72 us (3%)
  matrix products  5.56 us (2%)
  other arithmetic  3.55 us (1%)
    all_gather x1, blocking collectives, body(): lax.all_gather(jnp.concatenate([image_cache, label_parts], axis=1), 'dp',...  54.4 us
    ppermute x4, waiting for transfers between devices, shift_z(): return lax.ppermute(a, 'dp', ring)  48.1 us
    ppermute x12, starting transfers between devices, shift_x(): return lax.ppermute(a, 'dp', ring)  40.8 us
    ppermute x12, waiting for transfers between devices, shift_x(): return lax.ppermute(a, 'dp', ring)  28.7 us
    all_to_all x1, starting transfers between devices, body(): lax.all_to_all(jnp.broadcast_to(reps[None], (n_exp, n_dp, wide)), 'expert...  24.8 us
    all_to_all x1, blocking collectives, body(): part = lax.all_to_all(part, 'dp', split_axis=0, concat_axis=0, tiled=True)  22.1 us
    ppermute x4, starting transfers between devices, shift_z(): return lax.ppermute(a, 'dp', ring)  18.4 us
    pallas_call x1, Pallas kernels, expert_grads(): pl.pallas_call(expert_kernel, out_shape=(jax.ShapeDtypeStruct((width, hid...  13.8 us
  transfers between devices with their start and end apart: 19, of which 7 were waited for; matrix products, arithmetic and copies ran while one was open for 2% of the time, Pallas kernels for 0%

profile of v1, /device:TPU:1, one launch (start us, length us, event | category | flops | bytes accessed | tf_op | source)
XLA Modules:
  0.0 297.8 jit_solution(3862788520345876843)
XLA Ops:
  0.6 0.9 fusion.2
  1.6 0.7 fusion.35
  2.2 0.9 fusion.1
  3.2 1.4 fusion
  4.5 0.7 broadcast_in_dim.16
  5.3 1.0 pad_maximum_fusion
  6.2 10.6 %all-to-all-start = ((bf16[32,8,1664]{2,1,0:T(8,128)(2,1)}), bf16[32,8,1664]{2,1,0:T(8,128)(2,1)S(1)}, u32[]{:S(2)}, u32[]{:S(2)}) async-start(bf16[32,8,1664]{2,1,0:T(8,128)(2,1)} %pad_maximum_fusion), calls=%async_computation | async-start | bytes 1703936 | tf_op jit(solution)/shard_map/all_to_all | solution.py:143
  17.0 54.4 %all_gather.3 = bf16[128,640]{1,0:T(8,128)(2,1)S(1)} all-gather(bf16[8,640]{1,0:T(8,128)(2,1)S(1)} %fusion.25), channel_id=1, replica_groups=mesh['dp'=16,'expert'=32] {'dp'}, dimensions={0}, use_global_device_ids=true | all-gather | bytes 174080 | tf_op jit(solution)/shard_map/all_gather | solution.py:127
  71.4 0.2 add_reduce_fusion
  71.5 0.3 fusion.36
  71.9 0.2 fusion.12
  72.1 0.1 copy.49
  72.2 0.1 convert_reduce_fusion.1
  72.3 0.1 select_reduce_fusion
  72.5 0.2 convolution_convert_fusion.3
  72.7 0.2 convolution_convert_fusion.2
  73.0 22.1 %all_to_all.20 = bf16[16,8,1408]{2,1,0:T(8,128)(2,1)S(1)} all-to-all(bf16[16,8,1408]{2,1,0:T(8,128)(2,1)S(1)} %fusion.8), channel_id=1, replica_groups=mesh['dp'=16,'expert'=32] {'dp'}, dimensions={0} | all-to-all | bytes 720896 | tf_op jit(solution)/shard_map/all_to_all | solution.py:170
  95.1 0.2 copy.50
  95.4 0.1 slice_reduce_fusion
  95.5 0.2 fusion.28
  95.8 0.1 multiply_reduce_fusion
  95.9 0.1 copy.58
  96.0 0.1 copy.59
  96.2 0.1 fusion.9
  96.3 0.5 broadcast.78
  96.9 0.7 reduce.8
  97.6 0.6 reshape.95
  98.2 3.6 %all-to-all-start.2 = ((bf16[16,2,256]{2,1,0:T(2,128)(2,1)}), bf16[16,2,256]{2,1,0:T(2,128)(2,1)S(1)}, u32[]{:S(2)}, u32[]{:S(2)}) async-start(bf16[16,2,256]{2,1,0:T(2,128)(2,1)} %reshape.95), calls=%async_computation.2 | async-start | bytes 32768 | tf_op jit(solution)/shard_map/all_to_all | solution.py:186
  102.1 13.4 %all-to-all-done.2 = bf16[16,2,256]{2,1,0:T(2,128)(2,1)S(1)} async-done(((bf16[16,2,256]{2,1,0:T(2,128)(2,1)}), bf16[16,2,256]{2,1,0:T(2,128)(2,1)S(1)}, u32[]{:S(2)}, u32[]{:S(2)}) %all-to-all-start.2) | async-done | bytes 16416 | tf_op jit(solution)/shard_map/all_to_all | solution.py:186
  115.5 0.2 convolution_convert_fusion.5
  115.7 0.8 broadcast_in_dim.21
  116.5 24.8 %all-to-all-start.3 = ((bf16[32,16,512]{2,1,0:T(8,128)(2,1)}), bf16[32,16,512]{2,1,0:T(8,128)(2,1)}, u32[]{:S(2)}, u32[]{:S(2)}) async-start(bf16[32,16,512]{2,1,0:T(8,128)(2,1)} %broadcast_in_dim.21), calls=%async_computation.3 | async-start | bytes 1048576 | tf_op jit(solution)/shard_map/all_to_all | solution.py:190
  141.4 2.2 collective-permute-start.3
  143.7 7.0 %collective-permute-start.7 = (bf16[256,1024]{1,0:T(8,128)(2,1)S(1)}, bf16[256,1024]{1,0:T(8,128)(2,1)S(1)}, u32[]{:S(2)}, u32[]{:S(2)}) collective-permute-start(bf16[256,1024]{1,0:T(8,128)(2,1)S(1)} %slice_bitcast_fusion.refs_0_), channel_id=1, source_target_pairs={{0,384},{32,416},{64,448},{96,480},{128,0},{160,32},{192,64},{224,... | collective-permute-start | bytes 1572872 | tf_op jit(solution)/shard_map/ppermute | solution.py:35
  150.6 2.8 collective-permute-start.1
  153.4 2.5 collective-permute-start
  155.9 35.3 %collective-permute-done.3.refs_4_ = bf16[256,1024]{1,0:T(8,128)(2,1)S(1)} collective-permute-done((bf16[256,1024]{1,0:T(8,128)(2,1)S(1)}, bf16[256,1024]{1,0:T(8,128)(2,1)S(1)}, u32[]{:S(2)}, u32[]{:S(2)}) %collective-permute-start.3) | collective-permute-done | bytes 524320 | tf_op jit(solution)/shard_map/ppermute | solution.py:35
  191.2 6.2 %collective-permute-start.11 = (bf16[128,1024]{1,0:T(8,128)(2,1)S(1)}, bf16[128,1024]{1,0:T(8,128)(2,1)S(1)}, u32[]{:S(2)}, u32[]{:S(2)}) collective-permute-start(bf16[128,1024]{1,0:T(8,128)(2,1)S(1)} %slice.82), channel_id=1, source_target_pairs={{0,128},{32,160},{64,192},{96,224},{128,256},{160,288},{192,320},{... | collective-permute-start | bytes 786440 | tf_op jit(solution)/shard_map/ppermute | solution.py:35
  197.4 3.0 %collective-permute-start.12 = (bf16[128,1024]{1,0:T(8,128)(2,1)S(1)}, bf16[128,1024]{1,0:T(8,128)(2,1)S(1)}, u32[]{:S(2)}, u32[]{:S(2)}) collective-permute-start(bf16[128,1024]{1,0:T(8,128)(2,1)S(1)} %slice.83), channel_id=1, source_target_pairs={{0,384},{32,416},{64,448},{96,480},{128,0},{160,32},{192,64},{224,... | collective-permute-start | bytes 786440 | tf_op jit(solution)/shard_map/ppermute | solution.py:35
  200.5 2.8 collective-permute-start.9
  203.3 12.8 %collective-permute-done.11 = bf16[128,1024]{1,0:T(8,128)(2,1)S(1)} collective-permute-done((bf16[128,1024]{1,0:T(8,128)(2,1)S(1)}, bf16[128,1024]{1,0:T(8,128)(2,1)S(1)}, u32[]{:S(2)}, u32[]{:S(2)}) %collective-permute-start.11) | collective-permute-done | bytes 262176 | tf_op jit(solution)/shard_map/ppermute | solution.py:35
  216.1 2.2 collective-permute-start.8
  218.3 10.8 %collective-permute-start.5 = (bf16[256,1024]{1,0:T(8,128)(2,1)S(1)}, bf16[256,1024]{1,0:T(8,128)(2,1)}, u32[]{:S(2)}, u32[]{:S(2)}) collective-permute-start(bf16[256,1024]{1,0:T(8,128)(2,1)S(1)} %collective-permute-done.3.refs_4_), channel_id=1, source_target_pairs={{0,96},{32,0},{64,32},{96,64},{128,224},{160,128},{192,160},{224,1... | collective-permute-start | bytes 1572872 | tf_op jit(solution)/shard_map/ppermute | solution.py:42
  229.2 0.8 copy-done.2
  230.0 1.9 collective-permute-start.4
  231.9 0.8 copy-done.4
  232.7 4.6 %collective-permute-start.14 = (bf16[256,1024]{1,0:T(8,128)(2,1)S(1)}, bf16[256,1024]{1,0:T(8,128)(2,1)}, u32[]{:S(2)}, u32[]{:S(2)}) collective-permute-start(bf16[256,1024]{1,0:T(8,128)(2,1)S(1)} %constant_dynamic-update-slice_fusion.refs_12_), channel_id=1, source_target_pairs={{0,96},{32,0},{64,32},{96,64},{128,224},{160,128},{192,160},{224,1... | collective-permute-start | bytes 1572872 | tf_op jit(solution)/shard_map/ppermute | solution.py:42
  237.3 0.7 copy.56
  238.0 0.8 slice.85
  238.8 0.2 convolution_convert_fusion.6.refs_19_
  239.0 1.4 copy.54
  240.5 1.9 collective-permute-start.2
  242.4 1.9 collective-permute-start.13
  244.3 3.0 %collective-permute-start.10 = (bf16[256,1024]{1,0:T(8,128)(2,1)}, bf16[256,1024]{1,0:T(8,128)(2,1)S(1)}, u32[]{:S(2)}, u32[]{:S(2)}) collective-permute-start(bf16[256,1024]{1,0:T(8,128)(2,1)} %collective-permute-done.8.refs_9_), channel_id=1, source_target_pairs={{0,32},{32,64},{64,96},{96,0},{128,160},{160,192},{192,224},{224,1... | collective-permute-start | bytes 1572872 | tf_op jit(solution)/shard_map/ppermute | solution.py:42
  247.3 3.0 %collective-permute-done.4.refs_5_ = bf16[256,1024]{1,0:T(8,128)(2,1)} collective-permute-done((bf16[256,1024]{1,0:T(8,128)(2,1)S(1)}, bf16[256,1024]{1,0:T(8,128)(2,1)}, u32[]{:S(2)}, u32[]{:S(2)}) %collective-permute-start.4) | collective-permute-done | bytes 524320 | tf_op jit(solution)/shard_map/ppermute | solution.py:42
  250.4 3.0 %collective-permute-start.6 = (bf16[256,1024]{1,0:T(8,128)(2,1)}, bf16[256,1024]{1,0:T(8,128)(2,1)S(1)}, u32[]{:S(2)}, u32[]{:S(2)}) collective-permute-start(bf16[256,1024]{1,0:T(8,128)(2,1)} %collective-permute-done.5.refs_6_), channel_id=1, source_target_pairs={{0,96},{32,0},{64,32},{96,64},{128,224},{160,128},{192,160},{224,1... | collective-permute-start | bytes 1572872 | tf_op jit(solution)/shard_map/ppermute | solution.py:42
  253.4 3.3 %collective-permute-start.15 = (bf16[256,1024]{1,0:T(8,128)(2,1)}, bf16[256,1024]{1,0:T(8,128)(2,1)S(1)}, u32[]{:S(2)}, u32[]{:S(2)}) collective-permute-start(bf16[256,1024]{1,0:T(8,128)(2,1)} %collective-permute-done.14.refs_14_), channel_id=1, source_target_pairs={{0,96},{32,0},{64,32},{96,64},{128,224},{160,128},{192,160},{224,1... | collective-permute-start | bytes 1572872 | tf_op jit(solution)/shard_map/ppermute | solution.py:42
  256.8 0.7 convolution_convert_fusion.refs_20_
  257.5 0.3 copy-done.8
  257.8 0.5 fusion.4
  258.3 3.2 %collective-permute-done.2.refs_3_ = bf16[256,1024]{1,0:T(8,128)(2,1)S(1)} collective-permute-done((bf16[256,1024]{1,0:T(8,128)(2,1)S(1)}, bf16[256,1024]{1,0:T(8,128)(2,1)S(1)}, u32[]{:S(2)}, u32[]{:S(2)}) %collective-permute-start.2) | collective-permute-done | bytes 524320 | tf_op jit(solution)/shard_map/ppermute | solution.py:42
  261.5 11.2 %collective-permute-done.13.refs_13_ = bf16[256,1024]{1,0:T(8,128)(2,1)S(1)} collective-permute-done((bf16[256,1024]{1,0:T(8,128)(2,1)S(1)}, bf16[256,1024]{1,0:T(8,128)(2,1)S(1)}, u32[]{:S(2)}, u32[]{:S(2)}) %collective-permute-start.13) | collective-permute-done | bytes 524320 | tf_op jit(solution)/shard_map/ppermute | solution.py:42
  272.7 11.2 %collective-permute-done.10.refs_11_ = bf16[256,1024]{1,0:T(8,128)(2,1)S(1)} collective-permute-done((bf16[256,1024]{1,0:T(8,128)(2,1)}, bf16[256,1024]{1,0:T(8,128)(2,1)S(1)}, u32[]{:S(2)}, u32[]{:S(2)}) %collective-permute-start.10) | collective-permute-done | bytes 524320 | tf_op jit(solution)/shard_map/ppermute | solution.py:42
  284.0 13.8 %shard_map.112 = (f32[1024,256]{1,0:T(8,128)}, f32[256,1024]{1,0:T(8,128)}) custom-call(bf16[256,1024]{1,0:T(8,128)(2,1)S(1)} %slice_bitcast_fusion.refs_0_, bf16[256,1024]{1,0:T(8,128)(2,1)S(1)} %copy-done.5, bf16[256,1024]{1,0:T(8,128)(2,1)S(1)} %copy-done.3, bf16[256,1024]{1,0:T(8,128)(2,1)S(1)} %collective-permute-done.2.refs_3_, ...), custom_call_target="tpu_custom_call" | custom-call | flops 5000000000 | bytes 13000000 | tf_op jit(solution)/shard_map/pallas_call | solution.py:95
  (52 shorter events, 0.7 us)
Async XLA Ops:
  0.6 256.1 %copy-start = (bf16[1024,512]{1,0:T(8,128)(2,1)S(1)}, bf16[1024,512]{1,0:T(8,128)(2,1)}, u32[]{:S(2)}) copy-start(bf16[1024,512]{1,0:T(8,128)(2,1)} %param.14) | copy-start | bytes 3145732
  6.2 10.6 %copy-start.9 = (s32[8]{0:T(128)S(1)}, s32[8]{0:T(128)}, u32[]{:S(2)}) copy-start(s32[8]{0:T(128)} %param.17) | copy-start | bytes 100
  6.2 10.7 %copy-start.7 = (bf16[8,512]{1,0:T(8,128)(2,1)S(1)}, bf16[8,512]{1,0:T(8,128)(2,1)}, u32[]{:S(2)}) copy-start(bf16[8,512]{1,0:T(8,128)(2,1)} %param.15) | copy-start | bytes 24580
  6.2 65.3 %all-to-all-start = ((bf16[32,8,1664]{2,1,0:T(8,128)(2,1)}), bf16[32,8,1664]{2,1,0:T(8,128)(2,1)S(1)}, u32[]{:S(2)}, u32[]{:S(2)}) async-start(bf16[32,8,1664]{2,1,0:T(8,128)(2,1)} %pad_maximum_fusion), calls=%async_computation | async-start | bytes 1703936 | tf_op jit(solution)/shard_map/all_to_all | solution.py:143
  95.1 46.3 %copy-start.6 = (bf16[16,8,1408]{2,1,0:T(8,128)(2,1)}, bf16[16,8,1408]{2,1,0:T(8,128)(2,1)S(1)}, u32[]{:S(2)}) copy-start(bf16[16,8,1408]{2,1,0:T(8,128)(2,1)S(1)} %all_to_all.20) | copy-start | bytes 1081348
  98.2 17.3 %all-to-all-start.2 = ((bf16[16,2,256]{2,1,0:T(2,128)(2,1)}), bf16[16,2,256]{2,1,0:T(2,128)(2,1)S(1)}, u32[]{:S(2)}, u32[]{:S(2)}) async-start(bf16[16,2,256]{2,1,0:T(2,128)(2,1)} %reshape.95), calls=%async_computation.2 | async-start | bytes 32768 | tf_op jit(solution)/shard_map/all_to_all | solution.py:186
  116.5 122.5 %all-to-all-start.3 = ((bf16[32,16,512]{2,1,0:T(8,128)(2,1)}), bf16[32,16,512]{2,1,0:T(8,128)(2,1)}, u32[]{:S(2)}, u32[]{:S(2)}) async-start(bf16[32,16,512]{2,1,0:T(8,128)(2,1)} %broadcast_in_dim.21), calls=%async_computation.3 | async-start | bytes 1048576 | tf_op jit(solution)/shard_map/all_to_all | solution.py:190
  141.4 49.8 %collective-permute-start.3 = (bf16[256,1024]{1,0:T(8,128)(2,1)S(1)}, bf16[256,1024]{1,0:T(8,128)(2,1)S(1)}, u32[]{:S(2)}, u32[]{:S(2)}) collective-permute-start(bf16[256,1024]{1,0:T(8,128)(2,1)S(1)} %slice_bitcast_fusion.refs_0_), channel_id=1, source_target_pairs={{0,128},{32,160},{64,192},{96,224},{128,256},{160,288},{192,320},{... | collective-permute-start | bytes 1572872 | tf_op jit(solution)/shard_map/ppermute | solution.py:35
  143.7 53.8 %collective-permute-start.7 = (bf16[256,1024]{1,0:T(8,128)(2,1)S(1)}, bf16[256,1024]{1,0:T(8,128)(2,1)S(1)}, u32[]{:S(2)}, u32[]{:S(2)}) collective-permute-start(bf16[256,1024]{1,0:T(8,128)(2,1)S(1)} %slice_bitcast_fusion.refs_0_), channel_id=1, source_target_pairs={{0,384},{32,416},{64,448},{96,480},{128,0},{160,32},{192,64},{224,... | collective-permute-start | bytes 1572872 | tf_op jit(solution)/shard_map/ppermute | solution.py:35
  150.6 78.6 %collective-permute-start.1 = (bf16[256,1024]{1,0:T(8,128)(2,1)S(1)}, bf16[256,1024]{1,0:T(8,128)(2,1)S(1)}, u32[]{:S(2)}, u32[]{:S(2)}) collective-permute-start(bf16[256,1024]{1,0:T(8,128)(2,1)S(1)} %slice_bitcast_fusion.refs_0_), channel_id=1, source_target_pairs={{0,96},{32,0},{64,32},{96,64},{128,224},{160,128},{192,160},{224,1... | collective-permute-start | bytes 1572872 | tf_op jit(solution)/shard_map/ppermute | solution.py:42
  153.4 78.5 %collective-permute-start = (bf16[256,1024]{1,0:T(8,128)(2,1)S(1)}, bf16[256,1024]{1,0:T(8,128)(2,1)S(1)}, u32[]{:S(2)}, u32[]{:S(2)}) collective-permute-start(bf16[256,1024]{1,0:T(8,128)(2,1)S(1)} %slice_bitcast_fusion.refs_0_), channel_id=1, source_target_pairs={{0,32},{32,64},{64,96},{96,0},{128,160},{160,192},{192,224},{224,1... | collective-permute-start | bytes 1572872 | tf_op jit(solution)/shard_map/ppermute | solution.py:42
  191.2 24.9 %collective-permute-start.11 = (bf16[128,1024]{1,0:T(8,128)(2,1)S(1)}, bf16[128,1024]{1,0:T(8,128)(2,1)S(1)}, u32[]{:S(2)}, u32[]{:S(2)}) collective-permute-start(bf16[128,1024]{1,0:T(8,128)(2,1)S(1)} %slice.82), channel_id=1, source_target_pairs={{0,128},{32,160},{64,192},{96,224},{128,256},{160,288},{192,320},{... | collective-permute-start | bytes 786440 | tf_op jit(solution)/shard_map/ppermute | solution.py:35
  197.4 20.9 %collective-permute-start.12 = (bf16[128,1024]{1,0:T(8,128)(2,1)S(1)}, bf16[128,1024]{1,0:T(8,128)(2,1)S(1)}, u32[]{:S(2)}, u32[]{:S(2)}) collective-permute-start(bf16[128,1024]{1,0:T(8,128)(2,1)S(1)} %slice.83), channel_id=1, source_target_pairs={{0,384},{32,416},{64,448},{96,480},{128,0},{160,32},{192,64},{224,... | collective-permute-start | bytes 786440 | tf_op jit(solution)/shard_map/ppermute | solution.py:35
  200.5 40.0 %collective-permute-start.9 = (bf16[256,1024]{1,0:T(8,128)(2,1)S(1)}, bf16[256,1024]{1,0:T(8,128)(2,1)}, u32[]{:S(2)}, u32[]{:S(2)}) collective-permute-start(bf16[256,1024]{1,0:T(8,128)(2,1)S(1)} %collective-permute-done.7.refs_8_), channel_id=1, source_target_pairs={{0,96},{32,0},{64,32},{96,64},{128,224},{160,128},{192,160},{224,1... | collective-permute-start | bytes 1572872 | tf_op jit(solution)/shard_map/ppermute | solution.py:42
  216.1 26.3 %collective-permute-start.8 = (bf16[256,1024]{1,0:T(8,128)(2,1)S(1)}, bf16[256,1024]{1,0:T(8,128)(2,1)}, u32[]{:S(2)}, u32[]{:S(2)}) collective-permute-start(bf16[256,1024]{1,0:T(8,128)(2,1)S(1)} %collective-permute-done.7.refs_8_), channel_id=1, source_target_pairs={{0,32},{32,64},{64,96},{96,0},{128,160},{160,192},{192,224},{224,1... | collective-permute-start | bytes 1572872 | tf_op jit(solution)/shard_map/ppermute | solution.py:42
  218.3 26.0 %collective-permute-start.5 = (bf16[256,1024]{1,0:T(8,128)(2,1)S(1)}, bf16[256,1024]{1,0:T(8,128)(2,1)}, u32[]{:S(2)}, u32[]{:S(2)}) collective-permute-start(bf16[256,1024]{1,0:T(8,128)(2,1)S(1)} %collective-permute-done.3.refs_4_), channel_id=1, source_target_pairs={{0,96},{32,0},{64,32},{96,64},{128,224},{160,128},{192,160},{224,1... | collective-permute-start | bytes 1572872 | tf_op jit(solution)/shard_map/ppermute | solution.py:42
  229.2 0.8 copy-start.2
  230.0 20.4 %collective-permute-start.4 = (bf16[256,1024]{1,0:T(8,128)(2,1)S(1)}, bf16[256,1024]{1,0:T(8,128)(2,1)}, u32[]{:S(2)}, u32[]{:S(2)}) collective-permute-start(bf16[256,1024]{1,0:T(8,128)(2,1)S(1)} %collective-permute-done.3.refs_4_), channel_id=1, source_target_pairs={{0,32},{32,64},{64,96},{96,0},{128,160},{160,192},{192,224},{224,1... | collective-permute-start | bytes 1572872 | tf_op jit(solution)/shard_map/ppermute | solution.py:42
  231.9 0.8 copy-start.4
  232.7 20.7 %collective-permute-start.14 = (bf16[256,1024]{1,0:T(8,128)(2,1)S(1)}, bf16[256,1024]{1,0:T(8,128)(2,1)}, u32[]{:S(2)}, u32[]{:S(2)}) collective-permute-start(bf16[256,1024]{1,0:T(8,128)(2,1)S(1)} %constant_dynamic-update-slice_fusion.refs_12_), channel_id=1, source_target_pairs={{0,96},{32,0},{64,32},{96,64},{128,224},{160,128},{192,160},{224,1... | collective-permute-start | bytes 1572872 | tf_op jit(solution)/shard_map/ppermute | solution.py:42
  239.0 1.4 copy-start.5
  240.5 21.0 %collective-permute-start.2 = (bf16[256,1024]{1,0:T(8,128)(2,1)S(1)}, bf16[256,1024]{1,0:T(8,128)(2,1)S(1)}, u32[]{:S(2)}, u32[]{:S(2)}) collective-permute-start(bf16[256,1024]{1,0:T(8,128)(2,1)S(1)} %copy-done.5), channel_id=1, source_target_pairs={{0,32},{32,64},{64,96},{96,0},{128,160},{160,192},{192,224},{224,1... | collective-permute-start | bytes 1572872 | tf_op jit(solution)/shard_map/ppermute | solution.py:42
  242.4 30.3 %collective-permute-start.13 = (bf16[256,1024]{1,0:T(8,128)(2,1)S(1)}, bf16[256,1024]{1,0:T(8,128)(2,1)S(1)}, u32[]{:S(2)}, u32[]{:S(2)}) collective-permute-start(bf16[256,1024]{1,0:T(8,128)(2,1)S(1)} %constant_dynamic-update-slice_fusion.refs_12_), channel_id=1, source_target_pairs={{0,32},{32,64},{64,96},{96,0},{128,160},{160,192},{192,224},{224,1... | collective-permute-start | bytes 1572872 | tf_op jit(solution)/shard_map/ppermute | solution.py:42
  244.3 39.6 %collective-permute-start.10 = (bf16[256,1024]{1,0:T(8,128)(2,1)}, bf16[256,1024]{1,0:T(8,128)(2,1)S(1)}, u32[]{:S(2)}, u32[]{:S(2)}) collective-permute-start(bf16[256,1024]{1,0:T(8,128)(2,1)} %collective-permute-done.8.refs_9_), channel_id=1, source_target_pairs={{0,32},{32,64},{64,96},{96,0},{128,160},{160,192},{192,224},{224,1... | collective-permute-start | bytes 1572872 | tf_op jit(solution)/shard_map/ppermute | solution.py:42
  250.4 33.6 %collective-permute-start.6 = (bf16[256,1024]{1,0:T(8,128)(2,1)}, bf16[256,1024]{1,0:T(8,128)(2,1)S(1)}, u32[]{:S(2)}, u32[]{:S(2)}) collective-permute-start(bf16[256,1024]{1,0:T(8,128)(2,1)} %collective-permute-done.5.refs_6_), channel_id=1, source_target_pairs={{0,96},{32,0},{64,32},{96,64},{128,224},{160,128},{192,160},{224,1... | collective-permute-start | bytes 1572872 | tf_op jit(solution)/shard_map/ppermute | solution.py:42
  253.4 30.6 %collective-permute-start.15 = (bf16[256,1024]{1,0:T(8,128)(2,1)}, bf16[256,1024]{1,0:T(8,128)(2,1)S(1)}, u32[]{:S(2)}, u32[]{:S(2)}) collective-permute-start(bf16[256,1024]{1,0:T(8,128)(2,1)} %collective-permute-done.14.refs_14_), channel_id=1, source_target_pairs={{0,96},{32,0},{64,32},{96,64},{128,224},{160,128},{192,160},{224,1... | collective-permute-start | bytes 1572872 | tf_op jit(solution)/shard_map/ppermute | solution.py:42
  256.8 1.0 copy-start.8
  257.8 26.2 %copy-start.1 = (bf16[1,1024,256]{2,1,0:T(8,128)(2,1)S(1)}, bf16[1,1024,256]{2,1,0:T(8,128)(2,1)}, u32[]{:S(2)}) copy-start(bf16[1,1024,256]{2,1,0:T(8,128)(2,1)} %param.12) | copy-start | bytes 1572868
  257.8 26.2 %copy-start.3 = (bf16[256,1024]{1,0:T(8,128)(2,1)S(1)}, bf16[256,1024]{1,0:T(8,128)(2,1)}, u32[]{:S(2)}) copy-start(bf16[256,1024]{1,0:T(8,128)(2,1)} %copy-done.2) | copy-start | bytes 1572868

commit v2 on v0

v2 whole, which is shorter than its diff:
```python
import jax
import jax.numpy as jnp
import numpy as np
from jax import lax
from jax.experimental import pallas as pl
from jax.experimental.pallas import tpu as pltpu
from jax.sharding import PartitionSpec as P

LOGIT_SCALE = 0.125
GELU_K = 0.7978845608
GELU_C = 0.044715
SIDE = 4
SIDES = {
    "z_hi": ("dp", (SIDE, SIDE), 0),
    "x": ("dp", (SIDE, SIDE), 1),
    "y": ("expert", (SIDE, SIDE, 2), 0),
    "z_lo": ("expert", (SIDE, SIDE, 2), 1),
    "core": ("expert", (SIDE, SIDE, 2), 2),
}
BF = jnp.bfloat16
F32 = jnp.float32


def contract(a, b, da, db):
    return lax.dot_general(a, b, (((da,), (db,)), ((), ())), preferred_element_type=F32)


def gelu_parts(pre):
    inner = GELU_K * (pre + GELU_C * pre * pre * pre)
    tangent = jnp.tanh(inner)
    value = 0.5 * pre * (1.0 + tangent)
    slope = 0.5 * (1.0 + tangent) + 0.5 * pre * (1.0 - tangent * tangent) * GELU_K * (
        1.0 + 3.0 * GELU_C * pre * pre
    )
    return (value, slope)


def shift(a, axis, by):
    name, sizes, side = SIDES[axis]
    ring = []
    for at in np.ndindex(*sizes):
        to = list(at)
        to[side] = (to[side] + by) % sizes[side]
        ring.append((int(np.ravel_multi_index(at, sizes)), int(np.ravel_multi_index(to, sizes))))
    return lax.ppermute(a, name, ring)


def spread_along(a, axis):
    name, sizes, side = SIDES[axis]
    return [a] + [shift(a, axis, k) for k in range(1, sizes[side])]


def gather_x(a):
    rows = [[z * SIDE + x for x in range(SIDE)] for z in range(SIDE)]
    return lax.all_gather(a, "dp", axis=0, tiled=True, axis_index_groups=rows)


def after(a, *others):
    return lax.optimization_barrier((a, *others))[0]


def loss_kernel(*refs):
    n = 4 * SIDE // 2
    parts = refs[:n]
    want_ref, image_ref, own_meta_ref, head_ref, second_ref = refs[n : n + 5]
    grad_image_ref, cot_ref, back_hi_ref, back_lo_ref, gate_ref = refs[n + 5 : n + 10]
    images, reps, metas, logit, weights, hits = refs[n + 10 :]
    n_rep = want_ref.shape[0]
    n_own = image_ref.shape[0]
    n_all = images.shape[0]
    each = n_rep // n // SIDE
    step = n_own * each * SIDE
    block = (n_own + 2) * each
    row, expert = lax.axis_index("dp"), lax.axis_index("expert")
    z_hi, x = row >> 2, row & 3
    y, z_lo, core = expert >> 3, expert >> 1 & 3, expert & 1

    def device(part, k):
        at = ((z_hi - (k & 3)) & 3) * 4 + ((x - (k >> 4)) & 3)
        at = (at * 4 + ((y - part % SIDE) & 3)) * 4 + ((z_lo - (k >> 2 & 3)) & 3)
        return at * 2 + ((core - part // SIDE) & 1)

    def counted(size):
        return lax.broadcasted_iota(jnp.int32, (1, size), 1)

    def gathered(offset):
        for p, ref in enumerate(parts):
            for q in range(SIDE):
                to = (p * SIDE + q) * each
                reps[pl.ds(to, each), :] = ref[pl.ds(q * block + offset, each), :]
        return reps[...]

    def captions(ref):
        return jnp.concatenate([ref[pl.ds(q * block, n_own * each), :] for q in range(SIDE)], axis=0)

    sources = jnp.concatenate([device(p, counted(SIDE * each)) for p in range(n)], axis=1)
    pick = (want_ref[...] == sources).astype(BF)
    images[:n_rep, :] = jnp.dot(pick, gathered(n_own * each), preferred_element_type=F32).astype(BF)
    images[n_rep:, :] = jnp.zeros((n_all - n_rep, images.shape[1]), BF)
    images[n_rep : n_rep + n_own, :] = image_ref[...]
    found = jnp.dot(pick, gathered((n_own + 1) * each), preferred_element_type=F32)
    width = found.shape[1]
    source = lax.broadcasted_iota(jnp.int32, (width, 128), 0)
    slot = lax.broadcasted_iota(jnp.int32, (width, 128), 1)
    label_at = 256
    select = jnp.where(slot < 8, expert * 8 + slot, label_at + slot - 8)
    select = ((source == select) & (slot < 10)).astype(BF)
    found = jnp.dot(found.astype(BF), select, preferred_element_type=F32)
    gate_ref[...] = found.astype(BF)
    metas[:n_rep, :] = found
    metas[n_rep:, :] = jnp.full((n_all - n_rep, 128), -8.0, F32)
    metas[n_rep : n_rep + n_own, :] = own_meta_ref[...]
    labels = (metas[:, 8:9] * 64.0 + metas[:, 9:10]).astype(jnp.int32)
    top = None
    for p, ref in enumerate(parts):
        ids = device(p, counted(step) >> 3) * 8 + (counted(step) & 7)
        part = LOGIT_SCALE * contract(images[...], captions(ref), 1, 1)
        logit[:, pl.ds(p * step, step)] = part
        hits[:, pl.ds(p * step, step)] = (labels == ids).astype(BF)
        peak = jnp.max(part, axis=1, keepdims=True)
        top = peak if top is None else jnp.maximum(top, peak)
    total = jnp.zeros((n_all, 1), F32)
    for p in range(n):
        expo = jnp.exp(logit[:, pl.ds(p * step, step)] - top)
        total = total + jnp.sum(expo, axis=1, keepdims=True)
        weights[:, pl.ds(p * step, step)] = expo.astype(BF)
    mix, labelled = jnp.zeros(images.shape, F32), jnp.zeros(images.shape, F32)
    for p, ref in enumerate(parts):
        rows = captions(ref)
        mix += jnp.dot(weights[:, pl.ds(p * step, step)], rows, preferred_element_type=F32)
        labelled += jnp.dot(hits[:, pl.ds(p * step, step)], rows, preferred_element_type=F32)
    grad = LOGIT_SCALE * (mix / total - labelled)
    grad_image_ref[...] = grad[n_rep : n_rep + n_own, :]
    cot = contract(grad[:n_rep].astype(BF), head_ref[...], 1, 1).astype(BF)
    cot_ref[...] = cot
    back = contract(cot, second_ref[...], 1, 1)
    back_hi = back.astype(BF)
    back_hi_ref[...] = back_hi
    back_lo_ref[...] = (back - back_hi.astype(F32)).astype(BF)


def image_grads(parts, want, image_cache, own_meta, head, second):
    n_rep, n_own, wide = want.shape[0], image_cache.shape[0], image_cache.shape[1]
    n_all = n_rep + 16
    n_text = n_rep * n_own
    hidden, width = second.shape
    vmem = pl.BlockSpec(memory_space=pltpu.VMEM)
    return pl.pallas_call(
        loss_kernel,
        out_shape=(
            jax.ShapeDtypeStruct((n_own, wide), F32),
            jax.ShapeDtypeStruct((n_rep, width), BF),
            jax.ShapeDtypeStruct((n_rep, hidden), BF),
            jax.ShapeDtypeStruct((n_rep, hidden), BF),
            jax.ShapeDtypeStruct((n_rep, 128), BF),
        ),
        in_specs=[vmem] * (len(parts) + 5),
        out_specs=(vmem,) * 5,
        scratch_shapes=[
            pltpu.VMEM((n_all, wide), BF),
            pltpu.VMEM((n_rep, wide), BF),
            pltpu.VMEM((n_all, 128), F32),
            pltpu.VMEM((n_all, n_text), F32),
            pltpu.VMEM((n_all, n_text), BF),
            pltpu.VMEM((n_all, n_text), BF),
        ],
        compiler_params=pltpu.CompilerParams(vmem_limit_bytes=60 * 1024 * 1024),
        cost_estimate=pl.CostEstimate(
            flops=10_000_000_000, bytes_accessed=9_000_000, transcendentals=3_000_000
        ),
    )(*parts, want, image_cache, own_meta, head, second)


def expert_kernel(*refs):
    n = len(refs) - 16
    sources, targets = refs[: n + 5], refs[n + 7 : n + 12]
    grad_in_ref, grad_out_ref = refs[n + 5 : n + 7]
    acc, sums, held = refs[n + 12 : n + 15]
    sems = refs[n + 15]
    first_ref, back_hi_ref, back_lo_ref, gate_ref, cot_ref = targets
    copies, at = [], 0
    for i in range(5):
        copies.append(pltpu.make_async_copy(sources[n + i], targets[i], sems.at[n + i]))
    for i in range(n):
        size = sources[i].shape[0]
        copies.append(pltpu.make_async_copy(sources[i], held.at[pl.ds(at, size)], sems.at[i]))
        at += size
    for copy in copies[:4] + copies[5:] + copies[4:5]:
        copy.start()
    for copy in copies[:4]:
        copy.wait()
    images = 32
    per = 8
    rows = images * per
    first = first_ref[...]
    column = lax.broadcasted_iota(jnp.int32, (images, rows), 1)
    mask = column // per == lax.broadcasted_iota(jnp.int32, (images, rows), 0)
    widen = (
        lax.broadcasted_iota(jnp.int32, (128, rows), 1) % per
        == lax.broadcasted_iota(jnp.int32, (128, rows), 0)
    ).astype(BF)
    c = 0
    for i in range(n):
        copies[5 + i].wait()
        for _ in range(sources[i].shape[0] // rows):
            here = pl.ds(c * images, images)
            x = held[pl.ds(c * rows, rows), :]
            gates = jnp.dot(gate_ref[here, :], widen, preferred_element_type=F32)
            spread = jnp.where(mask, gates, 0.0).astype(BF)
            pre = jnp.dot(x, first, preferred_element_type=F32)
            value, slope = gelu_parts(pre)
            hidden = value.astype(BF)
            back = contract(spread, back_hi_ref[here, :], 0, 0) + contract(
                spread, back_lo_ref[here, :], 0, 0
            )
            hidden_grad = (back * slope).astype(BF)
            term = contract(hidden_grad, x, 0, 0)
            if c == 0:
                acc[...] = term
            else:
                acc[...] += term
            sums[here, :] = jnp.dot(spread, hidden, preferred_element_type=F32).astype(BF)
            c += 1
    copies[4].wait()
    grad_in_ref[...] = acc[...].T
    grad_out_ref[...] = contract(sums[...], cot_ref[...], 0, 0)


def expert_grads(pieces, first, back_hi, back_lo, gates, cot):
    width, hidden = first.shape
    vmem = pl.BlockSpec(memory_space=pltpu.VMEM)
    rest = (first, back_hi, back_lo, gates, cot)
    return pl.pallas_call(
        expert_kernel,
        out_shape=(
            jax.ShapeDtypeStruct((width, hidden), F32),
            jax.ShapeDtypeStruct((hidden, width), F32),
        ),
        in_specs=[pl.BlockSpec(memory_space=pltpu.HBM)] * (len(pieces) + 5),
        out_specs=(vmem, vmem),
        scratch_shapes=[
            *(pltpu.VMEM(r.shape, BF) for r in rest),
            pltpu.VMEM((hidden, width), F32),
            pltpu.VMEM((cot.shape[0], hidden), BF),
            pltpu.VMEM((sum(p.shape[0] for p in pieces), width), BF),
            pltpu.SemaphoreType.DMA((len(pieces) + 5,)),
        ],
        compiler_params=pltpu.CompilerParams(vmem_limit_bytes=60 * 1024 * 1024),
        cost_estimate=pl.CostEstimate(
            flops=5_000_000_000, bytes_accessed=13_000_000, transcendentals=1_000_000
        ),
    )(*pieces, *rest)


def slots(chosen, n_exp, capacity):
    n_tok = chosen.shape[0]
    onehot = (chosen[:, None] == jnp.arange(n_exp, dtype=jnp.int32)[None, :]).astype(BF)
    lower = (jnp.arange(n_tok)[:, None] > jnp.arange(n_tok)[None, :]).astype(BF)
    before = jnp.dot(lower, onehot, preferred_element_type=F32)
    rank = jnp.sum(before * onehot.astype(F32), axis=1).astype(jnp.int32)
    position = chosen * capacity + rank
    return (position[:, None] == jnp.arange(n_exp * capacity, dtype=jnp.int32)[None, :]).astype(BF)


def body(tokens, expert_id, gate_prob, w_in, w_out, head, image_cache, text_cache, pair_label):
    n_tok, width = tokens.shape
    n_exp = lax.axis_size("expert")
    n_dp = lax.axis_size("dp")
    capacity = 2 * n_tok // n_exp
    n_slots = n_exp * capacity
    n_pairs, wide = image_cache.shape
    row = lax.axis_index("dp")
    z_hi, x = row // SIDE, row % SIDE
    first = w_in[0]
    second = w_out[0]

    chosen = expert_id[:, :1]

    dispatch = slots(chosen[:, 0], n_exp, capacity)
    buffer = contract(dispatch, tokens, 0, 0).astype(BF).reshape(n_exp, capacity, width)
    own = lax.all_to_all(buffer, "expert", split_axis=0, concat_axis=0, tiled=True)
    own = own.reshape(n_slots, width)

    label_parts = jnp.stack([pair_label // 64, pair_label % 64], axis=1).astype(BF)
    slot_gate = jnp.dot(gate_prob[None, :], dispatch, preferred_element_type=F32).astype(BF)
    meta = jnp.concatenate([slot_gate, label_parts[:1], jnp.zeros((1, wide - n_slots - 2), BF)], axis=1)
    known = jnp.concatenate([text_cache, image_cache[:1], meta, jnp.zeros((6, wide), BF)], axis=0)
    known = jnp.stack(spread_along(known, "z_hi"))
    cuts = (0, n_pairs, n_pairs + 1, n_pairs + 2)
    known = [known[:, i:j].reshape(-1, wide) for i, j in zip(cuts, cuts[1:])]
    known = jnp.concatenate(known, axis=0)
    own = after(own, known)
    got = jnp.stack(spread_along(known, "z_lo"))
    cuts = tuple(SIDE * c for c in cuts)
    known = [got[:, i:j].reshape(-1, wide) for i, j in zip(cuts, cuts[1:])]
    known = jnp.concatenate(known, axis=0)

    later = after(own, known)
    below, above = shift(later, "z_hi", 1), shift(later, "z_hi", -1)
    known = spread_along(known, "x")
    near = spread_along(jnp.concatenate(known, axis=0), "y")

    own_x = gather_x(own)
    below, above = after(below, *near[1:]), after(above, *near[1:])
    half = n_slots // 2
    far = jnp.concatenate([shift(below[:half], "z_hi", 1), shift(above[half:], "z_hi", -1)], axis=0)
    both = jnp.concatenate([below, above], axis=0)
    left, right = shift(both, "x", 1), shift(both, "x", -1)
    left_far, right_far = shift(left[:n_slots], "x", 1), shift(right[n_slots:], "x", -1)
    far = after(far, left, right)
    far = [far, shift(far, "x", 1), shift(far, "x", -1), shift(far, "x", 2)]
    pieces = [own_x, both, left, right, left_far, right_far] + far
    other = [shift(p, "core", 1) for p in near]

    places = [(0, j, 0) for j in range(SIDE)]
    places += [(i, j, 1) for j in (0, -1, 1, 2) for i in (-1, 1)]
    places += [(2, j, 1) for j in (0, -1, 1, 2)]
    along_z, along_x, moved = (jnp.asarray(c, jnp.int32) for c in np.asarray(places).T)
    order = (z_hi + along_z) % SIDE * SIDE + (x * moved + along_x) % SIDE
    want = (order[:, None] * n_exp + jnp.arange(n_exp, dtype=jnp.int32)[None, :]).reshape(-1, 1)
    own_meta = jnp.pad(label_parts.astype(F32), ((0, 0), (8, 118)))

    grad_image, cot, back_hi, back_lo, gates = image_grads(
        [after(near[0], left, right)] + near[1:] + other, want, image_cache, own_meta, head, second
    )
    grad_in, grad_out = expert_grads(pieces, first, back_hi, back_lo, gates, cot)
    return (grad_image, grad_in[None], grad_out[None])


def solution(mesh):
    placed = (
        P(("dp", "expert"), None),
        P(("dp", "expert"), None),
        P(("dp", "expert")),
        P("expert", None, "dp"),
        P("expert", "dp", None),
        P(),
        P(("dp", "expert"), None),
        P(("dp", "expert"), None),
        P(("dp", "expert")),
    )
    return jax.shard_map(
        body,
        mesh=mesh,
        in_specs=placed,
        out_specs=(P(("dp", "expert"), None), P("expert", None, "dp"), P("expert", "dp", None)),
        check_vma=False,
    )
```

time: 1290 us -> 256 us (0.20)
  waiting for transfers between devices: 1160 us -> 80.9 us
  starting transfers between devices: 0.12 us -> 116 us
  blocking collectives: 79.2 us -> 0 us
  matrix products: 38.6 us -> 2.93 us
  Pallas kernels: 0 us -> 30.5 us
    all_gather x3 -> x1, waiting for transfers between devices: 1160 us -> 0.02 us  [gather_x(): return lax.all_gather(a, 'dp', axis=0, tiled=True, axis_index_groups=rows)]
    ppermute x0 -> x27, starting transfers between devices: none -> 109 us  [shift(): return lax.ppermute(a, name, ring)]
    ppermute x0 -> x27, waiting for transfers between devices: none -> 80.9 us  [shift(): return lax.ppermute(a, name, ring)]
    all_to_all x2 -> x0, blocking collectives: 79.2 us -> none  [the longest x1 52.1 us: body(): lax.all_to_all(g_buffer, 'expert', split_axis=0, concat_axis=0, tiled=True)]
    dot_general x10 -> x3, matrix products: 38.6 us -> 2.93 us  [the longest x1 1.2 us: contract(): lax.dot_general(a, b, (((da,), (db,)), ((), ())), preferred_element_type=...]
    pallas_call x0 -> x2, Pallas kernels: none -> 30.5 us  [the longest x1 16.4 us: expert_grads(): pl.pallas_call(expert_kernel, out_shape=(jax.ShapeDtypeStruct((width, hid...]
  transfers between devices with their start and end apart: 3 -> 29, of which waited for: 3 -> 10; matrix products, arithmetic and copies ran while one was open for 1% -> 3% of each run, Pallas kernels for 0% -> 6%
where the time goes in v2:
time: 256 us; the launch traced here: 255 us
  starting transfers between devices  116 us (45%)
  waiting for transfers between devices  80.9 us (32%)
  Pallas kernels  30.5 us (12%)
  between operations  14.7 us (6%)
  local copies, waits for them, and re-layouts  5.71 us (2%)
  other arithmetic  3.84 us (2%)
  matrix products  2.93 us (1%)
    ppermute x27, starting transfers between devices, shift(): return lax.ppermute(a, name, ring)  109 us
    ppermute x27, waiting for transfers between devices, shift(): return lax.ppermute(a, name, ring)  80.9 us
    pallas_call x1, Pallas kernels, expert_grads(): pl.pallas_call(expert_kernel, out_shape=(jax.ShapeDtypeStruct((width, hid...  16.4 us
    pallas_call x1, Pallas kernels, image_grads(): pl.pallas_call(loss_kernel, out_shape=(jax.ShapeDtypeStruct((n_own, wide)...  14.1 us
    all_to_all x1, starting transfers between devices, body(): lax.all_to_all(buffer, 'expert', split_axis=0, concat_axis=0, tiled=True)  7.5 us
  transfers between devices with their start and end apart: 29, of which 10 were waited for; matrix products, arithmetic and copies ran while one was open for 3% of the time, Pallas kernels for 6%

profile of v2, /device:TPU:1, one launch (start us, length us, event | category | flops | bytes accessed | tf_op | source)
XLA Modules:
  0.0 254.8 jit_solution(395050766485868317)
XLA Ops:
  7.2 0.0 copy-start
  7.2 0.7 convert_bitcast_fusion
  7.9 0.1 copy.20
  8.0 0.9 fusion.1
  8.9 0.7 fusion.15
  9.6 0.9 fusion.2
  10.4 0.7 slice.36
  11.2 0.1 pad.29.clone
  11.2 0.8 maximum_maximum_fusion
  12.0 13.3 %collective-permute-start.2 = (bf16[16,512]{1,0:T(8,128)(2,1)S(1)}, bf16[16,512]{1,0:T(8,128)(2,1)S(1)}, u32[]{:S(2)}, u32[]{:S(2)}) collective-permute-start(bf16[16,512]{1,0:T(8,128)(2,1)S(1)} %maximum_maximum_fusion), channel_id=1, source_target_pairs={{0,384},{32,416},{64,448},{96,480},{128,0},{160,32},{192,64},{224,... | collective-permute-start | bytes 49160 | tf_op jit(solution)/shard_map/ppermute | solution.py:45
  25.3 4.9 %collective-permute-start.1 = (bf16[16,512]{1,0:T(8,128)(2,1)S(1)}, bf16[16,512]{1,0:T(8,128)(2,1)S(1)}, u32[]{:S(2)}, u32[]{:S(2)}) collective-permute-start(bf16[16,512]{1,0:T(8,128)(2,1)S(1)} %maximum_maximum_fusion), channel_id=1, source_target_pairs={{0,256},{32,288},{64,320},{96,352},{128,384},{160,416},{192,448},{... | collective-permute-start | bytes 49160 | tf_op jit(solution)/shard_map/ppermute | solution.py:45
  30.2 7.3 %collective-permute-start = (bf16[16,512]{1,0:T(8,128)(2,1)S(1)}, bf16[16,512]{1,0:T(8,128)(2,1)S(1)}, u32[]{:S(2)}, u32[]{:S(2)}) collective-permute-start(bf16[16,512]{1,0:T(8,128)(2,1)S(1)} %maximum_maximum_fusion), channel_id=1, source_target_pairs={{0,128},{32,160},{64,192},{96,224},{128,256},{160,288},{192,320},{... | collective-permute-start | bytes 49160 | tf_op jit(solution)/shard_map/ppermute | solution.py:45
  37.5 1.2 fusion
  38.7 7.5 %all-to-all-start = ((bf16[32,8,1024]{2,1,0:T(8,128)(2,1)}), bf16[32,8,1024]{2,1,0:T(8,128)(2,1)S(1)}, u32[]{:S(2)}, u32[]{:S(2)}) async-start(bf16[32,8,1024]{2,1,0:T(8,128)(2,1)} %fusion), calls=%async_computation | async-start | bytes 1048576 | tf_op jit(solution)/shard_map/all_to_all | solution.py:281
  46.2 0.0 all-gather.2.cloned.1.call-start
  46.3 0.8 fusion.18
  47.2 5.1 %collective-permute-start.5 = (bf16[40,512]{1,0:T(8,128)(2,1)S(1)}, bf16[40,512]{1,0:T(8,128)(2,1)S(1)}, u32[]{:S(2)}, u32[]{:S(2)}) collective-permute-start(bf16[40,512]{1,0:T(8,128)(2,1)S(1)} %get-tuple-element.34), channel_id=1, source_target_pairs={{0,6},{1,7},{2,0},{3,1},{4,2},{5,3},{6,4},{7,5},{8,14},{9,15},{10,... | collective-permute-start | bytes 122888 | tf_op jit(solution)/shard_map/ppermute | solution.py:45
  52.3 1.9 collective-permute-start.4
  54.2 2.5 collective-permute-start.3
  56.7 7.4 %collective-permute-done.4 = bf16[40,512]{1,0:T(8,128)(2,1)S(1)} collective-permute-done((bf16[40,512]{1,0:T(8,128)(2,1)S(1)}, bf16[40,512]{1,0:T(8,128)(2,1)S(1)}, u32[]{:S(2)}, u32[]{:S(2)}) %collective-permute-start.4) | collective-permute-done | bytes 40992 | tf_op jit(solution)/shard_map/ppermute | solution.py:45
  64.2 3.1 %collective-permute-start.6 = (bf16[160,512]{1,0:T(8,128)(2,1)S(1)}, bf16[160,512]{1,0:T(8,128)(2,1)S(1)}, u32[]{:S(2)}, u32[]{:S(2)}) collective-permute-start(bf16[160,512]{1,0:T(8,128)(2,1)S(1)} %pad_maximum_fusion.2), channel_id=1, source_target_pairs={{0,32},{32,64},{64,96},{96,0},{128,160},{160,192},{192,224},{224,1... | collective-permute-start | bytes 491528 | tf_op jit(solution)/shard_map/ppermute | solution.py:45
  67.4 4.4 %collective-permute-start.7 = (bf16[160,512]{1,0:T(8,128)(2,1)S(1)}, bf16[160,512]{1,0:T(8,128)(2,1)S(1)}, u32[]{:S(2)}, u32[]{:S(2)}) collective-permute-start(bf16[160,512]{1,0:T(8,128)(2,1)S(1)} %pad_maximum_fusion.2), channel_id=1, source_target_pairs={{0,64},{32,96},{64,0},{96,32},{128,192},{160,224},{192,128},{224,1... | collective-permute-start | bytes 491528 | tf_op jit(solution)/shard_map/ppermute | solution.py:45
  71.7 3.1 %collective-permute-start.8 = (bf16[160,512]{1,0:T(8,128)(2,1)S(1)}, bf16[160,512]{1,0:T(8,128)(2,1)S(1)}, u32[]{:S(2)}, u32[]{:S(2)}) collective-permute-start(bf16[160,512]{1,0:T(8,128)(2,1)S(1)} %pad_maximum_fusion.2), channel_id=1, source_target_pairs={{0,96},{32,0},{64,32},{96,64},{128,224},{160,128},{192,160},{224,1... | collective-permute-start | bytes 491528 | tf_op jit(solution)/shard_map/ppermute | solution.py:45
  74.9 2.1 collective-permute-done.7
  77.0 0.0 copy-start.5
  77.0 0.0 copy-start.6
  77.0 1.0 collective-permute-done.8
  78.1 2.8 %collective-permute-start.10 = (bf16[640,512]{1,0:T(8,128)(2,1)S(1)}, bf16[640,512]{1,0:T(8,128)(2,1)S(1)}, u32[]{:S(2)}, u32[]{:S(2)}) collective-permute-start(bf16[640,512]{1,0:T(8,128)(2,1)S(1)} %constant_dynamic-update-slice_fusion.refs_0_), channel_id=1, source_target_pairs={{0,8},{1,9},{2,10},{3,11},{4,12},{5,13},{6,14},{7,15},{8,16},{9,17... | collective-permute-start | bytes 1966088 | tf_op jit(solution)/shard_map/ppermute | solution.py:45
  80.9 4.4 %collective-permute-start.11 = (bf16[640,512]{1,0:T(8,128)(2,1)S(1)}, bf16[640,512]{1,0:T(8,128)(2,1)}, u32[]{:S(2)}, u32[]{:S(2)}) collective-permute-start(bf16[640,512]{1,0:T(8,128)(2,1)S(1)} %constant_dynamic-update-slice_fusion.refs_0_), channel_id=1, source_target_pairs={{0,16},{1,17},{2,18},{3,19},{4,20},{5,21},{6,22},{7,23},{8,24},{9,... | collective-permute-start | bytes 1966088 | tf_op jit(solution)/shard_map/ppermute | solution.py:45
  85.3 3.0 %collective-permute-start.12 = (bf16[640,512]{1,0:T(8,128)(2,1)S(1)}, bf16[640,512]{1,0:T(8,128)(2,1)}, u32[]{:S(2)}, u32[]{:S(2)}) collective-permute-start(bf16[640,512]{1,0:T(8,128)(2,1)S(1)} %constant_dynamic-update-slice_fusion.refs_0_), channel_id=1, source_target_pairs={{0,24},{1,25},{2,26},{3,27},{4,28},{5,29},{6,30},{7,31},{8,0},{9,1... | collective-permute-start | bytes 1966088 | tf_op jit(solution)/shard_map/ppermute | solution.py:45
  88.3 4.0 %collective-permute-start.9 = (bf16[256,1024]{1,0:T(8,128)(2,1)S(1)}, bf16[256,1024]{1,0:T(8,128)(2,1)S(1)}, u32[]{:S(2)}, u32[]{:S(2)}) collective-permute-start(bf16[256,1024]{1,0:T(8,128)(2,1)S(1)} %bitcast.41), channel_id=1, source_target_pairs={{0,128},{32,160},{64,192},{96,224},{128,256},{160,288},{192,320},{... | collective-permute-start | bytes 1572872 | tf_op jit(solution)/shard_map/ppermute | solution.py:45
  92.3 5.2 %collective-permute-start.13 = (bf16[256,1024]{1,0:T(8,128)(2,1)S(1)}, bf16[256,1024]{1,0:T(8,128)(2,1)S(1)}, u32[]{:S(2)}, u32[]{:S(2)}) collective-permute-start(bf16[256,1024]{1,0:T(8,128)(2,1)S(1)} %bitcast.42), channel_id=1, source_target_pairs={{0,384},{32,416},{64,448},{96,480},{128,0},{160,32},{192,64},{224,... | collective-permute-start | bytes 1572872 | tf_op jit(solution)/shard_map/ppermute | solution.py:45
  97.5 0.0 all-gather.2.cloned.1.call-update
  97.6 12.0 %collective-permute-done.11.refs_2_ = bf16[640,512]{1,0:T(8,128)(2,1)} collective-permute-done((bf16[640,512]{1,0:T(8,128)(2,1)S(1)}, bf16[640,512]{1,0:T(8,128)(2,1)}, u32[]{:S(2)}, u32[]{:S(2)}) %collective-permute-start.11) | collective-permute-done | bytes 655392 | tf_op jit(solution)/shard_map/ppermute | solution.py:45
  109.6 3.7 %collective-permute-done.12.refs_3_ = bf16[640,512]{1,0:T(8,128)(2,1)} collective-permute-done((bf16[640,512]{1,0:T(8,128)(2,1)S(1)}, bf16[640,512]{1,0:T(8,128)(2,1)}, u32[]{:S(2)}, u32[]{:S(2)}) %collective-permute-start.12) | collective-permute-done | bytes 655392 | tf_op jit(solution)/shard_map/ppermute | solution.py:45
  113.4 5.9 %collective-permute-done.9 = bf16[256,1024]{1,0:T(8,128)(2,1)S(1)} collective-permute-done((bf16[256,1024]{1,0:T(8,128)(2,1)S(1)}, bf16[256,1024]{1,0:T(8,128)(2,1)S(1)}, u32[]{:S(2)}, u32[]{:S(2)}) %collective-permute-start.9) | collective-permute-done | bytes 524320 | tf_op jit(solution)/shard_map/ppermute | solution.py:45
  119.3 26.6 %collective-permute-done.13 = bf16[256,1024]{1,0:T(8,128)(2,1)S(1)} collective-permute-done((bf16[256,1024]{1,0:T(8,128)(2,1)S(1)}, bf16[256,1024]{1,0:T(8,128)(2,1)S(1)}, u32[]{:S(2)}, u32[]{:S(2)}) %collective-permute-start.13) | collective-permute-done | bytes 524320 | tf_op jit(solution)/shard_map/ppermute | solution.py:45
  145.9 0.8 constant_dynamic-update-slice_fusion.7
  146.7 0.8 constant_dynamic-update-slice_fusion.6.refs_1_
  147.6 1.9 collective-permute-start.14
  149.5 4.6 %collective-permute-start.15 = (bf16[512,1024]{1,0:T(8,128)(2,1)}, bf16[512,1024]{1,0:T(8,128)(2,1)}, u32[]{:S(2)}, u32[]{:S(2)}) collective-permute-start(bf16[512,1024]{1,0:T(8,128)(2,1)} %constant_dynamic-update-slice_fusion.6.refs_1_), channel_id=1, source_target_pairs={{0,96},{32,0},{64,32},{96,64},{128,224},{160,128},{192,160},{224,1... | collective-permute-start | bytes 3145736 | tf_op jit(solution)/shard_map/ppermute | solution.py:45
  154.1 2.9 %collective-permute-start.23 = (bf16[128,1024]{1,0:T(8,128)(2,1)S(1)}, bf16[128,1024]{1,0:T(8,128)(2,1)S(1)}, u32[]{:S(2)}, u32[]{:S(2)}) collective-permute-start(bf16[128,1024]{1,0:T(8,128)(2,1)S(1)} %slice.47), channel_id=1, source_target_pairs={{0,384},{32,416},{64,448},{96,480},{128,0},{160,32},{192,64},{224,... | collective-permute-start | bytes 786440 | tf_op jit(solution)/shard_map/ppermute | solution.py:45
  157.1 6.3 %collective-permute-start.22 = (bf16[128,1024]{1,0:T(8,128)(2,1)S(1)}, bf16[128,1024]{1,0:T(8,128)(2,1)S(1)}, u32[]{:S(2)}, u32[]{:S(2)}) collective-permute-start(bf16[128,1024]{1,0:T(8,128)(2,1)S(1)} %slice.46), channel_id=1, source_target_pairs={{0,128},{32,160},{64,192},{96,224},{128,256},{160,288},{192,320},{... | collective-permute-start | bytes 786440 | tf_op jit(solution)/shard_map/ppermute | solution.py:45
  163.3 0.1 copy.21
  163.4 3.7 %collective-permute-start.16 = (bf16[640,512]{1,0:T(8,128)(2,1)S(1)}, bf16[640,512]{1,0:T(8,128)(2,1)}, u32[]{:S(2)}, u32[]{:S(2)}) collective-permute-start(bf16[640,512]{1,0:T(8,128)(2,1)S(1)} %constant_dynamic-update-slice_fusion.refs_0_), channel_id=1, source_target_pairs={{0,1},{1,0},{2,3},{3,2},{4,5},{5,4},{6,7},{7,6},{8,9},{9,8},{10,11... | collective-permute-start | bytes 1966088 | tf_op jit(solution)/shard_map/ppermute | solution.py:45
  167.1 10.7 %collective-permute-done.23 = bf16[128,1024]{1,0:T(8,128)(2,1)S(1)} collective-permute-done((bf16[128,1024]{1,0:T(8,128)(2,1)S(1)}, bf16[128,1024]{1,0:T(8,128)(2,1)S(1)}, u32[]{:S(2)}, u32[]{:S(2)}) %collective-permute-start.23) | collective-permute-done | bytes 262176 | tf_op jit(solution)/shard_map/ppermute | solution.py:45
  177.8 2.4 collective-permute-start.17
  180.2 1.9 collective-permute-start.18
  182.2 2.4 collective-permute-start.19
  184.6 0.1 iota_add_fusion
  184.7 1.0 add.76.refs_8_
  185.7 0.7 pad_convert_fusion.refs_10_
  186.4 5.4 %collective-permute-start.24 = (bf16[256,1024]{1,0:T(8,128)(2,1)S(1)}, bf16[256,1024]{1,0:T(8,128)(2,1)S(1)}, u32[]{:S(2)}, u32[]{:S(2)}) collective-permute-start(bf16[256,1024]{1,0:T(8,128)(2,1)S(1)} %pad_maximum_fusion.refs_6_), channel_id=1, source_target_pairs={{0,32},{32,64},{64,96},{96,0},{128,160},{160,192},{192,224},{224,1... | collective-permute-start | bytes 1572872 | tf_op jit(solution)/shard_map/ppermute | solution.py:45
  191.9 1.1 slice.51
  193.0 1.9 collective-permute-start.25
  194.9 3.7 %collective-permute-start.26 = (bf16[256,1024]{1,0:T(8,128)(2,1)S(1)}, bf16[256,1024]{1,0:T(8,128)(2,1)}, u32[]{:S(2)}, u32[]{:S(2)}) collective-permute-start(bf16[256,1024]{1,0:T(8,128)(2,1)S(1)} %pad_maximum_fusion.refs_6_), channel_id=1, source_target_pairs={{0,64},{32,96},{64,0},{96,32},{128,192},{160,224},{192,128},{224,1... | collective-permute-start | bytes 1572872 | tf_op jit(solution)/shard_map/ppermute | solution.py:45
  198.6 1.9 collective-permute-start.20
  200.6 4.8 %collective-permute-start.21 = (bf16[256,1024]{1,0:T(8,128)(2,1)S(1)}, bf16[256,1024]{1,0:T(8,128)(2,1)}, u32[]{:S(2)}, u32[]{:S(2)}) collective-permute-start(bf16[256,1024]{1,0:T(8,128)(2,1)S(1)} %slice.51), channel_id=1, source_target_pairs={{0,96},{32,0},{64,32},{96,64},{128,224},{160,128},{192,160},{224,1... | collective-permute-start | bytes 1572872 | tf_op jit(solution)/shard_map/ppermute | solution.py:45
  205.3 14.1 %shard_map.139 = (f32[8,512]{1,0:T(8,128)}, bf16[512,1024]{1,0:T(8,128)(2,1)}, bf16[512,256]{1,0:T(8,128)(2,1)}, bf16[512,256]{1,0:T(8,128)(2,1)}, bf16[512,128]{1,0:T(8,128)(2,1)}) custom-call(bf16[640,512]{1,0:T(8,128)(2,1)} %copy-done.4, bf16[640,512]{1,0:T(8,128)(2,1)} %copy-done.8, bf16[640,512]{1,0:T(8,128)(2,1)} %collective-permute-done.11.refs_2_, ...), custom_call_target="tpu_custom_call" | custom-call | flops 10000000000 | bytes 9000000 | tf_op jit(solution)/shard_map/pallas_call | solution.py:148
  219.4 6.5 %collective-permute-done.20.refs_4_ = bf16[256,1024]{1,0:T(8,128)(2,1)} collective-permute-done((bf16[256,1024]{1,0:T(8,128)(2,1)S(1)}, bf16[256,1024]{1,0:T(8,128)(2,1)}, u32[]{:S(2)}, u32[]{:S(2)}) %collective-permute-start.20) | collective-permute-done | bytes 524320 | tf_op jit(solution)/shard_map/ppermute | solution.py:45
  226.0 4.7 %collective-permute-done.21.refs_5_ = bf16[256,1024]{1,0:T(8,128)(2,1)} collective-permute-done((bf16[256,1024]{1,0:T(8,128)(2,1)S(1)}, bf16[256,1024]{1,0:T(8,128)(2,1)}, u32[]{:S(2)}, u32[]{:S(2)}) %collective-permute-start.21) | collective-permute-done | bytes 524320 | tf_op jit(solution)/shard_map/ppermute | solution.py:45
  230.7 0.0 all-gather.2.cloned.1.call-done.refs_0_
  230.8 0.7 copy-done.9
  231.5 16.4 %shard_map.140 = (f32[1024,256]{1,0:T(8,128)}, f32[256,1024]{1,0:T(8,128)}) custom-call(bf16[1024,1024]{1,0:T(8,128)(2,1)} %all-gather.2.cloned.1.call-done.refs_0_, bf16[512,1024]{1,0:T(8,128)(2,1)} %constant_dynamic-update-slice_fusion.6.refs_1_, bf16[512,1024]{1,0:T(8,128)(2,1)} %copy-done.3, bf16[512,1024]{1,0:T(8,128)(2,1)} %collective-permute-done.15.refs_3_, ...), custom_call_target="tpu_custom_call" | custom-call | flops 5000000000 | bytes 13000000 | tf_op jit(solution)/shard_map/pallas_call | solution.py:233
  (61 shorter events, 0.4 us)
Async XLA Ops:
  7.2 30.3 %copy-start = (bf16[128,1024]{1,0:T(8,128)(2,1)S(1)}, bf16[128,1024]{1,0:T(8,128)(2,1)}, u32[]{:S(2)}) copy-start(bf16[128,1024]{1,0:T(8,128)(2,1)} %param.12) | copy-start | bytes 786436
  12.0 35.0 %collective-permute-start.2 = (bf16[16,512]{1,0:T(8,128)(2,1)S(1)}, bf16[16,512]{1,0:T(8,128)(2,1)S(1)}, u32[]{:S(2)}, u32[]{:S(2)}) collective-permute-start(bf16[16,512]{1,0:T(8,128)(2,1)S(1)} %maximum_maximum_fusion), channel_id=1, source_target_pairs={{0,384},{32,416},{64,448},{96,480},{128,0},{160,32},{192,64},{224,... | collective-permute-start | bytes 49160 | tf_op jit(solution)/shard_map/ppermute | solution.py:45
  25.3 21.8 %collective-permute-start.1 = (bf16[16,512]{1,0:T(8,128)(2,1)S(1)}, bf16[16,512]{1,0:T(8,128)(2,1)S(1)}, u32[]{:S(2)}, u32[]{:S(2)}) collective-permute-start(bf16[16,512]{1,0:T(8,128)(2,1)S(1)} %maximum_maximum_fusion), channel_id=1, source_target_pairs={{0,256},{32,288},{64,320},{96,352},{128,384},{160,416},{192,448},{... | collective-permute-start | bytes 49160 | tf_op jit(solution)/shard_map/ppermute | solution.py:45
  30.2 16.8 %collective-permute-start = (bf16[16,512]{1,0:T(8,128)(2,1)S(1)}, bf16[16,512]{1,0:T(8,128)(2,1)S(1)}, u32[]{:S(2)}, u32[]{:S(2)}) collective-permute-start(bf16[16,512]{1,0:T(8,128)(2,1)S(1)} %maximum_maximum_fusion), channel_id=1, source_target_pairs={{0,128},{32,160},{64,192},{96,224},{128,256},{160,288},{192,320},{... | collective-permute-start | bytes 49160 | tf_op jit(solution)/shard_map/ppermute | solution.py:45
  38.7 49.6 %all-to-all-start = ((bf16[32,8,1024]{2,1,0:T(8,128)(2,1)}), bf16[32,8,1024]{2,1,0:T(8,128)(2,1)S(1)}, u32[]{:S(2)}, u32[]{:S(2)}) async-start(bf16[32,8,1024]{2,1,0:T(8,128)(2,1)} %fusion), calls=%async_computation | async-start | bytes 1048576 | tf_op jit(solution)/shard_map/all_to_all | solution.py:281
  46.2 184.5 %all-gather.2.cloned.1.call-start = ((), (), s32[]{:S(2)}) async-start(), calls=%async_computation.1 | async-start | bytes 2621440 | tf_op jit(solution)/shard_map/all_gather | solution.py:55
  47.2 9.5 %collective-permute-start.5 = (bf16[40,512]{1,0:T(8,128)(2,1)S(1)}, bf16[40,512]{1,0:T(8,128)(2,1)S(1)}, u32[]{:S(2)}, u32[]{:S(2)}) collective-permute-start(bf16[40,512]{1,0:T(8,128)(2,1)S(1)} %get-tuple-element.34), channel_id=1, source_target_pairs={{0,6},{1,7},{2,0},{3,1},{4,2},{5,3},{6,4},{7,5},{8,14},{9,15},{10,... | collective-permute-start | bytes 122888 | tf_op jit(solution)/shard_map/ppermute | solution.py:45
  52.3 11.8 %collective-permute-start.4 = (bf16[40,512]{1,0:T(8,128)(2,1)S(1)}, bf16[40,512]{1,0:T(8,128)(2,1)S(1)}, u32[]{:S(2)}, u32[]{:S(2)}) collective-permute-start(bf16[40,512]{1,0:T(8,128)(2,1)S(1)} %get-tuple-element.34), channel_id=1, source_target_pairs={{0,4},{1,5},{2,6},{3,7},{4,0},{5,1},{6,2},{7,3},{8,12},{9,13},{10,... | collective-permute-start | bytes 122888 | tf_op jit(solution)/shard_map/ppermute | solution.py:45
  54.2 9.9 %collective-permute-start.3 = (bf16[40,512]{1,0:T(8,128)(2,1)S(1)}, bf16[40,512]{1,0:T(8,128)(2,1)S(1)}, u32[]{:S(2)}, u32[]{:S(2)}) collective-permute-start(bf16[40,512]{1,0:T(8,128)(2,1)S(1)} %get-tuple-element.34), channel_id=1, source_target_pairs={{0,2},{1,3},{2,4},{3,5},{4,6},{5,7},{6,0},{7,1},{8,10},{9,11},{10,... | collective-permute-start | bytes 122888 | tf_op jit(solution)/shard_map/ppermute | solution.py:45
  64.2 10.6 %collective-permute-start.6 = (bf16[160,512]{1,0:T(8,128)(2,1)S(1)}, bf16[160,512]{1,0:T(8,128)(2,1)S(1)}, u32[]{:S(2)}, u32[]{:S(2)}) collective-permute-start(bf16[160,512]{1,0:T(8,128)(2,1)S(1)} %pad_maximum_fusion.2), channel_id=1, source_target_pairs={{0,32},{32,64},{64,96},{96,0},{128,160},{160,192},{192,224},{224,1... | collective-permute-start | bytes 491528 | tf_op jit(solution)/shard_map/ppermute | solution.py:45
  67.4 9.6 %collective-permute-start.7 = (bf16[160,512]{1,0:T(8,128)(2,1)S(1)}, bf16[160,512]{1,0:T(8,128)(2,1)S(1)}, u32[]{:S(2)}, u32[]{:S(2)}) collective-permute-start(bf16[160,512]{1,0:T(8,128)(2,1)S(1)} %pad_maximum_fusion.2), channel_id=1, source_target_pairs={{0,64},{32,96},{64,0},{96,32},{128,192},{160,224},{192,128},{224,1... | collective-permute-start | bytes 491528 | tf_op jit(solution)/shard_map/ppermute | solution.py:45
  71.7 6.3 %collective-permute-start.8 = (bf16[160,512]{1,0:T(8,128)(2,1)S(1)}, bf16[160,512]{1,0:T(8,128)(2,1)S(1)}, u32[]{:S(2)}, u32[]{:S(2)}) collective-permute-start(bf16[160,512]{1,0:T(8,128)(2,1)S(1)} %pad_maximum_fusion.2), channel_id=1, source_target_pairs={{0,96},{32,0},{64,32},{96,64},{128,224},{160,128},{192,160},{224,1... | collective-permute-start | bytes 491528 | tf_op jit(solution)/shard_map/ppermute | solution.py:45
  77.0 107.6 %copy-start.5 = (s32[16]{0:T(128)S(1)}, s32[16]{0:T(128)}, u32[]{:S(2)}) copy-start(s32[16]{0:T(128)} %constant.89.clone) | copy-start | bytes 196
  77.0 107.6 %copy-start.6 = (s32[16]{0:T(128)S(1)}, s32[16]{0:T(128)}, u32[]{:S(2)}) copy-start(s32[16]{0:T(128)} %constant.90.clone) | copy-start | bytes 196
  77.0 107.6 %copy-start.7 = (s32[16]{0:T(128)S(1)}, s32[16]{0:T(128)}, u32[]{:S(2)}) copy-start(s32[16]{0:T(128)} %constant.91.clone) | copy-start | bytes 196
  78.1 127.2 %copy-start.4 = (bf16[640,512]{1,0:T(8,128)(2,1)}, bf16[640,512]{1,0:T(8,128)(2,1)S(1)}, u32[]{:S(2)}) copy-start(bf16[640,512]{1,0:T(8,128)(2,1)S(1)} %constant_dynamic-update-slice_fusion.refs_0_) | copy-start | bytes 1966084
  78.1 19.5 %collective-permute-start.10 = (bf16[640,512]{1,0:T(8,128)(2,1)S(1)}, bf16[640,512]{1,0:T(8,128)(2,1)S(1)}, u32[]{:S(2)}, u32[]{:S(2)}) collective-permute-start(bf16[640,512]{1,0:T(8,128)(2,1)S(1)} %constant_dynamic-update-slice_fusion.refs_0_), channel_id=1, source_target_pairs={{0,8},{1,9},{2,10},{3,11},{4,12},{5,13},{6,14},{7,15},{8,16},{9,17... | collective-permute-start | bytes 1966088 | tf_op jit(solution)/shard_map/ppermute | solution.py:45
  80.9 28.7 %collective-permute-start.11 = (bf16[640,512]{1,0:T(8,128)(2,1)S(1)}, bf16[640,512]{1,0:T(8,128)(2,1)}, u32[]{:S(2)}, u32[]{:S(2)}) collective-permute-start(bf16[640,512]{1,0:T(8,128)(2,1)S(1)} %constant_dynamic-update-slice_fusion.refs_0_), channel_id=1, source_target_pairs={{0,16},{1,17},{2,18},{3,19},{4,20},{5,21},{6,22},{7,23},{8,24},{9,... | collective-permute-start | bytes 1966088 | tf_op jit(solution)/shard_map/ppermute | solution.py:45
  85.3 28.1 %collective-permute-start.12 = (bf16[640,512]{1,0:T(8,128)(2,1)S(1)}, bf16[640,512]{1,0:T(8,128)(2,1)}, u32[]{:S(2)}, u32[]{:S(2)}) collective-permute-start(bf16[640,512]{1,0:T(8,128)(2,1)S(1)} %constant_dynamic-update-slice_fusion.refs_0_), channel_id=1, source_target_pairs={{0,24},{1,25},{2,26},{3,27},{4,28},{5,29},{6,30},{7,31},{8,0},{9,1... | collective-permute-start | bytes 1966088 | tf_op jit(solution)/shard_map/ppermute | solution.py:45
  88.3 9.2 %copy-start.1 = (bf16[32,8,1024]{2,1,0:T(8,128)(2,1)}, bf16[32,8,1024]{2,1,0:T(8,128)(2,1)S(1)}, u32[]{:S(2)}) copy-start(bf16[32,8,1024]{2,1,0:T(8,128)(2,1)S(1)} %all-to-all-done) | copy-start | bytes 1572868
  88.3 31.0 %collective-permute-start.9 = (bf16[256,1024]{1,0:T(8,128)(2,1)S(1)}, bf16[256,1024]{1,0:T(8,128)(2,1)S(1)}, u32[]{:S(2)}, u32[]{:S(2)}) collective-permute-start(bf16[256,1024]{1,0:T(8,128)(2,1)S(1)} %bitcast.41), channel_id=1, source_target_pairs={{0,128},{32,160},{64,192},{96,224},{128,256},{160,288},{192,320},{... | collective-permute-start | bytes 1572872 | tf_op jit(solution)/shard_map/ppermute | solution.py:45
  92.3 53.5 %collective-permute-start.13 = (bf16[256,1024]{1,0:T(8,128)(2,1)S(1)}, bf16[256,1024]{1,0:T(8,128)(2,1)S(1)}, u32[]{:S(2)}, u32[]{:S(2)}) collective-permute-start(bf16[256,1024]{1,0:T(8,128)(2,1)S(1)} %bitcast.42), channel_id=1, source_target_pairs={{0,384},{32,416},{64,448},{96,480},{128,0},{160,32},{192,64},{224,... | collective-permute-start | bytes 1572872 | tf_op jit(solution)/shard_map/ppermute | solution.py:45
  97.6 49.2 %copy-start.8 = (bf16[640,512]{1,0:T(8,128)(2,1)}, bf16[640,512]{1,0:T(8,128)(2,1)S(1)}, u32[]{:S(2)}) copy-start(bf16[640,512]{1,0:T(8,128)(2,1)S(1)} %collective-permute-done.10.refs_1_) | copy-start | bytes 1966084
  147.6 34.6 %collective-permute-start.14 = (bf16[512,1024]{1,0:T(8,128)(2,1)}, bf16[512,1024]{1,0:T(8,128)(2,1)S(1)}, u32[]{:S(2)}, u32[]{:S(2)}) collective-permute-start(bf16[512,1024]{1,0:T(8,128)(2,1)} %constant_dynamic-update-slice_fusion.6.refs_1_), channel_id=1, source_target_pairs={{0,32},{32,64},{64,96},{96,0},{128,160},{160,192},{192,224},{224,1... | collective-permute-start | bytes 3145736 | tf_op jit(solution)/shard_map/ppermute | solution.py:45
  149.5 36.9 %collective-permute-start.15 = (bf16[512,1024]{1,0:T(8,128)(2,1)}, bf16[512,1024]{1,0:T(8,128)(2,1)}, u32[]{:S(2)}, u32[]{:S(2)}) collective-permute-start(bf16[512,1024]{1,0:T(8,128)(2,1)} %constant_dynamic-update-slice_fusion.6.refs_1_), channel_id=1, source_target_pairs={{0,96},{32,0},{64,32},{96,64},{128,224},{160,128},{192,160},{224,1... | collective-permute-start | bytes 3145736 | tf_op jit(solution)/shard_map/ppermute | solution.py:45
  154.1 23.7 %collective-permute-start.23 = (bf16[128,1024]{1,0:T(8,128)(2,1)S(1)}, bf16[128,1024]{1,0:T(8,128)(2,1)S(1)}, u32[]{:S(2)}, u32[]{:S(2)}) collective-permute-start(bf16[128,1024]{1,0:T(8,128)(2,1)S(1)} %slice.47), channel_id=1, source_target_pairs={{0,384},{32,416},{64,448},{96,480},{128,0},{160,32},{192,64},{224,... | collective-permute-start | bytes 786440 | tf_op jit(solution)/shard_map/ppermute | solution.py:45
  157.1 23.2 %collective-permute-start.22 = (bf16[128,1024]{1,0:T(8,128)(2,1)S(1)}, bf16[128,1024]{1,0:T(8,128)(2,1)S(1)}, u32[]{:S(2)}, u32[]{:S(2)}) collective-permute-start(bf16[128,1024]{1,0:T(8,128)(2,1)S(1)} %slice.46), channel_id=1, source_target_pairs={{0,128},{32,160},{64,192},{96,224},{128,256},{160,288},{192,320},{... | collective-permute-start | bytes 786440 | tf_op jit(solution)/shard_map/ppermute | solution.py:45
  163.4 29.5 %collective-permute-start.16 = (bf16[640,512]{1,0:T(8,128)(2,1)S(1)}, bf16[640,512]{1,0:T(8,128)(2,1)}, u32[]{:S(2)}, u32[]{:S(2)}) collective-permute-start(bf16[640,512]{1,0:T(8,128)(2,1)S(1)} %constant_dynamic-update-slice_fusion.refs_0_), channel_id=1, source_target_pairs={{0,1},{1,0},{2,3},{3,2},{4,5},{5,4},{6,7},{7,6},{8,9},{9,8},{10,11... | collective-permute-start | bytes 1966088 | tf_op jit(solution)/shard_map/ppermute | solution.py:45
  177.8 17.1 %collective-permute-start.17 = (bf16[640,512]{1,0:T(8,128)(2,1)}, bf16[640,512]{1,0:T(8,128)(2,1)}, u32[]{:S(2)}, u32[]{:S(2)}) collective-permute-start(bf16[640,512]{1,0:T(8,128)(2,1)} %copy-done.8), channel_id=1, source_target_pairs={{0,1},{1,0},{2,3},{3,2},{4,5},{5,4},{6,7},{7,6},{8,9},{9,8},{10,11... | collective-permute-start | bytes 1966088 | tf_op jit(solution)/shard_map/ppermute | solution.py:45
  180.2 18.4 %collective-permute-start.18 = (bf16[640,512]{1,0:T(8,128)(2,1)}, bf16[640,512]{1,0:T(8,128)(2,1)}, u32[]{:S(2)}, u32[]{:S(2)}) collective-permute-start(bf16[640,512]{1,0:T(8,128)(2,1)} %collective-permute-done.11.refs_2_), channel_id=1, source_target_pairs={{0,1},{1,0},{2,3},{3,2},{4,5},{5,4},{6,7},{7,6},{8,9},{9,8},{10,11... | collective-permute-start | bytes 1966088 | tf_op jit(solution)/shard_map/ppermute | solution.py:45
  182.2 37.2 %copy-start.3 = (bf16[512,1024]{1,0:T(8,128)(2,1)}, bf16[512,1024]{1,0:T(8,128)(2,1)S(1)}, u32[]{:S(2)}) copy-start(bf16[512,1024]{1,0:T(8,128)(2,1)S(1)} %collective-permute-done.14.refs_2_) | copy-start | bytes 3145732
  182.2 18.4 %collective-permute-start.19 = (bf16[640,512]{1,0:T(8,128)(2,1)}, bf16[640,512]{1,0:T(8,128)(2,1)}, u32[]{:S(2)}, u32[]{:S(2)}) collective-permute-start(bf16[640,512]{1,0:T(8,128)(2,1)} %collective-permute-done.12.refs_3_), channel_id=1, source_target_pairs={{0,1},{1,0},{2,3},{3,2},{4,5},{5,4},{6,7},{7,6},{8,9},{9,8},{10,11... | collective-permute-start | bytes 1966088 | tf_op jit(solution)/shard_map/ppermute | solution.py:45
  186.4 33.0 %copy-start.2 = (bf16[256,1024]{1,0:T(8,128)(2,1)}, bf16[256,1024]{1,0:T(8,128)(2,1)S(1)}, u32[]{:S(2)}) copy-start(bf16[256,1024]{1,0:T(8,128)(2,1)S(1)} %pad_maximum_fusion.refs_6_) | copy-start | bytes 1572868
  186.4 44.3 %collective-permute-start.24 = (bf16[256,1024]{1,0:T(8,128)(2,1)S(1)}, bf16[256,1024]{1,0:T(8,128)(2,1)S(1)}, u32[]{:S(2)}, u32[]{:S(2)}) collective-permute-start(bf16[256,1024]{1,0:T(8,128)(2,1)S(1)} %pad_maximum_fusion.refs_6_), channel_id=1, source_target_pairs={{0,32},{32,64},{64,96},{96,0},{128,160},{160,192},{192,224},{224,1... | collective-permute-start | bytes 1572872 | tf_op jit(solution)/shard_map/ppermute | solution.py:45
  193.0 37.8 %collective-permute-start.25 = (bf16[256,1024]{1,0:T(8,128)(2,1)S(1)}, bf16[256,1024]{1,0:T(8,128)(2,1)}, u32[]{:S(2)}, u32[]{:S(2)}) collective-permute-start(bf16[256,1024]{1,0:T(8,128)(2,1)S(1)} %pad_maximum_fusion.refs_6_), channel_id=1, source_target_pairs={{0,96},{32,0},{64,32},{96,64},{128,224},{160,128},{192,160},{224,1... | collective-permute-start | bytes 1572872 | tf_op jit(solution)/shard_map/ppermute | solution.py:45
  194.9 35.8 %collective-permute-start.26 = (bf16[256,1024]{1,0:T(8,128)(2,1)S(1)}, bf16[256,1024]{1,0:T(8,128)(2,1)}, u32[]{:S(2)}, u32[]{:S(2)}) collective-permute-start(bf16[256,1024]{1,0:T(8,128)(2,1)S(1)} %pad_maximum_fusion.refs_6_), channel_id=1, source_target_pairs={{0,64},{32,96},{64,0},{96,32},{128,192},{160,224},{192,128},{224,1... | collective-permute-start | bytes 1572872 | tf_op jit(solution)/shard_map/ppermute | solution.py:45
  198.6 27.3 %collective-permute-start.20 = (bf16[256,1024]{1,0:T(8,128)(2,1)S(1)}, bf16[256,1024]{1,0:T(8,128)(2,1)}, u32[]{:S(2)}, u32[]{:S(2)}) collective-permute-start(bf16[256,1024]{1,0:T(8,128)(2,1)S(1)} %slice.50), channel_id=1, source_target_pairs={{0,32},{32,64},{64,96},{96,0},{128,160},{160,192},{192,224},{224,1... | collective-permute-start | bytes 1572872 | tf_op jit(solution)/shard_map/ppermute | solution.py:45
  200.6 30.1 %collective-permute-start.21 = (bf16[256,1024]{1,0:T(8,128)(2,1)S(1)}, bf16[256,1024]{1,0:T(8,128)(2,1)}, u32[]{:S(2)}, u32[]{:S(2)}) collective-permute-start(bf16[256,1024]{1,0:T(8,128)(2,1)S(1)} %slice.51), channel_id=1, source_target_pairs={{0,96},{32,0},{64,32},{96,64},{128,224},{160,128},{192,160},{224,1... | collective-permute-start | bytes 1572872 | tf_op jit(solution)/shard_map/ppermute | solution.py:45
  230.7 0.8 copy-start.9
Sparse Core Ops, SparseCore 0:
  97.7 32.2 all-gather.1

commit v3 on v2

--- a/solution.py
+++ b/solution.py
@@ -61,10 +61,10 @@
 
 def loss_kernel(*refs):
     n = 4 * SIDE // 2
-    parts = refs[:n]
-    want_ref, image_ref, own_meta_ref, head_ref, second_ref = refs[n : n + 5]
-    grad_image_ref, cot_ref, back_hi_ref, back_lo_ref, gate_ref = refs[n + 5 : n + 10]
-    images, reps, metas, logit, weights, hits = refs[n + 10 :]
+    halves, wholes, refs = refs[:n], refs[n : n + n // 2], refs[n + n // 2 :]
+    want_ref, image_ref, own_meta_ref, head_ref, second_ref = refs[:5]
+    grad_image_ref, cot_ref, back_hi_ref, back_lo_ref, gate_ref = refs[5:10]
+    images, reps, metas, logit, weights, hits = refs[10:]
     n_rep = want_ref.shape[0]
     n_own = image_ref.shape[0]
     n_all = images.shape[0]
@@ -83,15 +83,19 @@
     def counted(size):
         return lax.broadcasted_iota(jnp.int32, (1, size), 1)
 
+    def piece(p, q, offset, size):
+        if p < n // 2:
+            return halves[2 * p + q // 2][pl.ds(q % 2 * block + offset, size), :]
+        return wholes[p - n // 2][pl.ds(q * block + offset, size), :]
+
     def gathered(offset):
-        for p, ref in enumerate(parts):
+        for p in range(n):
             for q in range(SIDE):
-                to = (p * SIDE + q) * each
-                reps[pl.ds(to, each), :] = ref[pl.ds(q * block + offset, each), :]
+                reps[pl.ds((p * SIDE + q) * each, each), :] = piece(p, q, offset, each)
         return reps[...]
 
-    def captions(ref):
-        return jnp.concatenate([ref[pl.ds(q * block, n_own * each), :] for q in range(SIDE)], axis=0)
+    def captions(p):
+        return jnp.concatenate([piece(p, q, 0, n_own * each) for q in range(SIDE)], axis=0)
 
     sources = jnp.concatenate([device(p, counted(SIDE * each)) for p in range(n)], axis=1)
     pick = (want_ref[...] == sources).astype(BF)
@@ -112,9 +116,9 @@
     metas[n_rep : n_rep + n_own, :] = own_meta_ref[...]
     labels = (metas[:, 8:9] * 64.0 + metas[:, 9:10]).astype(jnp.int32)
     top = None
-    for p, ref in enumerate(parts):
+    for p in range(n):
         ids = device(p, counted(step) >> 3) * 8 + (counted(step) & 7)
-        part = LOGIT_SCALE * contract(images[...], captions(ref), 1, 1)
+        part = LOGIT_SCALE * contract(images[...], captions(p), 1, 1)
         logit[:, pl.ds(p * step, step)] = part
         hits[:, pl.ds(p * step, step)] = (labels == ids).astype(BF)
         peak = jnp.max(part, axis=1, keepdims=True)
@@ -125,8 +129,8 @@
         total = total + jnp.sum(expo, axis=1, keepdims=True)
         weights[:, pl.ds(p * step, step)] = expo.astype(BF)
     mix, labelled = jnp.zeros(images.shape, F32), jnp.zeros(images.shape, F32)
-    for p, ref in enumerate(parts):
-        rows = captions(ref)
+    for p in range(n):
+        rows = captions(p)
         mix += jnp.dot(weights[:, pl.ds(p * step, step)], rows, preferred_element_type=F32)
         labelled += jnp.dot(hits[:, pl.ds(p * step, step)], rows, preferred_element_type=F32)
     grad = LOGIT_SCALE * (mix / total - labelled)
@@ -298,23 +302,23 @@
     later = after(own, known)
     below, above = shift(later, "z_hi", 1), shift(later, "z_hi", -1)
     known = spread_along(known, "x")
-    near = spread_along(jnp.concatenate(known, axis=0), "y")
+    near = [spread_along(jnp.concatenate(known[i : i + 2], axis=0), "y") for i in (0, 2)]
+    near = [half for pair in zip(*near) for half in pair]
 
     own_x = gather_x(own)
-    below, above = after(below, *near[1:]), after(above, *near[1:])
     half = n_slots // 2
     far = jnp.concatenate([shift(below[:half], "z_hi", 1), shift(above[half:], "z_hi", -1)], axis=0)
-    both = jnp.concatenate([below, above], axis=0)
+    both = after(jnp.concatenate([below, above], axis=0), *near[2:7])
     left, right = shift(both, "x", 1), shift(both, "x", -1)
-    left_far, right_far = shift(left[:n_slots], "x", 1), shift(right[n_slots:], "x", -1)
-    far = after(far, left, right)
-    far = [far, shift(far, "x", 1), shift(far, "x", -1), shift(far, "x", 2)]
-    pieces = [own_x, both, left, right, left_far, right_far] + far
-    other = [shift(p, "core", 1) for p in near]
+    other = [shift(jnp.concatenate(near[i : i + 2], axis=0), "core", 1) for i in range(0, 2 * SIDE, 2)]
+    left_far = shift(after(left[:n_slots], far, *other), "x", 1)
+    right_far = shift(after(right[n_slots:], far, *other), "x", -1)
+    far_x = gather_x(after(far, left, right))
+    pieces = [own_x, both, left, right, left_far, right_far, far_x]
 
     places = [(0, j, 0) for j in range(SIDE)]
     places += [(i, j, 1) for j in (0, -1, 1, 2) for i in (-1, 1)]
-    places += [(2, j, 1) for j in (0, -1, 1, 2)]
+    places += [(2, j, 0) for j in range(SIDE)]
     along_z, along_x, moved = (jnp.asarray(c, jnp.int32) for c in np.asarray(places).T)
     order = (z_hi + along_z) % SIDE * SIDE + (x * moved + along_x) % SIDE
     want = (order[:, None] * n_exp + jnp.arange(n_exp, dtype=jnp.int32)[None, :]).reshape(-1, 1)

time: 256 us -> 245 us (0.957)
  waiting for transfers between devices: 80.9 us -> 71.5 us
    ppermute x27, waiting for transfers between devices: 80.9 us -> 71.4 us  [shift(): return lax.ppermute(a, name, ring)]
    all_to_all x1, starting transfers between devices: 7.5 us -> 10.4 us  [body(): lax.all_to_all(buffer, 'expert', split_axis=0, concat_axis=0, tiled=True)]
  transfers between devices with their start and end apart: 29 -> 30, of which waited for: 10 -> 10; matrix products, arithmetic and copies ran while one was open for 3% -> 2% of each run, Pallas kernels for 6% -> 6%
where the time goes in v3:
time: 245 us; the launch traced here: 244 us
  starting transfers between devices  117 us (48%)
  waiting for transfers between devices  71.5 us (29%)
  Pallas kernels  30.1 us (12%)
  between operations  14.9 us (6%)
  local copies, waits for them, and re-layouts  6.89 us (3%)
    ppermute x27, starting transfers between devices, shift(): return lax.ppermute(a, name, ring)  106 us
    ppermute x27, waiting for transfers between devices, shift(): return lax.ppermute(a, name, ring)  71.4 us
    pallas_call x1, Pallas kernels, expert_grads(): pl.pallas_call(expert_kernel, out_shape=(jax.ShapeDtypeStruct((width, hid...  16 us
    pallas_call x1, Pallas kernels, image_grads(): pl.pallas_call(loss_kernel, out_shape=(jax.ShapeDtypeStruct((n_own, wide)...  14.1 us
    all_to_all x1, starting transfers between devices, body(): lax.all_to_all(buffer, 'expert', split_axis=0, concat_axis=0, tiled=True)  10.4 us
  transfers between devices with their start and end apart: 30, of which 10 were waited for; matrix products, arithmetic and copies ran while one was open for 2% of the time, Pallas kernels for 6%

profile of v3, /device:TPU:1, one launch (start us, length us, event | category | flops | bytes accessed | tf_op | source)
XLA Modules:
  0.0 244.2 jit_solution(10474761877437381960)
XLA Ops:
  7.2 0.9 fusion.1
  8.1 0.7 fusion.15
  8.8 1.2 fusion
  10.0 10.4 %all-to-all-start = ((bf16[32,8,1024]{2,1,0:T(8,128)(2,1)}), bf16[32,8,1024]{2,1,0:T(8,128)(2,1)S(1)}, u32[]{:S(2)}, u32[]{:S(2)}) async-start(bf16[32,8,1024]{2,1,0:T(8,128)(2,1)} %fusion), calls=%async_computation | async-start | bytes 1048576 | tf_op jit(solution)/shard_map/all_to_all | solution.py:285
  20.4 0.0 all-gather.3.cloned.1.call-start
  20.5 0.1 copy.20
  20.6 0.2 fusion.2
  20.8 0.7 slice.36
  21.5 0.1 pad.39.clone
  21.6 0.1 maximum_maximum_fusion
  21.7 9.5 %collective-permute-start.2 = (bf16[16,512]{1,0:T(8,128)(2,1)S(1)}, bf16[16,512]{1,0:T(8,128)(2,1)S(1)}, u32[]{:S(2)}, u32[]{:S(2)}) collective-permute-start(bf16[16,512]{1,0:T(8,128)(2,1)S(1)} %maximum_maximum_fusion), channel_id=1, source_target_pairs={{0,384},{32,416},{64,448},{96,480},{128,0},{160,32},{192,64},{224,... | collective-permute-start | bytes 49160 | tf_op jit(solution)/shard_map/ppermute | solution.py:45
  31.2 6.1 %collective-permute-start.1 = (bf16[16,512]{1,0:T(8,128)(2,1)S(1)}, bf16[16,512]{1,0:T(8,128)(2,1)S(1)}, u32[]{:S(2)}, u32[]{:S(2)}) collective-permute-start(bf16[16,512]{1,0:T(8,128)(2,1)S(1)} %maximum_maximum_fusion), channel_id=1, source_target_pairs={{0,256},{32,288},{64,320},{96,352},{128,384},{160,416},{192,448},{... | collective-permute-start | bytes 49160 | tf_op jit(solution)/shard_map/ppermute | solution.py:45
  37.3 6.1 %collective-permute-start = (bf16[16,512]{1,0:T(8,128)(2,1)S(1)}, bf16[16,512]{1,0:T(8,128)(2,1)S(1)}, u32[]{:S(2)}, u32[]{:S(2)}) collective-permute-start(bf16[16,512]{1,0:T(8,128)(2,1)S(1)} %maximum_maximum_fusion), channel_id=1, source_target_pairs={{0,128},{32,160},{64,192},{96,224},{128,256},{160,288},{192,320},{... | collective-permute-start | bytes 49160 | tf_op jit(solution)/shard_map/ppermute | solution.py:45
  43.4 0.1 fusion.18
  43.5 0.9 collective-permute-done.1
  44.4 1.5 collective-permute-done
  46.0 0.8 copy-done.1
  46.8 0.0 all-gather.3.cloned.1.call-update
  46.8 0.0 all-gather.5.cloned.1.call-start
  46.9 5.7 %collective-permute-start.5 = (bf16[40,512]{1,0:T(8,128)(2,1)S(1)}, bf16[40,512]{1,0:T(8,128)(2,1)S(1)}, u32[]{:S(2)}, u32[]{:S(2)}) collective-permute-start(bf16[40,512]{1,0:T(8,128)(2,1)S(1)} %get-tuple-element.40), channel_id=1, source_target_pairs={{0,6},{1,7},{2,0},{3,1},{4,2},{5,3},{6,4},{7,5},{8,14},{9,15},{10,... | collective-permute-start | bytes 122888 | tf_op jit(solution)/shard_map/ppermute | solution.py:45
  52.6 1.9 collective-permute-start.4
  54.5 2.3 collective-permute-start.3
  56.8 1.9 collective-permute-done.4
  58.6 2.5 %collective-permute-done.3 = bf16[40,512]{1,0:T(8,128)(2,1)S(1)} collective-permute-done((bf16[40,512]{1,0:T(8,128)(2,1)S(1)}, bf16[40,512]{1,0:T(8,128)(2,1)S(1)}, u32[]{:S(2)}, u32[]{:S(2)}) %collective-permute-start.3) | collective-permute-done | bytes 40992 | tf_op jit(solution)/shard_map/ppermute | solution.py:45
  61.3 3.1 %collective-permute-start.6 = (bf16[160,512]{1,0:T(8,128)(2,1)S(1)}, bf16[160,512]{1,0:T(8,128)(2,1)S(1)}, u32[]{:S(2)}, u32[]{:S(2)}) collective-permute-start(bf16[160,512]{1,0:T(8,128)(2,1)S(1)} %pad_maximum_fusion.6), channel_id=1, source_target_pairs={{0,32},{32,64},{64,96},{96,0},{128,160},{160,192},{192,224},{224,1... | collective-permute-start | bytes 491528 | tf_op jit(solution)/shard_map/ppermute | solution.py:45
  64.4 4.4 %collective-permute-start.10 = (bf16[160,512]{1,0:T(8,128)(2,1)S(1)}, bf16[160,512]{1,0:T(8,128)(2,1)S(1)}, u32[]{:S(2)}, u32[]{:S(2)}) collective-permute-start(bf16[160,512]{1,0:T(8,128)(2,1)S(1)} %pad_maximum_fusion.6), channel_id=1, source_target_pairs={{0,64},{32,96},{64,0},{96,32},{128,192},{160,224},{192,128},{224,1... | collective-permute-start | bytes 491528 | tf_op jit(solution)/shard_map/ppermute | solution.py:45
  68.7 3.1 %collective-permute-start.11 = (bf16[160,512]{1,0:T(8,128)(2,1)S(1)}, bf16[160,512]{1,0:T(8,128)(2,1)S(1)}, u32[]{:S(2)}, u32[]{:S(2)}) collective-permute-start(bf16[160,512]{1,0:T(8,128)(2,1)S(1)} %pad_maximum_fusion.6), channel_id=1, source_target_pairs={{0,96},{32,0},{64,32},{96,64},{128,224},{160,128},{192,160},{224,1... | collective-permute-start | bytes 491528 | tf_op jit(solution)/shard_map/ppermute | solution.py:45
  71.9 3.4 %collective-permute-start.8 = (bf16[256,1024]{1,0:T(8,128)(2,1)S(1)}, bf16[256,1024]{1,0:T(8,128)(2,1)S(1)}, u32[]{:S(2)}, u32[]{:S(2)}) collective-permute-start(bf16[256,1024]{1,0:T(8,128)(2,1)S(1)} %bitcast.45), channel_id=1, source_target_pairs={{0,384},{32,416},{64,448},{96,480},{128,0},{160,32},{192,64},{224,... | collective-permute-start | bytes 1572872 | tf_op jit(solution)/shard_map/ppermute | solution.py:45
  75.3 5.8 %collective-permute-start.7 = (bf16[256,1024]{1,0:T(8,128)(2,1)S(1)}, bf16[256,1024]{1,0:T(8,128)(2,1)S(1)}, u32[]{:S(2)}, u32[]{:S(2)}) collective-permute-start(bf16[256,1024]{1,0:T(8,128)(2,1)S(1)} %bitcast.46), channel_id=1, source_target_pairs={{0,128},{32,160},{64,192},{96,224},{128,256},{160,288},{192,320},{... | collective-permute-start | bytes 1572872 | tf_op jit(solution)/shard_map/ppermute | solution.py:45
  81.1 3.2 %collective-permute-start.9 = (bf16[320,512]{1,0:T(8,128)(2,1)S(1)}, bf16[320,512]{1,0:T(8,128)(2,1)S(1)}, u32[]{:S(2)}, u32[]{:S(2)}) collective-permute-start(bf16[320,512]{1,0:T(8,128)(2,1)S(1)} %pad_maximum_fusion.4.refs_0_), channel_id=1, source_target_pairs={{0,8},{1,9},{2,10},{3,11},{4,12},{5,13},{6,14},{7,15},{8,16},{9,17... | collective-permute-start | bytes 983048 | tf_op jit(solution)/shard_map/ppermute | solution.py:45
  84.4 4.4 %collective-permute-start.13 = (bf16[320,512]{1,0:T(8,128)(2,1)S(1)}, bf16[320,512]{1,0:T(8,128)(2,1)S(1)}, u32[]{:S(2)}, u32[]{:S(2)}) collective-permute-start(bf16[320,512]{1,0:T(8,128)(2,1)S(1)} %pad_maximum_fusion.4.refs_0_), channel_id=1, source_target_pairs={{0,16},{1,17},{2,18},{3,19},{4,20},{5,21},{6,22},{7,23},{8,24},{9,... | collective-permute-start | bytes 983048 | tf_op jit(solution)/shard_map/ppermute | solution.py:45
  88.9 1.9 collective-permute-start.12
  90.8 32.9 %collective-permute-done.8 = bf16[256,1024]{1,0:T(8,128)(2,1)S(1)} collective-permute-done((bf16[256,1024]{1,0:T(8,128)(2,1)S(1)}, bf16[256,1024]{1,0:T(8,128)(2,1)S(1)}, u32[]{:S(2)}, u32[]{:S(2)}) %collective-permute-start.8) | collective-permute-done | bytes 524320 | tf_op jit(solution)/shard_map/ppermute | solution.py:45
  123.7 4.7 %collective-permute-start.14 = (bf16[320,512]{1,0:T(8,128)(2,1)S(1)}, bf16[320,512]{1,0:T(8,128)(2,1)S(1)}, u32[]{:S(2)}, u32[]{:S(2)}) collective-permute-start(bf16[320,512]{1,0:T(8,128)(2,1)S(1)} %get-tuple-element.32.refs_1_), channel_id=1, source_target_pairs={{0,16},{1,17},{2,18},{3,19},{4,20},{5,21},{6,22},{7,23},{8,24},{9,... | collective-permute-start | bytes 983048 | tf_op jit(solution)/shard_map/ppermute | solution.py:45
  128.4 3.0 %collective-permute-start.15 = (bf16[320,512]{1,0:T(8,128)(2,1)S(1)}, bf16[320,512]{1,0:T(8,128)(2,1)S(1)}, u32[]{:S(2)}, u32[]{:S(2)}) collective-permute-start(bf16[320,512]{1,0:T(8,128)(2,1)S(1)} %pad_maximum_fusion.4.refs_0_), channel_id=1, source_target_pairs={{0,24},{1,25},{2,26},{3,27},{4,28},{5,29},{6,30},{7,31},{8,0},{9,1... | collective-permute-start | bytes 983048 | tf_op jit(solution)/shard_map/ppermute | solution.py:45
  131.5 0.1 pad_maximum_fusion.refs_1_
  131.6 4.2 %collective-permute-done.14.refs_5_ = bf16[320,512]{1,0:T(8,128)(2,1)S(1)} collective-permute-done((bf16[320,512]{1,0:T(8,128)(2,1)S(1)}, bf16[320,512]{1,0:T(8,128)(2,1)S(1)}, u32[]{:S(2)}, u32[]{:S(2)}) %collective-permute-start.14) | collective-permute-done | bytes 327712 | tf_op jit(solution)/shard_map/ppermute | solution.py:45
  135.8 7.3 %collective-permute-done.15.refs_6_ = bf16[320,512]{1,0:T(8,128)(2,1)S(1)} collective-permute-done((bf16[320,512]{1,0:T(8,128)(2,1)S(1)}, bf16[320,512]{1,0:T(8,128)(2,1)S(1)}, u32[]{:S(2)}, u32[]{:S(2)}) %collective-permute-start.15) | collective-permute-done | bytes 327712 | tf_op jit(solution)/shard_map/ppermute | solution.py:45
  143.1 2.2 collective-permute-start.16
  145.3 4.3 %collective-permute-start.17 = (bf16[512,1024]{1,0:T(8,128)(2,1)S(1)}, bf16[512,1024]{1,0:T(8,128)(2,1)}, u32[]{:S(2)}, u32[]{:S(2)}) collective-permute-start(bf16[512,1024]{1,0:T(8,128)(2,1)S(1)} %pad_maximum_fusion.refs_1_), channel_id=1, source_target_pairs={{0,96},{32,0},{64,32},{96,64},{128,224},{160,128},{192,160},{224,1... | collective-permute-start | bytes 3145736 | tf_op jit(solution)/shard_map/ppermute | solution.py:45
  149.7 3.4 %collective-permute-start.23 = (bf16[128,1024]{1,0:T(8,128)(2,1)S(1)}, bf16[128,1024]{1,0:T(8,128)(2,1)S(1)}, u32[]{:S(2)}, u32[]{:S(2)}) collective-permute-start(bf16[128,1024]{1,0:T(8,128)(2,1)S(1)} %slice.51), channel_id=1, source_target_pairs={{0,128},{32,160},{64,192},{96,224},{128,256},{160,288},{192,320},{... | collective-permute-start | bytes 786440 | tf_op jit(solution)/shard_map/ppermute | solution.py:45
  153.1 5.8 %collective-permute-start.24 = (bf16[128,1024]{1,0:T(8,128)(2,1)S(1)}, bf16[128,1024]{1,0:T(8,128)(2,1)S(1)}, u32[]{:S(2)}, u32[]{:S(2)}) collective-permute-start(bf16[128,1024]{1,0:T(8,128)(2,1)S(1)} %slice.52), channel_id=1, source_target_pairs={{0,384},{32,416},{64,448},{96,480},{128,0},{160,32},{192,64},{224,... | collective-permute-start | bytes 786440 | tf_op jit(solution)/shard_map/ppermute | solution.py:45
  158.9 7.6 %collective-permute-done.23 = bf16[128,1024]{1,0:T(8,128)(2,1)S(1)} collective-permute-done((bf16[128,1024]{1,0:T(8,128)(2,1)S(1)}, bf16[128,1024]{1,0:T(8,128)(2,1)S(1)}, u32[]{:S(2)}, u32[]{:S(2)}) %collective-permute-start.23) | collective-permute-done | bytes 262176 | tf_op jit(solution)/shard_map/ppermute | solution.py:45
  166.5 8.3 %collective-permute-done.24 = bf16[128,1024]{1,0:T(8,128)(2,1)S(1)} collective-permute-done((bf16[128,1024]{1,0:T(8,128)(2,1)S(1)}, bf16[128,1024]{1,0:T(8,128)(2,1)S(1)}, u32[]{:S(2)}, u32[]{:S(2)}) %collective-permute-start.24) | collective-permute-done | bytes 262176 | tf_op jit(solution)/shard_map/ppermute | solution.py:45
  174.8 0.8 copy-done.3
  175.6 5.3 %collective-permute-start.18 = (bf16[320,512]{1,0:T(8,128)(2,1)}, bf16[320,512]{1,0:T(8,128)(2,1)S(1)}, u32[]{:S(2)}, u32[]{:S(2)}) collective-permute-start(bf16[320,512]{1,0:T(8,128)(2,1)} %copy-done.13), channel_id=1, source_target_pairs={{0,24},{1,25},{2,26},{3,27},{4,28},{5,29},{6,30},{7,31},{8,0},{9,1... | collective-permute-start | bytes 983048 | tf_op jit(solution)/shard_map/ppermute | solution.py:45
  181.0 3.5 %collective-permute-start.19 = (bf16[640,512]{1,0:T(8,128)(2,1)}, bf16[640,512]{1,0:T(8,128)(2,1)S(1)}, u32[]{:S(2)}, u32[]{:S(2)}) collective-permute-start(bf16[640,512]{1,0:T(8,128)(2,1)} %copy-done.15), channel_id=1, source_target_pairs={{0,1},{1,0},{2,3},{3,2},{4,5},{5,4},{6,7},{7,6},{8,9},{9,8},{10,11... | collective-permute-start | bytes 1966088 | tf_op jit(solution)/shard_map/ppermute | solution.py:45
  184.6 2.1 collective-permute-start.20
  186.7 2.4 collective-permute-start.21
  189.2 1.9 collective-permute-start.22
  191.2 0.1 copy.21
  191.3 0.1 iota_add_fusion
  191.4 1.0 add.76.refs_12_
  192.3 0.7 pad_convert_fusion.refs_14_
  193.0 1.1 slice.50
  194.1 1.9 collective-permute-start.25
  196.1 1.1 slice.53
  197.2 4.7 %collective-permute-start.26 = (bf16[256,1024]{1,0:T(8,128)(2,1)S(1)}, bf16[256,1024]{1,0:T(8,128)(2,1)S(1)}, u32[]{:S(2)}, u32[]{:S(2)}) collective-permute-start(bf16[256,1024]{1,0:T(8,128)(2,1)S(1)} %slice.53), channel_id=1, source_target_pairs={{0,96},{32,0},{64,32},{96,64},{128,224},{160,128},{192,160},{224,1... | collective-permute-start | bytes 1572872 | tf_op jit(solution)/shard_map/ppermute | solution.py:45
  201.9 14.1 %shard_map.139 = (f32[8,512]{1,0:T(8,128)}, bf16[512,1024]{1,0:T(8,128)(2,1)}, bf16[512,256]{1,0:T(8,128)(2,1)}, bf16[512,256]{1,0:T(8,128)(2,1)}, bf16[512,128]{1,0:T(8,128)(2,1)}) custom-call(bf16[320,512]{1,0:T(8,128)(2,1)} %copy-done.12, bf16[320,512]{1,0:T(8,128)(2,1)} %copy-done.13, bf16[320,512]{1,0:T(8,128)(2,1)} %copy-done.5, ...), custom_call_target="tpu_custom_call" | custom-call | flops 10000000000 | bytes 9000000 | tf_op jit(solution)/shard_map/pallas_call | solution.py:152
  216.0 4.4 %collective-permute-done.25.refs_4_ = bf16[256,1024]{1,0:T(8,128)(2,1)S(1)} collective-permute-done((bf16[256,1024]{1,0:T(8,128)(2,1)S(1)}, bf16[256,1024]{1,0:T(8,128)(2,1)S(1)}, u32[]{:S(2)}, u32[]{:S(2)}) %collective-permute-start.25) | collective-permute-done | bytes 524320 | tf_op jit(solution)/shard_map/ppermute | solution.py:45
  220.4 0.0 all-gather.5.cloned.1.call-done.refs_6_
  220.5 0.7 copy-done.20
  221.2 0.2 copy-done.21
  221.4 16.0 %shard_map.140 = (f32[1024,256]{1,0:T(8,128)}, f32[256,1024]{1,0:T(8,128)}) custom-call(bf16[1024,1024]{1,0:T(8,128)(2,1)} %all-gather.3.cloned.1.call-done.refs_0_, bf16[512,1024]{1,0:T(8,128)(2,1)} %copy-done.4, bf16[512,1024]{1,0:T(8,128)(2,1)} %collective-permute-done.16.refs_2_, bf16[512,1024]{1,0:T(8,128)(2,1)} %collective-permute-done.17.refs_3_, ...), custom_call_target="tpu_custom_call" | custom-call | flops 5000000000 | bytes 13000000 | tf_op jit(solution)/shard_map/pallas_call | solution.py:237
  (96 shorter events, 0.7 us)
Async XLA Ops:
  7.2 1.6 copy-start
  7.2 13.3 %copy-start.22 = (s32[8]{0:T(128)S(1)}, s32[8]{0:T(128)}, u32[]{:S(2)}) copy-start(s32[8]{0:T(128)} %param.20) | copy-start | bytes 100
  7.2 13.4 %copy-start.23 = (bf16[128]{0:T(256)(128)(2,1)S(1)}, bf16[128]{0:T(256)(128)(2,1)}, u32[]{:S(2)}) copy-start(bf16[128]{0:T(256)(128)(2,1)} %param.14) | copy-start | bytes 772
  7.2 14.4 %copy-start.14 = (bf16[8,512]{1,0:T(8,128)(2,1)S(1)}, bf16[8,512]{1,0:T(8,128)(2,1)}, u32[]{:S(2)}) copy-start(bf16[8,512]{1,0:T(8,128)(2,1)} %param.19) | copy-start | bytes 24580
  10.0 36.0 %all-to-all-start = ((bf16[32,8,1024]{2,1,0:T(8,128)(2,1)}), bf16[32,8,1024]{2,1,0:T(8,128)(2,1)S(1)}, u32[]{:S(2)}, u32[]{:S(2)}) async-start(bf16[32,8,1024]{2,1,0:T(8,128)(2,1)} %fusion), calls=%async_computation | async-start | bytes 1048576 | tf_op jit(solution)/shard_map/all_to_all | solution.py:285
  20.4 200.0 %all-gather.3.cloned.1.call-start = ((), (), s32[]{:S(2)}) async-start(), calls=%async_computation.1 | async-start | bytes 2621440 | tf_op jit(solution)/shard_map/all_gather | solution.py:55
  21.7 21.8 %collective-permute-start.2 = (bf16[16,512]{1,0:T(8,128)(2,1)S(1)}, bf16[16,512]{1,0:T(8,128)(2,1)S(1)}, u32[]{:S(2)}, u32[]{:S(2)}) collective-permute-start(bf16[16,512]{1,0:T(8,128)(2,1)S(1)} %maximum_maximum_fusion), channel_id=1, source_target_pairs={{0,384},{32,416},{64,448},{96,480},{128,0},{160,32},{192,64},{224,... | collective-permute-start | bytes 49160 | tf_op jit(solution)/shard_map/ppermute | solution.py:45
  31.2 13.2 %collective-permute-start.1 = (bf16[16,512]{1,0:T(8,128)(2,1)S(1)}, bf16[16,512]{1,0:T(8,128)(2,1)S(1)}, u32[]{:S(2)}, u32[]{:S(2)}) collective-permute-start(bf16[16,512]{1,0:T(8,128)(2,1)S(1)} %maximum_maximum_fusion), channel_id=1, source_target_pairs={{0,256},{32,288},{64,320},{96,352},{128,384},{160,416},{192,448},{... | collective-permute-start | bytes 49160 | tf_op jit(solution)/shard_map/ppermute | solution.py:45
  37.3 8.6 %collective-permute-start = (bf16[16,512]{1,0:T(8,128)(2,1)S(1)}, bf16[16,512]{1,0:T(8,128)(2,1)S(1)}, u32[]{:S(2)}, u32[]{:S(2)}) collective-permute-start(bf16[16,512]{1,0:T(8,128)(2,1)S(1)} %maximum_maximum_fusion), channel_id=1, source_target_pairs={{0,128},{32,160},{64,192},{96,224},{128,256},{160,288},{192,320},{... | collective-permute-start | bytes 49160 | tf_op jit(solution)/shard_map/ppermute | solution.py:45
  46.0 0.8 copy-start.1
  46.8 25.0 %copy-start.2 = (bf16[32,8,1024]{2,1,0:T(8,128)(2,1)S(1)}, bf16[32,8,1024]{2,1,0:T(8,128)(2,1)}, u32[]{:S(2)}) copy-start(bf16[32,8,1024]{2,1,0:T(8,128)(2,1)} %copy-done.1) | copy-start | bytes 1572868
  46.8 173.6 %all-gather.5.cloned.1.call-start = ((), (), s32[]{:S(2)}) async-start(), calls=%async_computation.2 | async-start | bytes 2621440 | tf_op jit(solution)/shard_map/all_gather | solution.py:55
  46.9 9.9 %collective-permute-start.5 = (bf16[40,512]{1,0:T(8,128)(2,1)S(1)}, bf16[40,512]{1,0:T(8,128)(2,1)S(1)}, u32[]{:S(2)}, u32[]{:S(2)}) collective-permute-start(bf16[40,512]{1,0:T(8,128)(2,1)S(1)} %get-tuple-element.40), channel_id=1, source_target_pairs={{0,6},{1,7},{2,0},{3,1},{4,2},{5,3},{6,4},{7,5},{8,14},{9,15},{10,... | collective-permute-start | bytes 122888 | tf_op jit(solution)/shard_map/ppermute | solution.py:45
  52.6 6.1 %collective-permute-start.4 = (bf16[40,512]{1,0:T(8,128)(2,1)S(1)}, bf16[40,512]{1,0:T(8,128)(2,1)S(1)}, u32[]{:S(2)}, u32[]{:S(2)}) collective-permute-start(bf16[40,512]{1,0:T(8,128)(2,1)S(1)} %get-tuple-element.40), channel_id=1, source_target_pairs={{0,4},{1,5},{2,6},{3,7},{4,0},{5,1},{6,2},{7,3},{8,12},{9,13},{10,... | collective-permute-start | bytes 122888 | tf_op jit(solution)/shard_map/ppermute | solution.py:45
  54.5 6.6 %collective-permute-start.3 = (bf16[40,512]{1,0:T(8,128)(2,1)S(1)}, bf16[40,512]{1,0:T(8,128)(2,1)S(1)}, u32[]{:S(2)}, u32[]{:S(2)}) collective-permute-start(bf16[40,512]{1,0:T(8,128)(2,1)S(1)} %get-tuple-element.40), channel_id=1, source_target_pairs={{0,2},{1,3},{2,4},{3,5},{4,6},{5,7},{6,0},{7,1},{8,10},{9,11},{10,... | collective-permute-start | bytes 122888 | tf_op jit(solution)/shard_map/ppermute | solution.py:45
  61.3 19.8 %collective-permute-start.6 = (bf16[160,512]{1,0:T(8,128)(2,1)S(1)}, bf16[160,512]{1,0:T(8,128)(2,1)S(1)}, u32[]{:S(2)}, u32[]{:S(2)}) collective-permute-start(bf16[160,512]{1,0:T(8,128)(2,1)S(1)} %pad_maximum_fusion.6), channel_id=1, source_target_pairs={{0,32},{32,64},{64,96},{96,0},{128,160},{160,192},{192,224},{224,1... | collective-permute-start | bytes 491528 | tf_op jit(solution)/shard_map/ppermute | solution.py:45
  64.4 20.0 %collective-permute-start.10 = (bf16[160,512]{1,0:T(8,128)(2,1)S(1)}, bf16[160,512]{1,0:T(8,128)(2,1)S(1)}, u32[]{:S(2)}, u32[]{:S(2)}) collective-permute-start(bf16[160,512]{1,0:T(8,128)(2,1)S(1)} %pad_maximum_fusion.6), channel_id=1, source_target_pairs={{0,64},{32,96},{64,0},{96,32},{128,192},{160,224},{192,128},{224,1... | collective-permute-start | bytes 491528 | tf_op jit(solution)/shard_map/ppermute | solution.py:45
  68.7 20.0 %collective-permute-start.11 = (bf16[160,512]{1,0:T(8,128)(2,1)S(1)}, bf16[160,512]{1,0:T(8,128)(2,1)S(1)}, u32[]{:S(2)}, u32[]{:S(2)}) collective-permute-start(bf16[160,512]{1,0:T(8,128)(2,1)S(1)} %pad_maximum_fusion.6), channel_id=1, source_target_pairs={{0,96},{32,0},{64,32},{96,64},{128,224},{160,128},{192,160},{224,1... | collective-permute-start | bytes 491528 | tf_op jit(solution)/shard_map/ppermute | solution.py:45
  71.9 51.8 %collective-permute-start.8 = (bf16[256,1024]{1,0:T(8,128)(2,1)S(1)}, bf16[256,1024]{1,0:T(8,128)(2,1)S(1)}, u32[]{:S(2)}, u32[]{:S(2)}) collective-permute-start(bf16[256,1024]{1,0:T(8,128)(2,1)S(1)} %bitcast.45), channel_id=1, source_target_pairs={{0,384},{32,416},{64,448},{96,480},{128,0},{160,32},{192,64},{224,... | collective-permute-start | bytes 1572872 | tf_op jit(solution)/shard_map/ppermute | solution.py:45
  75.3 53.1 %collective-permute-start.7 = (bf16[256,1024]{1,0:T(8,128)(2,1)S(1)}, bf16[256,1024]{1,0:T(8,128)(2,1)S(1)}, u32[]{:S(2)}, u32[]{:S(2)}) collective-permute-start(bf16[256,1024]{1,0:T(8,128)(2,1)S(1)} %bitcast.46), channel_id=1, source_target_pairs={{0,128},{32,160},{64,192},{96,224},{128,256},{160,288},{192,320},{... | collective-permute-start | bytes 1572872 | tf_op jit(solution)/shard_map/ppermute | solution.py:45
  81.1 50.4 %copy-start.12 = (bf16[320,512]{1,0:T(8,128)(2,1)}, bf16[320,512]{1,0:T(8,128)(2,1)S(1)}, u32[]{:S(2)}) copy-start(bf16[320,512]{1,0:T(8,128)(2,1)S(1)} %pad_maximum_fusion.4.refs_0_) | copy-start | bytes 983044
  81.1 50.4 %collective-permute-start.9 = (bf16[320,512]{1,0:T(8,128)(2,1)S(1)}, bf16[320,512]{1,0:T(8,128)(2,1)S(1)}, u32[]{:S(2)}, u32[]{:S(2)}) collective-permute-start(bf16[320,512]{1,0:T(8,128)(2,1)S(1)} %pad_maximum_fusion.4.refs_0_), channel_id=1, source_target_pairs={{0,8},{1,9},{2,10},{3,11},{4,12},{5,13},{6,14},{7,15},{8,16},{9,17... | collective-permute-start | bytes 983048 | tf_op jit(solution)/shard_map/ppermute | solution.py:45
  84.4 47.2 %collective-permute-start.13 = (bf16[320,512]{1,0:T(8,128)(2,1)S(1)}, bf16[320,512]{1,0:T(8,128)(2,1)S(1)}, u32[]{:S(2)}, u32[]{:S(2)}) collective-permute-start(bf16[320,512]{1,0:T(8,128)(2,1)S(1)} %pad_maximum_fusion.4.refs_0_), channel_id=1, source_target_pairs={{0,16},{1,17},{2,18},{3,19},{4,20},{5,21},{6,22},{7,23},{8,24},{9,... | collective-permute-start | bytes 983048 | tf_op jit(solution)/shard_map/ppermute | solution.py:45
  88.8 39.6 %copy-start.15 = (bf16[640,512]{1,0:T(8,128)(2,1)}, bf16[640,512]{1,0:T(8,128)(2,1)S(1)}, u32[]{:S(2)}) copy-start(bf16[640,512]{1,0:T(8,128)(2,1)S(1)} %get-tuple-element.31) | copy-start | bytes 1966084
  88.8 60.8 %copy-start.13 = (bf16[320,512]{1,0:T(8,128)(2,1)}, bf16[320,512]{1,0:T(8,128)(2,1)S(1)}, u32[]{:S(2)}) copy-start(bf16[320,512]{1,0:T(8,128)(2,1)S(1)} %get-tuple-element.32.refs_1_) | copy-start | bytes 983044
  88.9 42.7 %collective-permute-start.12 = (bf16[320,512]{1,0:T(8,128)(2,1)S(1)}, bf16[320,512]{1,0:T(8,128)(2,1)S(1)}, u32[]{:S(2)}, u32[]{:S(2)}) collective-permute-start(bf16[320,512]{1,0:T(8,128)(2,1)S(1)} %get-tuple-element.32.refs_1_), channel_id=1, source_target_pairs={{0,8},{1,9},{2,10},{3,11},{4,12},{5,13},{6,14},{7,15},{8,16},{9,17... | collective-permute-start | bytes 983048 | tf_op jit(solution)/shard_map/ppermute | solution.py:45
  123.7 12.1 %collective-permute-start.14 = (bf16[320,512]{1,0:T(8,128)(2,1)S(1)}, bf16[320,512]{1,0:T(8,128)(2,1)S(1)}, u32[]{:S(2)}, u32[]{:S(2)}) collective-permute-start(bf16[320,512]{1,0:T(8,128)(2,1)S(1)} %get-tuple-element.32.refs_1_), channel_id=1, source_target_pairs={{0,16},{1,17},{2,18},{3,19},{4,20},{5,21},{6,22},{7,23},{8,24},{9,... | collective-permute-start | bytes 983048 | tf_op jit(solution)/shard_map/ppermute | solution.py:45
  128.4 14.7 %collective-permute-start.15 = (bf16[320,512]{1,0:T(8,128)(2,1)S(1)}, bf16[320,512]{1,0:T(8,128)(2,1)S(1)}, u32[]{:S(2)}, u32[]{:S(2)}) collective-permute-start(bf16[320,512]{1,0:T(8,128)(2,1)S(1)} %pad_maximum_fusion.4.refs_0_), channel_id=1, source_target_pairs={{0,24},{1,25},{2,26},{3,27},{4,28},{5,29},{6,30},{7,31},{8,0},{9,1... | collective-permute-start | bytes 983048 | tf_op jit(solution)/shard_map/ppermute | solution.py:45
  131.6 44.1 %copy-start.4 = (bf16[512,1024]{1,0:T(8,128)(2,1)}, bf16[512,1024]{1,0:T(8,128)(2,1)S(1)}, u32[]{:S(2)}) copy-start(bf16[512,1024]{1,0:T(8,128)(2,1)S(1)} %pad_maximum_fusion.refs_1_) | copy-start | bytes 3145732
  131.6 52.9 %copy-start.5 = (bf16[320,512]{1,0:T(8,128)(2,1)}, bf16[320,512]{1,0:T(8,128)(2,1)S(1)}, u32[]{:S(2)}) copy-start(bf16[320,512]{1,0:T(8,128)(2,1)S(1)} %collective-permute-done.9.refs_2_) | copy-start | bytes 983044
  131.6 52.9 %copy-start.7 = (bf16[320,512]{1,0:T(8,128)(2,1)}, bf16[320,512]{1,0:T(8,128)(2,1)S(1)}, u32[]{:S(2)}) copy-start(bf16[320,512]{1,0:T(8,128)(2,1)S(1)} %collective-permute-done.12.refs_3_) | copy-start | bytes 983044
  131.6 55.0 %copy-start.6 = (bf16[320,512]{1,0:T(8,128)(2,1)}, bf16[320,512]{1,0:T(8,128)(2,1)S(1)}, u32[]{:S(2)}) copy-start(bf16[320,512]{1,0:T(8,128)(2,1)S(1)} %collective-permute-done.13.refs_4_) | copy-start | bytes 983044
  135.8 58.3 %copy-start.8 = (bf16[320,512]{1,0:T(8,128)(2,1)}, bf16[320,512]{1,0:T(8,128)(2,1)S(1)}, u32[]{:S(2)}) copy-start(bf16[320,512]{1,0:T(8,128)(2,1)S(1)} %collective-permute-done.14.refs_5_) | copy-start | bytes 983044
  143.1 15.8 %copy-start.9 = (bf16[320,512]{1,0:T(8,128)(2,1)}, bf16[320,512]{1,0:T(8,128)(2,1)S(1)}, u32[]{:S(2)}) copy-start(bf16[320,512]{1,0:T(8,128)(2,1)S(1)} %collective-permute-done.15.refs_6_) | copy-start | bytes 983044
  143.1 31.7 %collective-permute-start.16 = (bf16[512,1024]{1,0:T(8,128)(2,1)S(1)}, bf16[512,1024]{1,0:T(8,128)(2,1)}, u32[]{:S(2)}, u32[]{:S(2)}) collective-permute-start(bf16[512,1024]{1,0:T(8,128)(2,1)S(1)} %pad_maximum_fusion.refs_1_), channel_id=1, source_target_pairs={{0,32},{32,64},{64,96},{96,0},{128,160},{160,192},{192,224},{224,1... | collective-permute-start | bytes 3145736 | tf_op jit(solution)/shard_map/ppermute | solution.py:45
  145.3 29.5 %collective-permute-start.17 = (bf16[512,1024]{1,0:T(8,128)(2,1)S(1)}, bf16[512,1024]{1,0:T(8,128)(2,1)}, u32[]{:S(2)}, u32[]{:S(2)}) collective-permute-start(bf16[512,1024]{1,0:T(8,128)(2,1)S(1)} %pad_maximum_fusion.refs_1_), channel_id=1, source_target_pairs={{0,96},{32,0},{64,32},{96,64},{128,224},{160,128},{192,160},{224,1... | collective-permute-start | bytes 3145736 | tf_op jit(solution)/shard_map/ppermute | solution.py:45
  149.7 16.8 %collective-permute-start.23 = (bf16[128,1024]{1,0:T(8,128)(2,1)S(1)}, bf16[128,1024]{1,0:T(8,128)(2,1)S(1)}, u32[]{:S(2)}, u32[]{:S(2)}) collective-permute-start(bf16[128,1024]{1,0:T(8,128)(2,1)S(1)} %slice.51), channel_id=1, source_target_pairs={{0,128},{32,160},{64,192},{96,224},{128,256},{160,288},{192,320},{... | collective-permute-start | bytes 786440 | tf_op jit(solution)/shard_map/ppermute | solution.py:45
  153.1 21.7 %collective-permute-start.24 = (bf16[128,1024]{1,0:T(8,128)(2,1)S(1)}, bf16[128,1024]{1,0:T(8,128)(2,1)S(1)}, u32[]{:S(2)}, u32[]{:S(2)}) collective-permute-start(bf16[128,1024]{1,0:T(8,128)(2,1)S(1)} %slice.52), channel_id=1, source_target_pairs={{0,384},{32,416},{64,448},{96,480},{128,0},{160,32},{192,64},{224,... | collective-permute-start | bytes 786440 | tf_op jit(solution)/shard_map/ppermute | solution.py:45
  174.8 0.8 copy-start.3
  175.6 13.5 %collective-permute-start.18 = (bf16[320,512]{1,0:T(8,128)(2,1)}, bf16[320,512]{1,0:T(8,128)(2,1)S(1)}, u32[]{:S(2)}, u32[]{:S(2)}) collective-permute-start(bf16[320,512]{1,0:T(8,128)(2,1)} %copy-done.13), channel_id=1, source_target_pairs={{0,24},{1,25},{2,26},{3,27},{4,28},{5,29},{6,30},{7,31},{8,0},{9,1... | collective-permute-start | bytes 983048 | tf_op jit(solution)/shard_map/ppermute | solution.py:45
  181.0 8.2 %copy-start.10 = (bf16[320,512]{1,0:T(8,128)(2,1)S(1)}, bf16[320,512]{1,0:T(8,128)(2,1)}, u32[]{:S(2)}) copy-start(bf16[320,512]{1,0:T(8,128)(2,1)} %copy-done.9) | copy-start | bytes 983044
  181.0 13.1 %collective-permute-start.19 = (bf16[640,512]{1,0:T(8,128)(2,1)}, bf16[640,512]{1,0:T(8,128)(2,1)S(1)}, u32[]{:S(2)}, u32[]{:S(2)}) collective-permute-start(bf16[640,512]{1,0:T(8,128)(2,1)} %copy-done.15), channel_id=1, source_target_pairs={{0,1},{1,0},{2,3},{3,2},{4,5},{5,4},{6,7},{7,6},{8,9},{9,8},{10,11... | collective-permute-start | bytes 1966088 | tf_op jit(solution)/shard_map/ppermute | solution.py:45
  184.5 6.7 %copy-start.16 = (s32[16]{0:T(128)S(1)}, s32[16]{0:T(128)}, u32[]{:S(2)}) copy-start(s32[16]{0:T(128)} %constant.89.clone) | copy-start | bytes 196
  184.6 6.7 %copy-start.17 = (s32[16]{0:T(128)S(1)}, s32[16]{0:T(128)}, u32[]{:S(2)}) copy-start(s32[16]{0:T(128)} %constant.90.clone) | copy-start | bytes 196
  184.6 6.7 %copy-start.18 = (s32[16]{0:T(128)S(1)}, s32[16]{0:T(128)}, u32[]{:S(2)}) copy-start(s32[16]{0:T(128)} %constant.91.clone) | copy-start | bytes 196
  184.6 9.5 %collective-permute-start.20 = (bf16[640,512]{1,0:T(8,128)(2,1)S(1)}, bf16[640,512]{1,0:T(8,128)(2,1)}, u32[]{:S(2)}, u32[]{:S(2)}) collective-permute-start(bf16[640,512]{1,0:T(8,128)(2,1)S(1)} %pad_maximum_fusion.1), channel_id=1, source_target_pairs={{0,1},{1,0},{2,3},{3,2},{4,5},{5,4},{6,7},{7,6},{8,9},{9,8},{10,11... | collective-permute-start | bytes 1966088 | tf_op jit(solution)/shard_map/ppermute | solution.py:45
  186.7 7.4 %collective-permute-start.21 = (bf16[640,512]{1,0:T(8,128)(2,1)S(1)}, bf16[640,512]{1,0:T(8,128)(2,1)}, u32[]{:S(2)}, u32[]{:S(2)}) collective-permute-start(bf16[640,512]{1,0:T(8,128)(2,1)S(1)} %pad_maximum_fusion.2), channel_id=1, source_target_pairs={{0,1},{1,0},{2,3},{3,2},{4,5},{5,4},{6,7},{7,6},{8,9},{9,8},{10,11... | collective-permute-start | bytes 1966088 | tf_op jit(solution)/shard_map/ppermute | solution.py:45
  189.1 2.0 copy-start.11
  189.2 4.9 %collective-permute-start.22 = (bf16[640,512]{1,0:T(8,128)(2,1)S(1)}, bf16[640,512]{1,0:T(8,128)(2,1)}, u32[]{:S(2)}, u32[]{:S(2)}) collective-permute-start(bf16[640,512]{1,0:T(8,128)(2,1)S(1)} %pad_maximum_fusion.3), channel_id=1, source_target_pairs={{0,1},{1,0},{2,3},{3,2},{4,5},{5,4},{6,7},{7,6},{8,9},{9,8},{10,11... | collective-permute-start | bytes 1966088 | tf_op jit(solution)/shard_map/ppermute | solution.py:45
  194.1 7.8 %copy-start.19 = (bf16[640,512]{1,0:T(8,128)(2,1)}, bf16[640,512]{1,0:T(8,128)(2,1)S(1)}, u32[]{:S(2)}) copy-start(bf16[640,512]{1,0:T(8,128)(2,1)S(1)} %collective-permute-done.19.refs_8_) | copy-start | bytes 1966084
  194.1 26.3 %collective-permute-start.25 = (bf16[256,1024]{1,0:T(8,128)(2,1)S(1)}, bf16[256,1024]{1,0:T(8,128)(2,1)S(1)}, u32[]{:S(2)}, u32[]{:S(2)}) collective-permute-start(bf16[256,1024]{1,0:T(8,128)(2,1)S(1)} %slice.50), channel_id=1, source_target_pairs={{0,32},{32,64},{64,96},{96,0},{128,160},{160,192},{192,224},{224,1... | collective-permute-start | bytes 1572872 | tf_op jit(solution)/shard_map/ppermute | solution.py:45
  197.2 23.3 %collective-permute-start.26 = (bf16[256,1024]{1,0:T(8,128)(2,1)S(1)}, bf16[256,1024]{1,0:T(8,128)(2,1)S(1)}, u32[]{:S(2)}, u32[]{:S(2)}) collective-permute-start(bf16[256,1024]{1,0:T(8,128)(2,1)S(1)} %slice.53), channel_id=1, source_target_pairs={{0,96},{32,0},{64,32},{96,64},{128,224},{160,128},{192,160},{224,1... | collective-permute-start | bytes 1572872 | tf_op jit(solution)/shard_map/ppermute | solution.py:45
  220.4 0.8 copy-start.20
  220.4 1.0 copy-start.21
Sparse Core Ops, SparseCore 0:
  46.9 44.2 all-gather.2
  175.7 42.7 all-gather.4

commit v4 on v3

--- a/solution.py
+++ b/solution.py
@@ -308,7 +308,7 @@
     own_x = gather_x(own)
     half = n_slots // 2
     far = jnp.concatenate([shift(below[:half], "z_hi", 1), shift(above[half:], "z_hi", -1)], axis=0)
-    both = after(jnp.concatenate([below, above], axis=0), *near[2:7])
+    both = after(jnp.concatenate([below, above], axis=0), *near[2:5])
     left, right = shift(both, "x", 1), shift(both, "x", -1)
     other = [shift(jnp.concatenate(near[i : i + 2], axis=0), "core", 1) for i in range(0, 2 * SIDE, 2)]
     left_far = shift(after(left[:n_slots], far, *other), "x", 1)

time: 245 us -> 248 us (1.012)
  local copies, waits for them, and re-layouts: 6.89 us -> 10.7 us
  waiting for transfers between devices: 71.5 us -> 67.9 us
    ppermute x27, waiting for transfers between devices: 71.4 us -> 67.8 us  [shift(): return lax.ppermute(a, name, ring)]
    unnamed x55 -> x51, local copies, waits for them, and re-layouts: 2.64 us -> 5.81 us
  transfers between devices with their start and end apart: 30 -> 30, of which waited for: 10 -> 8; matrix products, arithmetic and copies ran while one was open for 2% -> 4% of each run, Pallas kernels for 6% -> 6%
where the time goes in v4:
time: 248 us; the launch traced here: 246 us
  starting transfers between devices  119 us (48%)
  waiting for transfers between devices  67.9 us (27%)
  Pallas kernels  30 us (12%)
  between operations  14.8 us (6%)
  local copies, waits for them, and re-layouts  10.7 us (4%)
    ppermute x27, starting transfers between devices, shift(): return lax.ppermute(a, name, ring)  108 us
    ppermute x27, waiting for transfers between devices, shift(): return lax.ppermute(a, name, ring)  67.8 us
    pallas_call x1, Pallas kernels, expert_grads(): pl.pallas_call(expert_kernel, out_shape=(jax.ShapeDtypeStruct((width, hid...  16 us
    pallas_call x1, Pallas kernels, image_grads(): pl.pallas_call(loss_kernel, out_shape=(jax.ShapeDtypeStruct((n_own, wide)...  14.1 us
    all_to_all x1, starting transfers between devices, body(): lax.all_to_all(buffer, 'expert', split_axis=0, concat_axis=0, tiled=True)  10.4 us
    unnamed x51, local copies, waits for them, and re-layouts  5.81 us
  transfers between devices with their start and end apart: 30, of which 8 were waited for; matrix products, arithmetic and copies ran while one was open for 4% of the time, Pallas kernels for 6%

profile of v4, /device:TPU:1, one launch (start us, length us, event | category | flops | bytes accessed | tf_op | source)
XLA Modules:
  0.0 246.4 jit_solution(10542115903406034112)
XLA Ops:
  7.2 0.9 fusion.1
  8.1 0.7 fusion.15
  8.8 1.2 fusion
  10.0 10.4 %all-to-all-start = ((bf16[32,8,1024]{2,1,0:T(8,128)(2,1)}), bf16[32,8,1024]{2,1,0:T(8,128)(2,1)S(1)}, u32[]{:S(2)}, u32[]{:S(2)}) async-start(bf16[32,8,1024]{2,1,0:T(8,128)(2,1)} %fusion), calls=%async_computation | async-start | bytes 1048576 | tf_op jit(solution)/shard_map/all_to_all | solution.py:285
  20.5 0.1 copy.20
  20.6 0.2 fusion.2
  20.8 0.7 slice.36
  21.5 0.1 pad.39.clone
  21.6 0.1 maximum_maximum_fusion
  21.7 9.5 %collective-permute-start.2 = (bf16[16,512]{1,0:T(8,128)(2,1)S(1)}, bf16[16,512]{1,0:T(8,128)(2,1)S(1)}, u32[]{:S(2)}, u32[]{:S(2)}) collective-permute-start(bf16[16,512]{1,0:T(8,128)(2,1)S(1)} %maximum_maximum_fusion), channel_id=1, source_target_pairs={{0,384},{32,416},{64,448},{96,480},{128,0},{160,32},{192,64},{224,... | collective-permute-start | bytes 49160 | tf_op jit(solution)/shard_map/ppermute | solution.py:45
  31.2 6.1 %collective-permute-start.1 = (bf16[16,512]{1,0:T(8,128)(2,1)S(1)}, bf16[16,512]{1,0:T(8,128)(2,1)S(1)}, u32[]{:S(2)}, u32[]{:S(2)}) collective-permute-start(bf16[16,512]{1,0:T(8,128)(2,1)S(1)} %maximum_maximum_fusion), channel_id=1, source_target_pairs={{0,256},{32,288},{64,320},{96,352},{128,384},{160,416},{192,448},{... | collective-permute-start | bytes 49160 | tf_op jit(solution)/shard_map/ppermute | solution.py:45
  37.3 6.1 %collective-permute-start = (bf16[16,512]{1,0:T(8,128)(2,1)S(1)}, bf16[16,512]{1,0:T(8,128)(2,1)S(1)}, u32[]{:S(2)}, u32[]{:S(2)}) collective-permute-start(bf16[16,512]{1,0:T(8,128)(2,1)S(1)} %maximum_maximum_fusion), channel_id=1, source_target_pairs={{0,128},{32,160},{64,192},{96,224},{128,256},{160,288},{192,320},{... | collective-permute-start | bytes 49160 | tf_op jit(solution)/shard_map/ppermute | solution.py:45
  43.4 0.1 fusion.18
  43.5 0.9 collective-permute-done.1
  44.4 1.5 collective-permute-done
  46.0 0.8 copy-done.1
  46.9 5.7 %collective-permute-start.5 = (bf16[40,512]{1,0:T(8,128)(2,1)S(1)}, bf16[40,512]{1,0:T(8,128)(2,1)S(1)}, u32[]{:S(2)}, u32[]{:S(2)}) collective-permute-start(bf16[40,512]{1,0:T(8,128)(2,1)S(1)} %get-tuple-element.40), channel_id=1, source_target_pairs={{0,6},{1,7},{2,0},{3,1},{4,2},{5,3},{6,4},{7,5},{8,14},{9,15},{10,... | collective-permute-start | bytes 122888 | tf_op jit(solution)/shard_map/ppermute | solution.py:45
  52.6 1.9 collective-permute-start.4
  54.5 2.3 collective-permute-start.3
  56.8 1.9 collective-permute-done.4
  58.6 2.5 %collective-permute-done.3 = bf16[40,512]{1,0:T(8,128)(2,1)S(1)} collective-permute-done((bf16[40,512]{1,0:T(8,128)(2,1)S(1)}, bf16[40,512]{1,0:T(8,128)(2,1)S(1)}, u32[]{:S(2)}, u32[]{:S(2)}) %collective-permute-start.3) | collective-permute-done | bytes 40992 | tf_op jit(solution)/shard_map/ppermute | solution.py:45
  61.3 3.1 %collective-permute-start.6 = (bf16[160,512]{1,0:T(8,128)(2,1)S(1)}, bf16[160,512]{1,0:T(8,128)(2,1)S(1)}, u32[]{:S(2)}, u32[]{:S(2)}) collective-permute-start(bf16[160,512]{1,0:T(8,128)(2,1)S(1)} %pad_maximum_fusion.6), channel_id=1, source_target_pairs={{0,32},{32,64},{64,96},{96,0},{128,160},{160,192},{192,224},{224,1... | collective-permute-start | bytes 491528 | tf_op jit(solution)/shard_map/ppermute | solution.py:45
  64.4 4.4 %collective-permute-start.10 = (bf16[160,512]{1,0:T(8,128)(2,1)S(1)}, bf16[160,512]{1,0:T(8,128)(2,1)S(1)}, u32[]{:S(2)}, u32[]{:S(2)}) collective-permute-start(bf16[160,512]{1,0:T(8,128)(2,1)S(1)} %pad_maximum_fusion.6), channel_id=1, source_target_pairs={{0,64},{32,96},{64,0},{96,32},{128,192},{160,224},{192,128},{224,1... | collective-permute-start | bytes 491528 | tf_op jit(solution)/shard_map/ppermute | solution.py:45
  68.7 3.1 %collective-permute-start.11 = (bf16[160,512]{1,0:T(8,128)(2,1)S(1)}, bf16[160,512]{1,0:T(8,128)(2,1)S(1)}, u32[]{:S(2)}, u32[]{:S(2)}) collective-permute-start(bf16[160,512]{1,0:T(8,128)(2,1)S(1)} %pad_maximum_fusion.6), channel_id=1, source_target_pairs={{0,96},{32,0},{64,32},{96,64},{128,224},{160,128},{192,160},{224,1... | collective-permute-start | bytes 491528 | tf_op jit(solution)/shard_map/ppermute | solution.py:45
  71.8 0.7 constant_dynamic-update-slice_fusion.7
  72.5 0.6 constant_dynamic-update-slice_fusion.6
  73.1 0.6 constant_dynamic-update-slice_fusion.5
  73.7 3.2 %collective-permute-start.9 = (bf16[320,512]{1,0:T(8,128)(2,1)S(1)}, bf16[320,512]{1,0:T(8,128)(2,1)S(1)}, u32[]{:S(2)}, u32[]{:S(2)}) collective-permute-start(bf16[320,512]{1,0:T(8,128)(2,1)S(1)} %pad_maximum_fusion.4.refs_0_), channel_id=1, source_target_pairs={{0,8},{1,9},{2,10},{3,11},{4,12},{5,13},{6,14},{7,15},{8,16},{9,17... | collective-permute-start | bytes 983048 | tf_op jit(solution)/shard_map/ppermute | solution.py:45
  76.9 3.3 %collective-permute-start.8 = (bf16[256,1024]{1,0:T(8,128)(2,1)S(1)}, bf16[256,1024]{1,0:T(8,128)(2,1)S(1)}, u32[]{:S(2)}, u32[]{:S(2)}) collective-permute-start(bf16[256,1024]{1,0:T(8,128)(2,1)S(1)} %bitcast.45), channel_id=1, source_target_pairs={{0,384},{32,416},{64,448},{96,480},{128,0},{160,32},{192,64},{224,... | collective-permute-start | bytes 1572872 | tf_op jit(solution)/shard_map/ppermute | solution.py:45
  80.3 5.9 %collective-permute-start.7 = (bf16[256,1024]{1,0:T(8,128)(2,1)S(1)}, bf16[256,1024]{1,0:T(8,128)(2,1)S(1)}, u32[]{:S(2)}, u32[]{:S(2)}) collective-permute-start(bf16[256,1024]{1,0:T(8,128)(2,1)S(1)} %bitcast.46), channel_id=1, source_target_pairs={{0,128},{32,160},{64,192},{96,224},{128,256},{160,288},{192,320},{... | collective-permute-start | bytes 1572872 | tf_op jit(solution)/shard_map/ppermute | solution.py:45
  86.2 0.7 constant_dynamic-update-slice_fusion.4
  86.8 0.7 constant_dynamic-update-slice_fusion.3
  87.5 0.7 constant_dynamic-update-slice_fusion.2
  88.2 3.1 %collective-permute-start.12 = (bf16[320,512]{1,0:T(8,128)(2,1)S(1)}, bf16[320,512]{1,0:T(8,128)(2,1)S(1)}, u32[]{:S(2)}, u32[]{:S(2)}) collective-permute-start(bf16[320,512]{1,0:T(8,128)(2,1)S(1)} %get-tuple-element.32.refs_1_), channel_id=1, source_target_pairs={{0,8},{1,9},{2,10},{3,11},{4,12},{5,13},{6,14},{7,15},{8,16},{9,17... | collective-permute-start | bytes 983048 | tf_op jit(solution)/shard_map/ppermute | solution.py:45
  91.3 3.3 %collective-permute-start.13 = (bf16[320,512]{1,0:T(8,128)(2,1)S(1)}, bf16[320,512]{1,0:T(8,128)(2,1)S(1)}, u32[]{:S(2)}, u32[]{:S(2)}) collective-permute-start(bf16[320,512]{1,0:T(8,128)(2,1)S(1)} %pad_maximum_fusion.4.refs_0_), channel_id=1, source_target_pairs={{0,16},{1,17},{2,18},{3,19},{4,20},{5,21},{6,22},{7,23},{8,24},{9,... | collective-permute-start | bytes 983048 | tf_op jit(solution)/shard_map/ppermute | solution.py:45
  94.6 34.5 %collective-permute-done.8 = bf16[256,1024]{1,0:T(8,128)(2,1)S(1)} collective-permute-done((bf16[256,1024]{1,0:T(8,128)(2,1)S(1)}, bf16[256,1024]{1,0:T(8,128)(2,1)S(1)}, u32[]{:S(2)}, u32[]{:S(2)}) %collective-permute-start.8) | collective-permute-done | bytes 524320 | tf_op jit(solution)/shard_map/ppermute | solution.py:45
  129.1 0.1 pad_maximum_fusion.refs_1_
  129.3 2.2 collective-permute-start.14
  131.5 4.3 %collective-permute-start.15 = (bf16[512,1024]{1,0:T(8,128)(2,1)S(1)}, bf16[512,1024]{1,0:T(8,128)(2,1)}, u32[]{:S(2)}, u32[]{:S(2)}) collective-permute-start(bf16[512,1024]{1,0:T(8,128)(2,1)S(1)} %pad_maximum_fusion.refs_1_), channel_id=1, source_target_pairs={{0,96},{32,0},{64,32},{96,64},{128,224},{160,128},{192,160},{224,1... | collective-permute-start | bytes 3145736 | tf_op jit(solution)/shard_map/ppermute | solution.py:45
  135.8 3.5 %collective-permute-start.23 = (bf16[128,1024]{1,0:T(8,128)(2,1)S(1)}, bf16[128,1024]{1,0:T(8,128)(2,1)S(1)}, u32[]{:S(2)}, u32[]{:S(2)}) collective-permute-start(bf16[128,1024]{1,0:T(8,128)(2,1)S(1)} %slice.51), channel_id=1, source_target_pairs={{0,128},{32,160},{64,192},{96,224},{128,256},{160,288},{192,320},{... | collective-permute-start | bytes 786440 | tf_op jit(solution)/shard_map/ppermute | solution.py:45
  139.4 5.7 %collective-permute-start.24 = (bf16[128,1024]{1,0:T(8,128)(2,1)S(1)}, bf16[128,1024]{1,0:T(8,128)(2,1)S(1)}, u32[]{:S(2)}, u32[]{:S(2)}) collective-permute-start(bf16[128,1024]{1,0:T(8,128)(2,1)S(1)} %slice.52), channel_id=1, source_target_pairs={{0,384},{32,416},{64,448},{96,480},{128,0},{160,32},{192,64},{224,... | collective-permute-start | bytes 786440 | tf_op jit(solution)/shard_map/ppermute | solution.py:45
  145.0 15.4 %collective-permute-done.23 = bf16[128,1024]{1,0:T(8,128)(2,1)S(1)} collective-permute-done((bf16[128,1024]{1,0:T(8,128)(2,1)S(1)}, bf16[128,1024]{1,0:T(8,128)(2,1)S(1)}, u32[]{:S(2)}, u32[]{:S(2)}) %collective-permute-start.23) | collective-permute-done | bytes 262176 | tf_op jit(solution)/shard_map/ppermute | solution.py:45
  160.6 0.8 copy-done.3
  161.4 4.3 %collective-permute-start.16 = (bf16[320,512]{1,0:T(8,128)(2,1)}, bf16[320,512]{1,0:T(8,128)(2,1)S(1)}, u32[]{:S(2)}, u32[]{:S(2)}) collective-permute-start(bf16[320,512]{1,0:T(8,128)(2,1)} %copy-done.12), channel_id=1, source_target_pairs={{0,16},{1,17},{2,18},{3,19},{4,20},{5,21},{6,22},{7,23},{8,24},{9,... | collective-permute-start | bytes 983048 | tf_op jit(solution)/shard_map/ppermute | solution.py:45
  165.7 8.4 %collective-permute-start.17 = (bf16[320,512]{1,0:T(8,128)(2,1)S(1)}, bf16[320,512]{1,0:T(8,128)(2,1)S(1)}, u32[]{:S(2)}, u32[]{:S(2)}) collective-permute-start(bf16[320,512]{1,0:T(8,128)(2,1)S(1)} %pad_maximum_fusion.4.refs_0_), channel_id=1, source_target_pairs={{0,24},{1,25},{2,26},{3,27},{4,28},{5,29},{6,30},{7,31},{8,0},{9,1... | collective-permute-start | bytes 983048 | tf_op jit(solution)/shard_map/ppermute | solution.py:45
  174.2 1.9 collective-permute-start.18
  176.1 2.7 %collective-permute-start.19 = (bf16[640,512]{1,0:T(8,128)(2,1)}, bf16[640,512]{1,0:T(8,128)(2,1)}, u32[]{:S(2)}, u32[]{:S(2)}) collective-permute-start(bf16[640,512]{1,0:T(8,128)(2,1)} %get-tuple-element.31), channel_id=1, source_target_pairs={{0,1},{1,0},{2,3},{3,2},{4,5},{5,4},{6,7},{7,6},{8,9},{9,8},{10,11... | collective-permute-start | bytes 1966088 | tf_op jit(solution)/shard_map/ppermute | solution.py:45
  178.9 2.1 collective-permute-start.20
  181.1 2.4 collective-permute-start.21
  183.5 4.0 %collective-permute-done.17.refs_6_ = bf16[320,512]{1,0:T(8,128)(2,1)S(1)} collective-permute-done((bf16[320,512]{1,0:T(8,128)(2,1)S(1)}, bf16[320,512]{1,0:T(8,128)(2,1)S(1)}, u32[]{:S(2)}, u32[]{:S(2)}) %collective-permute-start.17) | collective-permute-done | bytes 327712 | tf_op jit(solution)/shard_map/ppermute | solution.py:45
  187.5 7.0 %collective-permute-done.18.refs_7_ = bf16[320,512]{1,0:T(8,128)(2,1)S(1)} collective-permute-done((bf16[320,512]{1,0:T(8,128)(2,1)}, bf16[320,512]{1,0:T(8,128)(2,1)S(1)}, u32[]{:S(2)}, u32[]{:S(2)}) %collective-permute-start.18) | collective-permute-done | bytes 327712 | tf_op jit(solution)/shard_map/ppermute | solution.py:45
  194.6 3.1 %collective-permute-start.22 = (bf16[640,512]{1,0:T(8,128)(2,1)S(1)}, bf16[640,512]{1,0:T(8,128)(2,1)}, u32[]{:S(2)}, u32[]{:S(2)}) collective-permute-start(bf16[640,512]{1,0:T(8,128)(2,1)S(1)} %pad_maximum_fusion.3), channel_id=1, source_target_pairs={{0,1},{1,0},{2,3},{3,2},{4,5},{5,4},{6,7},{7,6},{8,9},{9,8},{10,11... | collective-permute-start | bytes 1966088 | tf_op jit(solution)/shard_map/ppermute | solution.py:45
  197.8 0.1 copy.21
  197.9 0.1 iota_add_fusion
  198.0 1.0 add.76.refs_12_
  198.9 0.7 pad_convert_fusion.refs_14_
  199.6 1.1 slice.50
  200.7 1.9 collective-permute-start.25
  202.7 1.1 slice.53
  203.7 4.8 %collective-permute-start.26 = (bf16[256,1024]{1,0:T(8,128)(2,1)S(1)}, bf16[256,1024]{1,0:T(8,128)(2,1)S(1)}, u32[]{:S(2)}, u32[]{:S(2)}) collective-permute-start(bf16[256,1024]{1,0:T(8,128)(2,1)S(1)} %slice.53), channel_id=1, source_target_pairs={{0,96},{32,0},{64,32},{96,64},{128,224},{160,128},{192,160},{224,1... | collective-permute-start | bytes 1572872 | tf_op jit(solution)/shard_map/ppermute | solution.py:45
  208.5 14.1 %shard_map.139 = (f32[8,512]{1,0:T(8,128)}, bf16[512,1024]{1,0:T(8,128)(2,1)}, bf16[512,256]{1,0:T(8,128)(2,1)}, bf16[512,256]{1,0:T(8,128)(2,1)}, bf16[512,128]{1,0:T(8,128)(2,1)}) custom-call(bf16[320,512]{1,0:T(8,128)(2,1)} %copy-done.11, bf16[320,512]{1,0:T(8,128)(2,1)} %copy-done.12, bf16[320,512]{1,0:T(8,128)(2,1)} %copy-done.5, ...), custom_call_target="tpu_custom_call" | custom-call | flops 10000000000 | bytes 9000000 | tf_op jit(solution)/shard_map/pallas_call | solution.py:152
  222.7 0.7 copy-done.18
  223.4 0.2 copy-done.19
  223.6 16.0 %shard_map.140 = (f32[1024,256]{1,0:T(8,128)}, f32[256,1024]{1,0:T(8,128)}) custom-call(bf16[1024,1024]{1,0:T(8,128)(2,1)} %all-gather.3.cloned.1.call-done.refs_0_, bf16[512,1024]{1,0:T(8,128)(2,1)} %copy-done.4, bf16[512,1024]{1,0:T(8,128)(2,1)} %collective-permute-done.14.refs_2_, bf16[512,1024]{1,0:T(8,128)(2,1)} %collective-permute-done.15.refs_3_, ...), custom_call_target="tpu_custom_call" | custom-call | flops 5000000000 | bytes 13000000 | tf_op jit(solution)/shard_map/pallas_call | solution.py:237
  (92 shorter events, 0.7 us)
Async XLA Ops:
  7.2 1.6 copy-start
  7.2 13.3 %copy-start.20 = (s32[8]{0:T(128)S(1)}, s32[8]{0:T(128)}, u32[]{:S(2)}) copy-start(s32[8]{0:T(128)} %param.20) | copy-start | bytes 100
  7.2 13.4 %copy-start.21 = (bf16[128]{0:T(256)(128)(2,1)S(1)}, bf16[128]{0:T(256)(128)(2,1)}, u32[]{:S(2)}) copy-start(bf16[128]{0:T(256)(128)(2,1)} %param.14) | copy-start | bytes 772
  7.2 14.4 %copy-start.13 = (bf16[8,512]{1,0:T(8,128)(2,1)S(1)}, bf16[8,512]{1,0:T(8,128)(2,1)}, u32[]{:S(2)}) copy-start(bf16[8,512]{1,0:T(8,128)(2,1)} %param.19) | copy-start | bytes 24580
  10.0 36.0 %all-to-all-start = ((bf16[32,8,1024]{2,1,0:T(8,128)(2,1)}), bf16[32,8,1024]{2,1,0:T(8,128)(2,1)S(1)}, u32[]{:S(2)}, u32[]{:S(2)}) async-start(bf16[32,8,1024]{2,1,0:T(8,128)(2,1)} %fusion), calls=%async_computation | async-start | bytes 1048576 | tf_op jit(solution)/shard_map/all_to_all | solution.py:285
  20.4 202.2 %all-gather.3.cloned.1.call-start = ((), (), s32[]{:S(2)}) async-start(), calls=%async_computation.1 | async-start | bytes 2621440 | tf_op jit(solution)/shard_map/all_gather | solution.py:55
  21.7 21.8 %collective-permute-start.2 = (bf16[16,512]{1,0:T(8,128)(2,1)S(1)}, bf16[16,512]{1,0:T(8,128)(2,1)S(1)}, u32[]{:S(2)}, u32[]{:S(2)}) collective-permute-start(bf16[16,512]{1,0:T(8,128)(2,1)S(1)} %maximum_maximum_fusion), channel_id=1, source_target_pairs={{0,384},{32,416},{64,448},{96,480},{128,0},{160,32},{192,64},{224,... | collective-permute-start | bytes 49160 | tf_op jit(solution)/shard_map/ppermute | solution.py:45
  31.2 13.2 %collective-permute-start.1 = (bf16[16,512]{1,0:T(8,128)(2,1)S(1)}, bf16[16,512]{1,0:T(8,128)(2,1)S(1)}, u32[]{:S(2)}, u32[]{:S(2)}) collective-permute-start(bf16[16,512]{1,0:T(8,128)(2,1)S(1)} %maximum_maximum_fusion), channel_id=1, source_target_pairs={{0,256},{32,288},{64,320},{96,352},{128,384},{160,416},{192,448},{... | collective-permute-start | bytes 49160 | tf_op jit(solution)/shard_map/ppermute | solution.py:45
  37.3 8.6 %collective-permute-start = (bf16[16,512]{1,0:T(8,128)(2,1)S(1)}, bf16[16,512]{1,0:T(8,128)(2,1)S(1)}, u32[]{:S(2)}, u32[]{:S(2)}) collective-permute-start(bf16[16,512]{1,0:T(8,128)(2,1)S(1)} %maximum_maximum_fusion), channel_id=1, source_target_pairs={{0,128},{32,160},{64,192},{96,224},{128,256},{160,288},{192,320},{... | collective-permute-start | bytes 49160 | tf_op jit(solution)/shard_map/ppermute | solution.py:45
  46.0 0.8 copy-start.1
  46.8 30.1 %copy-start.2 = (bf16[32,8,1024]{2,1,0:T(8,128)(2,1)S(1)}, bf16[32,8,1024]{2,1,0:T(8,128)(2,1)}, u32[]{:S(2)}) copy-start(bf16[32,8,1024]{2,1,0:T(8,128)(2,1)} %copy-done.1) | copy-start | bytes 1572868
  46.8 175.8 %all-gather.5.cloned.1.call-start = ((), (), s32[]{:S(2)}) async-start(), calls=%async_computation.2 | async-start | bytes 2621440 | tf_op jit(solution)/shard_map/all_gather | solution.py:55
  46.9 9.9 %collective-permute-start.5 = (bf16[40,512]{1,0:T(8,128)(2,1)S(1)}, bf16[40,512]{1,0:T(8,128)(2,1)S(1)}, u32[]{:S(2)}, u32[]{:S(2)}) collective-permute-start(bf16[40,512]{1,0:T(8,128)(2,1)S(1)} %get-tuple-element.40), channel_id=1, source_target_pairs={{0,6},{1,7},{2,0},{3,1},{4,2},{5,3},{6,4},{7,5},{8,14},{9,15},{10,... | collective-permute-start | bytes 122888 | tf_op jit(solution)/shard_map/ppermute | solution.py:45
  52.6 6.1 %collective-permute-start.4 = (bf16[40,512]{1,0:T(8,128)(2,1)S(1)}, bf16[40,512]{1,0:T(8,128)(2,1)S(1)}, u32[]{:S(2)}, u32[]{:S(2)}) collective-permute-start(bf16[40,512]{1,0:T(8,128)(2,1)S(1)} %get-tuple-element.40), channel_id=1, source_target_pairs={{0,4},{1,5},{2,6},{3,7},{4,0},{5,1},{6,2},{7,3},{8,12},{9,13},{10,... | collective-permute-start | bytes 122888 | tf_op jit(solution)/shard_map/ppermute | solution.py:45
  54.5 6.6 %collective-permute-start.3 = (bf16[40,512]{1,0:T(8,128)(2,1)S(1)}, bf16[40,512]{1,0:T(8,128)(2,1)S(1)}, u32[]{:S(2)}, u32[]{:S(2)}) collective-permute-start(bf16[40,512]{1,0:T(8,128)(2,1)S(1)} %get-tuple-element.40), channel_id=1, source_target_pairs={{0,2},{1,3},{2,4},{3,5},{4,6},{5,7},{6,0},{7,1},{8,10},{9,11},{10,... | collective-permute-start | bytes 122888 | tf_op jit(solution)/shard_map/ppermute | solution.py:45
  61.3 12.4 %collective-permute-start.6 = (bf16[160,512]{1,0:T(8,128)(2,1)S(1)}, bf16[160,512]{1,0:T(8,128)(2,1)S(1)}, u32[]{:S(2)}, u32[]{:S(2)}) collective-permute-start(bf16[160,512]{1,0:T(8,128)(2,1)S(1)} %pad_maximum_fusion.6), channel_id=1, source_target_pairs={{0,32},{32,64},{64,96},{96,0},{128,160},{160,192},{192,224},{224,1... | collective-permute-start | bytes 491528 | tf_op jit(solution)/shard_map/ppermute | solution.py:45
  64.4 22.5 %collective-permute-start.10 = (bf16[160,512]{1,0:T(8,128)(2,1)S(1)}, bf16[160,512]{1,0:T(8,128)(2,1)S(1)}, u32[]{:S(2)}, u32[]{:S(2)}) collective-permute-start(bf16[160,512]{1,0:T(8,128)(2,1)S(1)} %pad_maximum_fusion.6), channel_id=1, source_target_pairs={{0,64},{32,96},{64,0},{96,32},{128,192},{160,224},{192,128},{224,1... | collective-permute-start | bytes 491528 | tf_op jit(solution)/shard_map/ppermute | solution.py:45
  68.7 18.8 %collective-permute-start.11 = (bf16[160,512]{1,0:T(8,128)(2,1)S(1)}, bf16[160,512]{1,0:T(8,128)(2,1)S(1)}, u32[]{:S(2)}, u32[]{:S(2)}) collective-permute-start(bf16[160,512]{1,0:T(8,128)(2,1)S(1)} %pad_maximum_fusion.6), channel_id=1, source_target_pairs={{0,96},{32,0},{64,32},{96,64},{128,224},{160,128},{192,160},{224,1... | collective-permute-start | bytes 491528 | tf_op jit(solution)/shard_map/ppermute | solution.py:45
  73.7 92.0 %copy-start.11 = (bf16[320,512]{1,0:T(8,128)(2,1)}, bf16[320,512]{1,0:T(8,128)(2,1)S(1)}, u32[]{:S(2)}) copy-start(bf16[320,512]{1,0:T(8,128)(2,1)S(1)} %pad_maximum_fusion.4.refs_0_) | copy-start | bytes 983044
  73.7 55.5 %collective-permute-start.9 = (bf16[320,512]{1,0:T(8,128)(2,1)S(1)}, bf16[320,512]{1,0:T(8,128)(2,1)S(1)}, u32[]{:S(2)}, u32[]{:S(2)}) collective-permute-start(bf16[320,512]{1,0:T(8,128)(2,1)S(1)} %pad_maximum_fusion.4.refs_0_), channel_id=1, source_target_pairs={{0,8},{1,9},{2,10},{3,11},{4,12},{5,13},{6,14},{7,15},{8,16},{9,17... | collective-permute-start | bytes 983048 | tf_op jit(solution)/shard_map/ppermute | solution.py:45
  76.9 52.2 %collective-permute-start.8 = (bf16[256,1024]{1,0:T(8,128)(2,1)S(1)}, bf16[256,1024]{1,0:T(8,128)(2,1)S(1)}, u32[]{:S(2)}, u32[]{:S(2)}) collective-permute-start(bf16[256,1024]{1,0:T(8,128)(2,1)S(1)} %bitcast.45), channel_id=1, source_target_pairs={{0,384},{32,416},{64,448},{96,480},{128,0},{160,32},{192,64},{224,... | collective-permute-start | bytes 1572872 | tf_op jit(solution)/shard_map/ppermute | solution.py:45
  80.3 48.8 %collective-permute-start.7 = (bf16[256,1024]{1,0:T(8,128)(2,1)S(1)}, bf16[256,1024]{1,0:T(8,128)(2,1)S(1)}, u32[]{:S(2)}, u32[]{:S(2)}) collective-permute-start(bf16[256,1024]{1,0:T(8,128)(2,1)S(1)} %bitcast.46), channel_id=1, source_target_pairs={{0,128},{32,160},{64,192},{96,224},{128,256},{160,288},{192,320},{... | collective-permute-start | bytes 1572872 | tf_op jit(solution)/shard_map/ppermute | solution.py:45
  88.2 72.3 %copy-start.12 = (bf16[320,512]{1,0:T(8,128)(2,1)}, bf16[320,512]{1,0:T(8,128)(2,1)S(1)}, u32[]{:S(2)}) copy-start(bf16[320,512]{1,0:T(8,128)(2,1)S(1)} %get-tuple-element.32.refs_1_) | copy-start | bytes 983044
  88.2 41.0 %collective-permute-start.12 = (bf16[320,512]{1,0:T(8,128)(2,1)S(1)}, bf16[320,512]{1,0:T(8,128)(2,1)S(1)}, u32[]{:S(2)}, u32[]{:S(2)}) collective-permute-start(bf16[320,512]{1,0:T(8,128)(2,1)S(1)} %get-tuple-element.32.refs_1_), channel_id=1, source_target_pairs={{0,8},{1,9},{2,10},{3,11},{4,12},{5,13},{6,14},{7,15},{8,16},{9,17... | collective-permute-start | bytes 983048 | tf_op jit(solution)/shard_map/ppermute | solution.py:45
  91.3 37.9 %collective-permute-start.13 = (bf16[320,512]{1,0:T(8,128)(2,1)S(1)}, bf16[320,512]{1,0:T(8,128)(2,1)S(1)}, u32[]{:S(2)}, u32[]{:S(2)}) collective-permute-start(bf16[320,512]{1,0:T(8,128)(2,1)S(1)} %pad_maximum_fusion.4.refs_0_), channel_id=1, source_target_pairs={{0,16},{1,17},{2,18},{3,19},{4,20},{5,21},{6,22},{7,23},{8,24},{9,... | collective-permute-start | bytes 983048 | tf_op jit(solution)/shard_map/ppermute | solution.py:45
  129.2 32.2 %copy-start.4 = (bf16[512,1024]{1,0:T(8,128)(2,1)}, bf16[512,1024]{1,0:T(8,128)(2,1)S(1)}, u32[]{:S(2)}) copy-start(bf16[512,1024]{1,0:T(8,128)(2,1)S(1)} %pad_maximum_fusion.refs_1_) | copy-start | bytes 3145732
  129.2 49.6 %copy-start.5 = (bf16[320,512]{1,0:T(8,128)(2,1)}, bf16[320,512]{1,0:T(8,128)(2,1)S(1)}, u32[]{:S(2)}) copy-start(bf16[320,512]{1,0:T(8,128)(2,1)S(1)} %collective-permute-done.9.refs_2_) | copy-start | bytes 983044
  129.2 49.6 %copy-start.6 = (bf16[320,512]{1,0:T(8,128)(2,1)}, bf16[320,512]{1,0:T(8,128)(2,1)S(1)}, u32[]{:S(2)}) copy-start(bf16[320,512]{1,0:T(8,128)(2,1)S(1)} %collective-permute-done.12.refs_3_) | copy-start | bytes 983044
  129.3 51.7 %copy-start.7 = (bf16[320,512]{1,0:T(8,128)(2,1)}, bf16[320,512]{1,0:T(8,128)(2,1)S(1)}, u32[]{:S(2)}) copy-start(bf16[320,512]{1,0:T(8,128)(2,1)S(1)} %collective-permute-done.13.refs_4_) | copy-start | bytes 983044
  129.3 31.3 %collective-permute-start.14 = (bf16[512,1024]{1,0:T(8,128)(2,1)S(1)}, bf16[512,1024]{1,0:T(8,128)(2,1)}, u32[]{:S(2)}, u32[]{:S(2)}) collective-permute-start(bf16[512,1024]{1,0:T(8,128)(2,1)S(1)} %pad_maximum_fusion.refs_1_), channel_id=1, source_target_pairs={{0,32},{32,64},{64,96},{96,0},{128,160},{160,192},{192,224},{224,1... | collective-permute-start | bytes 3145736 | tf_op jit(solution)/shard_map/ppermute | solution.py:45
  131.5 29.1 %collective-permute-start.15 = (bf16[512,1024]{1,0:T(8,128)(2,1)S(1)}, bf16[512,1024]{1,0:T(8,128)(2,1)}, u32[]{:S(2)}, u32[]{:S(2)}) collective-permute-start(bf16[512,1024]{1,0:T(8,128)(2,1)S(1)} %pad_maximum_fusion.refs_1_), channel_id=1, source_target_pairs={{0,96},{32,0},{64,32},{96,64},{128,224},{160,128},{192,160},{224,1... | collective-permute-start | bytes 3145736 | tf_op jit(solution)/shard_map/ppermute | solution.py:45
  135.8 24.7 %collective-permute-start.23 = (bf16[128,1024]{1,0:T(8,128)(2,1)S(1)}, bf16[128,1024]{1,0:T(8,128)(2,1)S(1)}, u32[]{:S(2)}, u32[]{:S(2)}) collective-permute-start(bf16[128,1024]{1,0:T(8,128)(2,1)S(1)} %slice.51), channel_id=1, source_target_pairs={{0,128},{32,160},{64,192},{96,224},{128,256},{160,288},{192,320},{... | collective-permute-start | bytes 786440 | tf_op jit(solution)/shard_map/ppermute | solution.py:45
  139.4 21.2 %collective-permute-start.24 = (bf16[128,1024]{1,0:T(8,128)(2,1)S(1)}, bf16[128,1024]{1,0:T(8,128)(2,1)S(1)}, u32[]{:S(2)}, u32[]{:S(2)}) collective-permute-start(bf16[128,1024]{1,0:T(8,128)(2,1)S(1)} %slice.52), channel_id=1, source_target_pairs={{0,384},{32,416},{64,448},{96,480},{128,0},{160,32},{192,64},{224,... | collective-permute-start | bytes 786440 | tf_op jit(solution)/shard_map/ppermute | solution.py:45
  160.5 0.8 copy-start.3
  161.4 19.6 %collective-permute-start.16 = (bf16[320,512]{1,0:T(8,128)(2,1)}, bf16[320,512]{1,0:T(8,128)(2,1)S(1)}, u32[]{:S(2)}, u32[]{:S(2)}) collective-permute-start(bf16[320,512]{1,0:T(8,128)(2,1)} %copy-done.12), channel_id=1, source_target_pairs={{0,16},{1,17},{2,18},{3,19},{4,20},{5,21},{6,22},{7,23},{8,24},{9,... | collective-permute-start | bytes 983048 | tf_op jit(solution)/shard_map/ppermute | solution.py:45
  165.7 21.8 %collective-permute-start.17 = (bf16[320,512]{1,0:T(8,128)(2,1)S(1)}, bf16[320,512]{1,0:T(8,128)(2,1)S(1)}, u32[]{:S(2)}, u32[]{:S(2)}) collective-permute-start(bf16[320,512]{1,0:T(8,128)(2,1)S(1)} %pad_maximum_fusion.4.refs_0_), channel_id=1, source_target_pairs={{0,24},{1,25},{2,26},{3,27},{4,28},{5,29},{6,30},{7,31},{8,0},{9,1... | collective-permute-start | bytes 983048 | tf_op jit(solution)/shard_map/ppermute | solution.py:45
  174.2 20.3 %collective-permute-start.18 = (bf16[320,512]{1,0:T(8,128)(2,1)}, bf16[320,512]{1,0:T(8,128)(2,1)S(1)}, u32[]{:S(2)}, u32[]{:S(2)}) collective-permute-start(bf16[320,512]{1,0:T(8,128)(2,1)} %copy-done.12), channel_id=1, source_target_pairs={{0,24},{1,25},{2,26},{3,27},{4,28},{5,29},{6,30},{7,31},{8,0},{9,1... | collective-permute-start | bytes 983048 | tf_op jit(solution)/shard_map/ppermute | solution.py:45
  176.1 24.6 %collective-permute-start.19 = (bf16[640,512]{1,0:T(8,128)(2,1)}, bf16[640,512]{1,0:T(8,128)(2,1)}, u32[]{:S(2)}, u32[]{:S(2)}) collective-permute-start(bf16[640,512]{1,0:T(8,128)(2,1)} %get-tuple-element.31), channel_id=1, source_target_pairs={{0,1},{1,0},{2,3},{3,2},{4,5},{5,4},{6,7},{7,6},{8,9},{9,8},{10,11... | collective-permute-start | bytes 1966088 | tf_op jit(solution)/shard_map/ppermute | solution.py:45
  178.9 19.0 %copy-start.14 = (s32[16]{0:T(128)S(1)}, s32[16]{0:T(128)}, u32[]{:S(2)}) copy-start(s32[16]{0:T(128)} %constant.89.clone) | copy-start | bytes 196
  178.9 19.0 %copy-start.15 = (s32[16]{0:T(128)S(1)}, s32[16]{0:T(128)}, u32[]{:S(2)}) copy-start(s32[16]{0:T(128)} %constant.90.clone) | copy-start | bytes 196
  178.9 19.0 %copy-start.16 = (s32[16]{0:T(128)S(1)}, s32[16]{0:T(128)}, u32[]{:S(2)}) copy-start(s32[16]{0:T(128)} %constant.91.clone) | copy-start | bytes 196
  178.9 21.8 %collective-permute-start.20 = (bf16[640,512]{1,0:T(8,128)(2,1)S(1)}, bf16[640,512]{1,0:T(8,128)(2,1)}, u32[]{:S(2)}, u32[]{:S(2)}) collective-permute-start(bf16[640,512]{1,0:T(8,128)(2,1)S(1)} %pad_maximum_fusion.1), channel_id=1, source_target_pairs={{0,1},{1,0},{2,3},{3,2},{4,5},{5,4},{6,7},{7,6},{8,9},{9,8},{10,11... | collective-permute-start | bytes 1966088 | tf_op jit(solution)/shard_map/ppermute | solution.py:45
  181.0 13.6 %copy-start.8 = (bf16[320,512]{1,0:T(8,128)(2,1)}, bf16[320,512]{1,0:T(8,128)(2,1)S(1)}, u32[]{:S(2)}) copy-start(bf16[320,512]{1,0:T(8,128)(2,1)S(1)} %collective-permute-done.16.refs_5_) | copy-start | bytes 983044
  181.1 19.6 %collective-permute-start.21 = (bf16[640,512]{1,0:T(8,128)(2,1)S(1)}, bf16[640,512]{1,0:T(8,128)(2,1)S(1)}, u32[]{:S(2)}, u32[]{:S(2)}) collective-permute-start(bf16[640,512]{1,0:T(8,128)(2,1)S(1)} %pad_maximum_fusion.2), channel_id=1, source_target_pairs={{0,1},{1,0},{2,3},{3,2},{4,5},{5,4},{6,7},{7,6},{8,9},{9,8},{10,11... | collective-permute-start | bytes 1966088 | tf_op jit(solution)/shard_map/ppermute | solution.py:45
  187.5 10.2 %copy-start.9 = (bf16[320,512]{1,0:T(8,128)(2,1)}, bf16[320,512]{1,0:T(8,128)(2,1)S(1)}, u32[]{:S(2)}) copy-start(bf16[320,512]{1,0:T(8,128)(2,1)S(1)} %collective-permute-done.17.refs_6_) | copy-start | bytes 983044
  194.5 3.2 %copy-start.10 = (bf16[320,512]{1,0:T(8,128)(2,1)}, bf16[320,512]{1,0:T(8,128)(2,1)S(1)}, u32[]{:S(2)}) copy-start(bf16[320,512]{1,0:T(8,128)(2,1)S(1)} %collective-permute-done.18.refs_7_) | copy-start | bytes 983044
  194.6 6.1 %collective-permute-start.22 = (bf16[640,512]{1,0:T(8,128)(2,1)S(1)}, bf16[640,512]{1,0:T(8,128)(2,1)}, u32[]{:S(2)}, u32[]{:S(2)}) collective-permute-start(bf16[640,512]{1,0:T(8,128)(2,1)S(1)} %pad_maximum_fusion.3), channel_id=1, source_target_pairs={{0,1},{1,0},{2,3},{3,2},{4,5},{5,4},{6,7},{7,6},{8,9},{9,8},{10,11... | collective-permute-start | bytes 1966088 | tf_op jit(solution)/shard_map/ppermute | solution.py:45
  200.7 7.8 %copy-start.17 = (bf16[640,512]{1,0:T(8,128)(2,1)}, bf16[640,512]{1,0:T(8,128)(2,1)S(1)}, u32[]{:S(2)}) copy-start(bf16[640,512]{1,0:T(8,128)(2,1)S(1)} %collective-permute-done.21.refs_10_) | copy-start | bytes 1966084
  200.7 21.9 %collective-permute-start.25 = (bf16[256,1024]{1,0:T(8,128)(2,1)S(1)}, bf16[256,1024]{1,0:T(8,128)(2,1)S(1)}, u32[]{:S(2)}, u32[]{:S(2)}) collective-permute-start(bf16[256,1024]{1,0:T(8,128)(2,1)S(1)} %slice.50), channel_id=1, source_target_pairs={{0,32},{32,64},{64,96},{96,0},{128,160},{160,192},{192,224},{224,1... | collective-permute-start | bytes 1572872 | tf_op jit(solution)/shard_map/ppermute | solution.py:45
  203.7 18.9 %collective-permute-start.26 = (bf16[256,1024]{1,0:T(8,128)(2,1)S(1)}, bf16[256,1024]{1,0:T(8,128)(2,1)S(1)}, u32[]{:S(2)}, u32[]{:S(2)}) collective-permute-start(bf16[256,1024]{1,0:T(8,128)(2,1)S(1)} %slice.53), channel_id=1, source_target_pairs={{0,96},{32,0},{64,32},{96,64},{128,224},{160,128},{192,160},{224,1... | collective-permute-start | bytes 1572872 | tf_op jit(solution)/shard_map/ppermute | solution.py:45
  222.6 0.8 copy-start.18
  222.6 1.0 copy-start.19
Sparse Core Ops, SparseCore 0:
  46.9 44.2 all-gather.2
  161.5 36.1 all-gather.4
